TPU v7x, 32 devices: a whole 2x2x4 slice. The times are simulated.
32 devices in a mesh: node: 8 (over z, core), local: 4 (over y, x), tp: 1.
Axes of the slice: x: 2, y: 2, z: 4, core: 2. Of those that a mesh axis runs over, the one named last changes fastest.
Arguments:
- tokens: bfloat16 [1024, 2048], P(('node', 'local'), 'tp'), may hold values from -6 to 6
- grad_out: bfloat16 [1024, 2048], P(('node', 'local'), 'tp'), may hold values from -6 to 6
- routes: int32 [1024, 8], P(('node', 'local')), may hold values from 0 to 15, all different within a row; in each aligned block of 32 rows (0 to 31, 32 to 63, ...) at most 24 rows name the same one
- route_weight: float32 [1024, 8], P(('node', 'local')), may hold values from 0.05 to 0.5
- w_gate: bfloat16 [32, 2048, 384], P(('node', 'local'), 'tp'), may hold values from -0.125 to 0.125
- w_up: bfloat16 [32, 2048, 384], P(('node', 'local'), 'tp'), may hold values from -0.125 to 0.125
- w_down: bfloat16 [32, 384, 2048], P(('node', 'local'), None, 'tp'), may hold values from -0.21875 to 0.21875
Outputs:
- mixed: bfloat16 [1024, 2048], P(('node', 'local'), 'tp')
- grad_tokens: bfloat16 [1024, 2048], P(('node', 'local'), 'tp')
- grad_gate: bfloat16 [32, 2048, 384], P(('node', 'local'), 'tp')
- grad_up: bfloat16 [32, 2048, 384], P(('node', 'local'), 'tp')
- grad_down: bfloat16 [32, 384, 2048], P(('node', 'local'), None, 'tp')
Inputs may be any that keep to these rules, and one draw needn't show every extreme that they name: `routes`: each row names 8 different experts; within each aligned block of 32 rows (the tokens of one index of node and local) no expert is named more than 24 times, a bound that some block reaches.
All inputs are finite; a program needn't handle non-finite values.
Results may differ from a plain program's by a relative error of at most 0.02.
Values may be sent and summed in bfloat16 or wider, within the bound.
No kernel may reach another device: no remote copies, remote signals or barrier semaphores. Data moves between devices by JAX's collectives and lax.ppermute only.
A program may use at most 64 MiB of HBM per device.

v0:
```python
import jax
import jax.numpy as jnp
from jax import lax
from jax.sharding import PartitionSpec as P


def slot_table(route_rows, experts, capacity):
    flat = route_rows.reshape(-1)
    count = flat.shape[0]
    onehot = (flat[:, None] == jnp.arange(experts, dtype=jnp.int32)[None, :]).astype(jnp.float32)
    lower = (jnp.arange(count)[:, None] > jnp.arange(count)[None, :]).astype(jnp.float32)
    before = jnp.dot(lower, onehot, precision=lax.Precision.HIGHEST)
    ranking = jnp.sum(before * onehot, axis=1).astype(jnp.int32)
    position = flat * capacity + ranking
    return (position[None, :] == jnp.arange(experts * capacity, dtype=jnp.int32)[:, None]).astype(
        jnp.float32
    )


def activate(gate, up_val, d_hidden):
    sig_gate = jax.nn.sigmoid(gate)
    activated = gate * sig_gate
    hidden = (activated * up_val).astype(jnp.bfloat16)
    d_gate = (d_hidden * up_val * sig_gate * (1.0 + gate * (1.0 - sig_gate))).astype(jnp.bfloat16)
    d_up = (d_hidden * activated).astype(jnp.bfloat16)
    return (hidden, d_gate, d_up)


def shards(tokens, grad_out, routes, route_weight, w_gate, w_up, w_down):
    n_node = lax.axis_size("node")
    n_local = lax.axis_size("local")
    experts = n_node * n_local // 2
    exp_node = n_local // 2
    tok_rows, features = tokens.shape
    topk = routes.shape[1]
    capacity = min(tok_rows, max(2, 3 * tok_rows * topk // (2 * experts)))
    table = slot_table(routes, experts, capacity)
    token_map = table.reshape(experts * capacity, tok_rows, topk).sum(-1).astype(jnp.bfloat16)
    table_low = table.astype(jnp.bfloat16)
    send_rows = jnp.dot(token_map, tokens, preferred_element_type=jnp.float32).astype(jnp.bfloat16)
    weights_flat = route_weight.reshape(-1)
    scaled = (
        weights_flat[:, None] * jnp.repeat(grad_out, topk, axis=0).astype(jnp.float32)
    ).astype(jnp.bfloat16)
    send_grads = jnp.dot(table_low, scaled, preferred_element_type=jnp.float32).astype(jnp.bfloat16)
    send_rows = send_rows.reshape(n_node, exp_node, capacity, features)
    send_grads = send_grads.reshape(n_node, exp_node, capacity, features)
    twice_rows = jnp.repeat(send_rows, 2, axis=1)
    twice_grads = jnp.repeat(send_grads, 2, axis=1)
    got_rows, got_grads = (
        lax.all_to_all(
            lax.all_to_all(twice_rows, "node", split_axis=0, concat_axis=2, tiled=True),
            "local",
            split_axis=1,
            concat_axis=2,
            tiled=True,
        ),
        lax.all_to_all(
            lax.all_to_all(twice_grads, "node", split_axis=0, concat_axis=2, tiled=True),
            "local",
            split_axis=1,
            concat_axis=2,
            tiled=True,
        ),
    )
    rows_all = got_rows.shape[2]
    got_rows = got_rows.reshape(rows_all, features)
    got_grads = got_grads.reshape(rows_all, features)
    weight_g = w_gate[0]
    weight_u = w_up[0]
    weight_d = w_down[0]
    contract_last = (((1,), (1,)), ((), ()))
    contract_first = (((0,), (0,)), ((), ()))
    gate_part = jnp.dot(got_rows, weight_g, preferred_element_type=jnp.float32)
    up_part = jnp.dot(got_rows, weight_u, preferred_element_type=jnp.float32)
    hidden_part = lax.dot_general(
        got_grads, weight_d, contract_last, preferred_element_type=jnp.float32
    )
    gate, up_val, d_hidden = (
        lax.psum(gate_part.astype(jnp.bfloat16), "tp").astype(jnp.float32),
        lax.psum(up_part.astype(jnp.bfloat16), "tp").astype(jnp.float32),
        lax.psum(hidden_part.astype(jnp.bfloat16), "tp").astype(jnp.float32),
    )
    hidden, d_gate, d_up = activate(gate, up_val, d_hidden)
    grad_wd = lax.dot_general(
        hidden, got_grads, contract_first, preferred_element_type=jnp.float32
    ).astype(jnp.bfloat16)
    grad_wg = lax.dot_general(
        got_rows, d_gate, contract_first, preferred_element_type=jnp.float32
    ).astype(jnp.bfloat16)
    grad_wu = lax.dot_general(
        got_rows, d_up, contract_first, preferred_element_type=jnp.float32
    ).astype(jnp.bfloat16)
    out_sum = jnp.dot(hidden, weight_d, preferred_element_type=jnp.float32).astype(jnp.bfloat16)
    back_sum = (
        lax.dot_general(d_gate, weight_g, contract_last, preferred_element_type=jnp.float32)
        + lax.dot_general(d_up, weight_u, contract_last, preferred_element_type=jnp.float32)
    ).astype(jnp.bfloat16)
    out_sum = out_sum.reshape(1, n_local, n_node * capacity, features)
    back_sum = back_sum.reshape(1, n_local, n_node * capacity, features)
    ret_out, ret_back = (
        lax.all_to_all(
            lax.all_to_all(out_sum, "node", split_axis=2, concat_axis=0, tiled=True),
            "local",
            split_axis=1,
            concat_axis=1,
            tiled=True,
        ),
        lax.all_to_all(
            lax.all_to_all(back_sum, "node", split_axis=2, concat_axis=0, tiled=True),
            "local",
            split_axis=1,
            concat_axis=1,
            tiled=True,
        ),
    )
    slot_out = ret_out.astype(jnp.float32).reshape(n_node, exp_node, 2, capacity, features).sum(2)
    slot_back = ret_back.astype(jnp.float32).reshape(n_node, exp_node, 2, capacity, features).sum(2)
    slot_out = slot_out.astype(jnp.bfloat16)
    slot_back = slot_back.astype(jnp.bfloat16)
    slot_out = slot_out.reshape(experts * capacity, features)
    slot_back = slot_back.reshape(experts * capacity, features)
    gathered = lax.dot_general(
        table_low, slot_out, contract_first, preferred_element_type=jnp.float32
    )
    mixed = jnp.sum(
        gathered.reshape(tok_rows, topk, features) * route_weight[..., None], axis=1
    ).astype(jnp.bfloat16)
    grad_tokens = lax.dot_general(
        token_map, slot_back, contract_first, preferred_element_type=jnp.float32
    ).astype(jnp.bfloat16)
    return (mixed, grad_tokens, grad_wg[None], grad_wu[None], grad_wd[None])


def solution(mesh):
    return jax.shard_map(
        shards,
        mesh=mesh,
        in_specs=(
            P(("node", "local"), "tp"),
            P(("node", "local"), "tp"),
            P(("node", "local"), None),
            P(("node", "local"), None),
            P(("node", "local"), "tp", None),
            P(("node", "local"), "tp", None),
            P(("node", "local"), None, "tp"),
        ),
        out_specs=(
            P(("node", "local"), "tp"),
            P(("node", "local"), "tp"),
            P(("node", "local"), "tp", None),
            P(("node", "local"), "tp", None),
            P(("node", "local"), None, "tp"),
        ),
        check_vma=False,
    )
```

profile of v0, /device:TPU:0, one launch (start us, length us, event | category | flops | bytes accessed | tf_op | source)
XLA Modules:
  0.0 478.0 jit_solution(12791314280433941552)
XLA Ops:
  3.6 2.1 broadcast_in_dim.24
  5.7 6.5 %all-to-all-start = ((bf16[8,4,24,2048]{3,2,1,0:T(8,128)(2,1)}), bf16[8,4,24,2048]{3,2,1,0:T(8,128)(2,1)}, u32[]{:S(2)}, u32[]{:S(2)}) async-start(bf16[8,4,24,2048]{3,2,1,0:T(8,128)(2,1)} %bitcast.88), calls=%async_computation | async-start | bytes 6291456 | tf_op jit(solution)/shard_map/all_to_all | solution.py:52
  13.1 70.8 %all-to-all-done = bf16[8,4,24,2048]{3,2,1,0:T(8,128)(2,1)} async-done(((bf16[8,4,24,2048]{3,2,1,0:T(8,128)(2,1)}), bf16[8,4,24,2048]{3,2,1,0:T(8,128)(2,1)}, u32[]{:S(2)}, u32[]{:S(2)}) %all-to-all-start) | async-done | bytes 3145760 | tf_op jit(solution)/shard_map/all_to_all | solution.py:52
  83.8 2.0 broadcast_in_dim.26
  85.9 4.5 all-to-all-start.4
  90.3 4.0 copy.63
  94.3 67.5 %all-to-all-done.4 = bf16[8,4,24,2048]{3,2,1,0:T(8,128)(2,1)} async-done(((bf16[8,4,24,2048]{3,2,1,0:T(8,128)(2,1)}), bf16[8,4,24,2048]{3,2,1,0:T(8,128)(2,1)}, u32[]{:S(2)}, u32[]{:S(2)}) %all-to-all-start.4) | async-done | bytes 3145760 | tf_op jit(solution)/shard_map/all_to_all | solution.py:59
  161.9 4.7 all-to-all-start.1
  166.5 4.0 copy.70
  170.5 32.3 %all-to-all-done.1 = bf16[1,4,192,2048]{3,2,0,1:T(8,128)(2,1)} async-done(((bf16[1,4,192,2048]{3,2,0,1:T(8,128)(2,1)}), bf16[1,4,192,2048]{3,2,0,1:T(8,128)(2,1)}, u32[]{:S(2)}, u32[]{:S(2)}) %all-to-all-start.1) | async-done | bytes 3145760 | tf_op jit(solution)/shard_map/all_to_all | solution.py:51
  202.8 4.7 all-to-all-start.5
  207.5 4.3 fusion.15
  211.7 3.9 fusion.18
  217.5 4.1 copy.65
  221.6 21.5 %all-to-all-done.5 = bf16[1,4,192,2048]{3,2,0,1:T(8,128)(2,1)} async-done(((bf16[1,4,192,2048]{3,2,0,1:T(8,128)(2,1)}), bf16[1,4,192,2048]{3,2,0,1:T(8,128)(2,1)}, u32[]{:S(2)}, u32[]{:S(2)}) %all-to-all-start.5) | async-done | bytes 3145760 | tf_op jit(solution)/shard_map/all_to_all | solution.py:58
  243.1 4.7 all-to-all-start.2
  247.8 3.8 fusion.21
  251.7 2.0 fusion.10
  253.7 1.9 add_convert_fusion
  255.6 4.1 copy.72
  259.7 59.4 %all-to-all-done.2 = bf16[1,4,192,2048]{3,1,0,2:T(4,128)(2,1)} async-done(((bf16[1,4,192,2048]{3,1,0,2:T(4,128)(2,1)}), bf16[1,4,192,2048]{3,1,0,2:T(4,128)(2,1)}, u32[]{:S(2)}, u32[]{:S(2)}) %all-to-all-start.2) | async-done | bytes 3145760 | tf_op jit(solution)/shard_map/all_to_all | solution.py:103
  319.1 4.5 all-to-all-start.6
  323.6 5.3 %copy.78 = bf16[1,4,8,24,2048]{4,3,2,1,0:T(8,128)(2,1)} copy(bf16[1,4,8,24,2048]{4,1,3,2,0:T(4,128)(2,1)} %bitcast.12) | data formatting | bytes 6291456 | tf_op jit(solution)/shard_map/all_to_all | solution.py:103
  328.8 66.3 %all-to-all-done.6 = bf16[1,4,192,2048]{3,1,0,2:T(4,128)(2,1)} async-done(((bf16[1,4,192,2048]{3,1,0,2:T(4,128)(2,1)}), bf16[1,4,192,2048]{3,1,0,2:T(4,128)(2,1)}, u32[]{:S(2)}, u32[]{:S(2)}) %all-to-all-start.6) | async-done | bytes 3145760 | tf_op jit(solution)/shard_map/all_to_all | solution.py:110
  395.1 3.7 all-to-all-start.3
  398.8 5.3 %copy.77 = bf16[1,4,8,24,2048]{4,3,2,1,0:T(8,128)(2,1)} copy(bf16[1,4,8,24,2048]{4,1,3,2,0:T(4,128)(2,1)} %bitcast.27) | data formatting | bytes 6291456 | tf_op jit(solution)/shard_map/all_to_all | solution.py:110
  404.1 30.8 %all-to-all-done.3 = bf16[8,4,24,2048]{3,2,0,1:T(8,128)(2,1)S(1)} async-done(((bf16[8,4,24,2048]{3,2,0,1:T(8,128)(2,1)}), bf16[8,4,24,2048]{3,2,0,1:T(8,128)(2,1)S(1)}, u32[]{:S(2)}, u32[]{:S(2)}) %all-to-all-start.3) | async-done | bytes 3145760 | tf_op jit(solution)/shard_map/all_to_all | solution.py:102
  436.6 3.9 all-to-all-start.7
  440.6 5.0 %fusion.2 = bf16[1,384,2048]{2,1,0:T(8,128)(2,1)} fusion(bf16[768,2048]{1,0:T(8,128)(2,1)} %bitcast.25, bf16[768,384]{1,0:T(8,128)(2,1)} %copy-done.13, bf16[768,384]{1,0:T(8,128)(2,1)} %copy-done.5), kind=kOutput, calls=%fused_computation.14 | convolution fusion | flops 1211105280 | bytes 5898240 | tf_op jit(solution)/shard_map/dot_general | solution.py:85
  445.6 5.0 %fusion.1 = bf16[1,2048,384]{2,1,0:T(8,128)(2,1)} fusion(bf16[768,2048]{1,0:T(8,128)(2,1)} %bitcast.7, bf16[768,384]{1,0:T(8,128)(2,1)S(1)} %copy-done.9, bf16[768,384]{1,0:T(8,128)(2,1)S(1)} %copy-done.7), kind=kOutput, calls=%fused_computation.13 | convolution fusion | flops 1211105280 | bytes 5898240 | tf_op jit(solution)/shard_map/dot_general | solution.py:91
  450.6 5.2 %fusion = bf16[1,2048,384]{2,1,0:T(8,128)(2,1)} fusion(bf16[768,2048]{1,0:T(8,128)(2,1)} %bitcast.7, bf16[768,384]{1,0:T(8,128)(2,1)S(1)} %copy-done.15, bf16[768,384]{1,0:T(8,128)(2,1)S(1)} %copy-done.9, bf16[768,384]{1,0:T(8,128)(2,1)S(1)} %copy-done.7), kind=kOutput, calls=%fused_computation.12 | convolution fusion | flops 1212579840 | bytes 6488064 | tf_op jit(solution)/shard_map/dot_general | solution.py:88
  458.3 17.5 %all-to-all-done.7 = bf16[8,4,24,2048]{3,2,0,1:T(8,128)(2,1)S(1)} async-done(((bf16[8,4,24,2048]{3,2,0,1:T(8,128)(2,1)}), bf16[8,4,24,2048]{3,2,0,1:T(8,128)(2,1)S(1)}, u32[]{:S(2)}, u32[]{:S(2)}) %all-to-all-start.7) | async-done | bytes 3145760 | tf_op jit(solution)/shard_map/all_to_all | solution.py:109
  (52 shorter events, 12.0 us)
Async XLA Ops:
  0.6 215.0 %copy-start = (bf16[1,384,2048]{2,1,0:T(8,128)(2,1)S(1)}, bf16[1,384,2048]{2,1,0:T(8,128)(2,1)}, u32[]{:S(2)}) copy-start(bf16[1,384,2048]{2,1,0:T(8,128)(2,1)} %param.13) | copy-start | bytes 4718596
  5.7 6.5 %copy-start.11 = (f32[32,8]{0,1:T(8,128)S(1)}, f32[32,8]{0,1:T(8,128)}, u32[]{:S(2)}) copy-start(f32[32,8]{0,1:T(8,128)} %param.10) | copy-start | bytes 3076
  5.7 6.6 %copy-start.10 = (bf16[32,2048]{1,0:T(8,128)(2,1)S(1)}, bf16[32,2048]{1,0:T(8,128)(2,1)}, u32[]{:S(2)}) copy-start(bf16[32,2048]{1,0:T(8,128)(2,1)} %param.8) | copy-start | bytes 393220
  5.7 78.1 %all-to-all-start = ((bf16[8,4,24,2048]{3,2,1,0:T(8,128)(2,1)}), bf16[8,4,24,2048]{3,2,1,0:T(8,128)(2,1)}, u32[]{:S(2)}, u32[]{:S(2)}) async-start(bf16[8,4,24,2048]{3,2,1,0:T(8,128)(2,1)} %bitcast.88), calls=%async_computation | async-start | bytes 6291456 | tf_op jit(solution)/shard_map/all_to_all | solution.py:52
  85.9 76.0 %all-to-all-start.4 = ((bf16[8,4,24,2048]{3,2,1,0:T(8,128)(2,1)}), bf16[8,4,24,2048]{3,2,1,0:T(8,128)(2,1)}, u32[]{:S(2)}, u32[]{:S(2)}) async-start(bf16[8,4,24,2048]{3,2,1,0:T(8,128)(2,1)} %bitcast.92), calls=%async_computation.4 | async-start | bytes 6291456 | tf_op jit(solution)/shard_map/all_to_all | solution.py:59
  161.9 40.9 %all-to-all-start.1 = ((bf16[1,4,192,2048]{3,2,0,1:T(8,128)(2,1)}), bf16[1,4,192,2048]{3,2,0,1:T(8,128)(2,1)}, u32[]{:S(2)}, u32[]{:S(2)}) async-start(bf16[1,4,192,2048]{3,2,0,1:T(8,128)(2,1)} %bitcast.90), calls=%async_computation.1 | async-start | bytes 6291456 | tf_op jit(solution)/shard_map/all_to_all | solution.py:51
  202.8 40.3 %all-to-all-start.5 = ((bf16[1,4,192,2048]{3,2,0,1:T(8,128)(2,1)}), bf16[1,4,192,2048]{3,2,0,1:T(8,128)(2,1)}, u32[]{:S(2)}, u32[]{:S(2)}) async-start(bf16[1,4,192,2048]{3,2,0,1:T(8,128)(2,1)} %bitcast.89), calls=%async_computation.5 | async-start | bytes 6291456 | tf_op jit(solution)/shard_map/all_to_all | solution.py:58
  207.5 4.3 copy-start.4
  211.7 3.9 copy-start.5
  215.7 1.9 copy-start.13
  243.1 76.0 %all-to-all-start.2 = ((bf16[1,4,192,2048]{3,1,0,2:T(4,128)(2,1)}), bf16[1,4,192,2048]{3,1,0,2:T(4,128)(2,1)}, u32[]{:S(2)}, u32[]{:S(2)}) async-start(bf16[1,4,192,2048]{3,1,0,2:T(4,128)(2,1)} %copy.65), calls=%async_computation.2 | async-start | bytes 6291456 | tf_op jit(solution)/shard_map/all_to_all | solution.py:103
  247.7 3.9 copy-start.6
  247.8 3.9 copy-start.12
  247.8 3.9 copy-start.14
  251.7 2.0 copy-start.8
  319.1 76.0 %all-to-all-start.6 = ((bf16[1,4,192,2048]{3,1,0,2:T(4,128)(2,1)}), bf16[1,4,192,2048]{3,1,0,2:T(4,128)(2,1)}, u32[]{:S(2)}, u32[]{:S(2)}) async-start(bf16[1,4,192,2048]{3,1,0,2:T(4,128)(2,1)} %copy.72), calls=%async_computation.6 | async-start | bytes 6291456 | tf_op jit(solution)/shard_map/all_to_all | solution.py:110
  395.1 39.9 %all-to-all-start.3 = ((bf16[8,4,24,2048]{3,2,0,1:T(8,128)(2,1)}), bf16[8,4,24,2048]{3,2,0,1:T(8,128)(2,1)S(1)}, u32[]{:S(2)}, u32[]{:S(2)}) async-start(bf16[8,4,24,2048]{3,2,0,1:T(8,128)(2,1)} %bitcast.91), calls=%async_computation.3 | async-start | bytes 6291456 | tf_op jit(solution)/shard_map/all_to_all | solution.py:102
  435.0 1.7 copy-start.2
  436.6 39.2 %all-to-all-start.7 = ((bf16[8,4,24,2048]{3,2,0,1:T(8,128)(2,1)}), bf16[8,4,24,2048]{3,2,0,1:T(8,128)(2,1)S(1)}, u32[]{:S(2)}, u32[]{:S(2)}) async-start(bf16[8,4,24,2048]{3,2,0,1:T(8,128)(2,1)} %bitcast.86), calls=%async_computation.7 | async-start | bytes 6291456 | tf_op jit(solution)/shard_map/all_to_all | solution.py:109
  440.6 5.0 %copy-start.7 = (bf16[768,384]{1,0:T(8,128)(2,1)S(1)}, bf16[768,384]{1,0:T(8,128)(2,1)}, u32[]{:S(2)}) copy-start(bf16[768,384]{1,0:T(8,128)(2,1)} %copy-done.5) | copy-start | bytes 1769476
  440.6 5.0 %copy-start.9 = (bf16[768,384]{1,0:T(8,128)(2,1)S(1)}, bf16[768,384]{1,0:T(8,128)(2,1)}, u32[]{:S(2)}) copy-start(bf16[768,384]{1,0:T(8,128)(2,1)} %copy-done.8) | copy-start | bytes 1769476
  445.6 5.0 %copy-start.15 = (bf16[768,384]{1,0:T(8,128)(2,1)S(1)}, bf16[768,384]{1,0:T(8,128)(2,1)}, u32[]{:S(2)}) copy-start(bf16[768,384]{1,0:T(8,128)(2,1)} %copy-done.13) | copy-start | bytes 1769476
  450.6 5.2 %copy-start.3 = (bf16[8,4,24,2048]{3,2,0,1:T(8,128)(2,1)S(1)}, bf16[8,4,24,2048]{3,2,0,1:T(8,128)(2,1)}, u32[]{:S(2)}) copy-start(bf16[8,4,24,2048]{3,2,0,1:T(8,128)(2,1)} %copy-done.2) | copy-start | bytes 9437188
  476.6 1.4 copy-start.1
where the time goes:
time: 479 us; the launch traced here: 478 us
  waiting for transfers between devices  366 us (76%)
  matrix products  38 us (8%)
  starting transfers between devices  37 us (8%)
  local copies, waits for them, and re-layouts  34.3 us (7%)
    all_to_all x1, waiting for transfers between devices, shards(): lax.all_to_all(twice_rows, 'node', split_axis=0, concat_axis=2, tiled=True)  70.8 us
    all_to_all x1, waiting for transfers between devices, shards(): lax.all_to_all(twice_grads, 'node', split_axis=0, concat_axis=2, tiled=True)  67.5 us
    all_to_all x1, waiting for transfers between devices, shards(): lax.all_to_all(back_sum, 'node', split_axis=2, concat_axis=0, tiled=True)  66.3 us
    all_to_all x1, waiting for transfers between devices, shards(): lax.all_to_all(out_sum, 'node', split_axis=2, concat_axis=0, tiled=True)  59.4 us
    all_to_all x1, waiting for transfers between devices, shards(): lax.all_to_all(lax.all_to_all(twice_rows, 'node', split_axis=0, concat_ax...  32.3 us
    all_to_all x1, waiting for transfers between devices, shards(): lax.all_to_all(lax.all_to_all(out_sum, 'node', split_axis=2, concat_axis=...  30.8 us
    all_to_all x1, waiting for transfers between devices, shards(): lax.all_to_all(lax.all_to_all(twice_grads, 'node', split_axis=0, concat_a...  21.5 us
    all_to_all x1, waiting for transfers between devices, shards(): lax.all_to_all(lax.all_to_all(back_sum, 'node', split_axis=2, concat_axis...  17.5 us
  transfers between devices with their start and end apart: 8, of which 8 were waited for; matrix products, arithmetic and copies ran while one was open for 13% of the time, Pallas kernels for 0%

commit v1 on v0

v1 whole, which is shorter than its diff:
```python
import functools

import jax
import jax.numpy as jnp
from jax import lax
from jax.experimental import pallas as pl
from jax.experimental.pallas import tpu as pltpu
from jax.sharding import PartitionSpec as P

LANES = 128
CONTRACT_LAST = (((1,), (1,)), ((), ()))
CONTRACT_FIRST = (((0,), (0,)), ((), ()))


def slot_table(route_rows, experts, capacity):
    flat = route_rows.reshape(-1)
    count = flat.shape[0]
    onehot = (flat[:, None] == jnp.arange(experts, dtype=jnp.int32)[None, :]).astype(jnp.float32)
    lower = (jnp.arange(count)[:, None] > jnp.arange(count)[None, :]).astype(jnp.float32)
    before = jnp.dot(lower, onehot, precision=lax.Precision.HIGHEST)
    ranking = jnp.sum(before * onehot, axis=1).astype(jnp.int32)
    position = flat * capacity + ranking
    return (position[None, :] == jnp.arange(experts * capacity, dtype=jnp.int32)[:, None]).astype(
        jnp.float32
    )


def activate(gate, up_val, d_hidden):
    sig_gate = jax.nn.sigmoid(gate)
    activated = gate * sig_gate
    hidden = (activated * up_val).astype(jnp.bfloat16)
    d_gate = (d_hidden * up_val * sig_gate * (1.0 + gate * (1.0 - sig_gate))).astype(jnp.bfloat16)
    d_up = (d_hidden * activated).astype(jnp.bfloat16)
    return (hidden, d_gate, d_up)


def sparse_shards(tokens, grad_out, routes, route_weight, w_gate, w_up, w_down):
    n_node = lax.axis_size("node")
    n_local = lax.axis_size("local")
    experts = n_node * n_local // 2
    exp_node = n_local // 2
    tok_rows, features = tokens.shape
    topk = routes.shape[1]
    capacity = min(tok_rows, max(2, 3 * tok_rows * topk // (2 * experts)))
    table = slot_table(routes, experts, capacity)
    token_map = table.reshape(experts * capacity, tok_rows, topk).sum(-1).astype(jnp.bfloat16)
    table_low = table.astype(jnp.bfloat16)
    send_rows = jnp.dot(token_map, tokens, preferred_element_type=jnp.float32).astype(jnp.bfloat16)
    weights_flat = route_weight.reshape(-1)
    scaled = (
        weights_flat[:, None] * jnp.repeat(grad_out, topk, axis=0).astype(jnp.float32)
    ).astype(jnp.bfloat16)
    send_grads = jnp.dot(table_low, scaled, preferred_element_type=jnp.float32).astype(jnp.bfloat16)

    def dispatch(rows):
        twice = jnp.repeat(rows.reshape(n_node, exp_node, capacity, features), 2, axis=1)
        got = lax.all_to_all(twice, "node", split_axis=0, concat_axis=2, tiled=True)
        got = lax.all_to_all(got, "local", split_axis=1, concat_axis=2, tiled=True)
        return got.reshape(got.shape[2], features)

    def combine(rows):
        rows = rows.reshape(1, n_local, n_node * capacity, features)
        got = lax.all_to_all(rows, "node", split_axis=2, concat_axis=0, tiled=True)
        got = lax.all_to_all(got, "local", split_axis=1, concat_axis=1, tiled=True)
        got = got.astype(jnp.float32).reshape(n_node, exp_node, 2, capacity, features).sum(2)
        return got.astype(jnp.bfloat16).reshape(experts * capacity, features)

    got_rows, got_grads = dispatch(send_rows), dispatch(send_grads)
    weight_g = w_gate[0]
    weight_u = w_up[0]
    weight_d = w_down[0]
    gate_part = jnp.dot(got_rows, weight_g, preferred_element_type=jnp.float32)
    up_part = jnp.dot(got_rows, weight_u, preferred_element_type=jnp.float32)
    hidden_part = lax.dot_general(
        got_grads, weight_d, CONTRACT_LAST, preferred_element_type=jnp.float32
    )
    gate, up_val, d_hidden = (
        lax.psum(gate_part.astype(jnp.bfloat16), "tp").astype(jnp.float32),
        lax.psum(up_part.astype(jnp.bfloat16), "tp").astype(jnp.float32),
        lax.psum(hidden_part.astype(jnp.bfloat16), "tp").astype(jnp.float32),
    )
    hidden, d_gate, d_up = activate(gate, up_val, d_hidden)
    grad_wd = lax.dot_general(
        hidden, got_grads, CONTRACT_FIRST, preferred_element_type=jnp.float32
    ).astype(jnp.bfloat16)
    grad_wg = lax.dot_general(
        got_rows, d_gate, CONTRACT_FIRST, preferred_element_type=jnp.float32
    ).astype(jnp.bfloat16)
    grad_wu = lax.dot_general(
        got_rows, d_up, CONTRACT_FIRST, preferred_element_type=jnp.float32
    ).astype(jnp.bfloat16)
    out_sum = jnp.dot(hidden, weight_d, preferred_element_type=jnp.float32).astype(jnp.bfloat16)
    back_sum = (
        lax.dot_general(d_gate, weight_g, CONTRACT_LAST, preferred_element_type=jnp.float32)
        + lax.dot_general(d_up, weight_u, CONTRACT_LAST, preferred_element_type=jnp.float32)
    ).astype(jnp.bfloat16)
    slot_out, slot_back = combine(out_sum), combine(back_sum)
    gathered = lax.dot_general(
        table_low, slot_out, CONTRACT_FIRST, preferred_element_type=jnp.float32
    )
    mixed = jnp.sum(
        gathered.reshape(tok_rows, topk, features) * route_weight[..., None], axis=1
    ).astype(jnp.bfloat16)
    grad_tokens = lax.dot_general(
        token_map, slot_back, CONTRACT_FIRST, preferred_element_type=jnp.float32
    ).astype(jnp.bfloat16)
    return (mixed, grad_tokens, grad_wg[None], grad_wu[None], grad_wd[None])


def pack_kernel(experts, tok_ref, grad_ref, route_ref, weight_ref, block_ref):
    rows, features = tok_ref.shape
    block_ref[:, :features] = tok_ref[...]
    block_ref[:, features : 2 * features] = grad_ref[...]
    lane = lax.broadcasted_iota(jnp.int32, (rows, LANES), 1)
    expert = lane % experts
    dense = jnp.zeros((rows, LANES), jnp.float32)
    for k in range(route_ref.shape[1]):
        dense += jnp.where(route_ref[:, k : k + 1] == expert, weight_ref[:, k : k + 1], 0.0)
    high = dense.astype(jnp.bfloat16).astype(jnp.float32)
    middle = (dense - high).astype(jnp.bfloat16).astype(jnp.float32)
    low = dense - high - middle
    part = lane // experts
    parts = jnp.where(part == 0, high, jnp.where(part == 1, middle, jnp.where(part == 2, low, 0.0)))
    block_ref[:, 2 * features :] = parts.astype(jnp.bfloat16)


def pack(tokens, grad_out, routes, route_weight, experts):
    rows, features = tokens.shape
    return pl.pallas_call(
        functools.partial(pack_kernel, experts),
        out_shape=jax.ShapeDtypeStruct((rows, 2 * features + LANES), jnp.bfloat16),
    )(tokens, grad_out, routes, route_weight)


def forward_kernel(
    experts, n_blocks, expert_ref, *refs
):
    blocks = refs[:n_blocks]
    wg_ref, wu_ref, wd_ref = refs[n_blocks : n_blocks + 3]
    x_ref, g_ref, keep_ref, send_ref, hid_ref, dgu_ref = refs[n_blocks + 3 : n_blocks + 9]
    wgu, wd, rw, sems, wsems = refs[n_blocks + 9 :]
    features, half = wg_ref.shape
    rows = blocks[0].shape[0]
    w_copies = [
        pltpu.make_async_copy(wg_ref, wgu.at[:, :half], wsems.at[0]),
        pltpu.make_async_copy(wu_ref, wgu.at[:, half:], wsems.at[1]),
        pltpu.make_async_copy(wd_ref, wd, wsems.at[2]),
    ]
    x_copies, g_copies, r_copies = [], [], []
    for i, block in enumerate(blocks):
        place = pl.ds(i * rows, rows)
        x_copies.append(
            pltpu.make_async_copy(block.at[:, :features], x_ref.at[place], sems.at[0, i])
        )
        g_copies.append(
            pltpu.make_async_copy(
                block.at[:, features : 2 * features], g_ref.at[place], sems.at[1, i]
            )
        )
        r_copies.append(
            pltpu.make_async_copy(block.at[:, 2 * features :], rw.at[place], sems.at[2, i])
        )
    for copy in w_copies[:2] + x_copies + r_copies + w_copies[2:] + g_copies:
        copy.start()
    for copy in w_copies[:2] + x_copies + r_copies:
        copy.wait()
    gate_up = jnp.dot(x_ref[...], wgu[...], preferred_element_type=jnp.float32)
    for copy in w_copies[2:] + g_copies:
        copy.wait()
    lane = lax.broadcasted_iota(jnp.int32, rw.shape, 1)
    chosen = (lane % experts == expert_ref[0]) & (lane < 3 * experts)
    weight = jnp.sum(jnp.where(chosen, rw[...].astype(jnp.float32), 0.0), axis=1, keepdims=True)
    d_hidden = (
        lax.dot_general(g_ref[...], wd[...], CONTRACT_LAST, preferred_element_type=jnp.float32)
        * weight
    )
    gate, up_val = gate_up[:, :half], gate_up[:, half:]
    sig_gate = jax.nn.sigmoid(gate)
    activated = gate * sig_gate
    hid_ref[...] = (weight * (activated * up_val)).astype(jnp.bfloat16)
    dgu_ref[:, :half] = (
        d_hidden * up_val * sig_gate * (1.0 + gate * (1.0 - sig_gate))
    ).astype(jnp.bfloat16)
    dgu_ref[:, half:] = (d_hidden * activated).astype(jnp.bfloat16)
    out = jnp.dot(hid_ref[...], wd[...], preferred_element_type=jnp.float32).astype(jnp.bfloat16)
    own = keep_ref.shape[0]
    keep_ref[:, :features] = out[:own]
    send_ref[:, :features] = out[own:]
    back = lax.dot_general(
        dgu_ref[...], wgu[...], CONTRACT_LAST, preferred_element_type=jnp.float32
    ).astype(jnp.bfloat16)
    keep_ref[:, features:] = back[:own]
    send_ref[:, features:] = back[own:]


def forward(expert, blocks, weight_g, weight_u, weight_d, experts):
    rows = blocks[0].shape[0] * len(blocks)
    features, half = weight_g.shape
    bf16 = jnp.bfloat16
    out_shape = (
        jax.ShapeDtypeStruct((rows, features), bf16),
        jax.ShapeDtypeStruct((rows, features), bf16),
        jax.ShapeDtypeStruct((rows // 2, 2 * features), bf16),
        jax.ShapeDtypeStruct((rows // 2, 2 * features), bf16),
        jax.ShapeDtypeStruct((rows, half), bf16),
        jax.ShapeDtypeStruct((rows, 2 * half), bf16),
    )
    return pl.pallas_call(
        functools.partial(forward_kernel, experts, len(blocks)),
        out_shape=out_shape,
        in_specs=[pl.BlockSpec(memory_space=pltpu.SMEM)]
        + [pl.BlockSpec(memory_space=pl.ANY)] * (len(blocks) + 3),
        out_specs=tuple(pl.BlockSpec(memory_space=pltpu.VMEM) for _ in out_shape),
        scratch_shapes=[
            pltpu.VMEM((features, 2 * half), bf16),
            pltpu.VMEM((half, features), bf16),
            pltpu.VMEM((rows, LANES), bf16),
            pltpu.SemaphoreType.DMA((3, len(blocks))),
            pltpu.SemaphoreType.DMA((3,)),
        ],
        compiler_params=pltpu.CompilerParams(vmem_limit_bytes=40 << 20),
        cost_estimate=pl.CostEstimate(
            flops=12 * rows * features * half,
            bytes_accessed=6 * features * half + 16 * rows * features,
            transcendentals=rows * half,
        ),
    )(expert, *blocks, weight_g, weight_u, weight_d)


def grads_kernel(n_slots, *refs):
    xs, gs, hids, dgus = (refs[i * n_slots : (i + 1) * n_slots] for i in range(4))
    gg_ref, gu_ref, gd_ref = refs[4 * n_slots :]
    half = gg_ref.shape[1]

    def product(lefts, rights):
        return sum(
            lax.dot_general(
                left[...], right[...], CONTRACT_FIRST, preferred_element_type=jnp.float32
            )
            for left, right in zip(lefts, rights)
        ).astype(jnp.bfloat16)

    grad_gu = product(xs, dgus)
    gg_ref[...] = grad_gu[:, :half]
    gu_ref[...] = grad_gu[:, half:]
    gd_ref[...] = product(hids, gs)


def weight_grads(xs, gs, hids, dgus):
    features, half, rows = xs[0].shape[1], hids[0].shape[1], xs[0].shape[0]
    tile = 256
    bf16 = jnp.bfloat16
    n_slots = len(xs)
    wide = pl.BlockSpec((rows, tile), lambda f: (0, f))
    return pl.pallas_call(
        functools.partial(grads_kernel, n_slots),
        grid=(features // tile,),
        out_shape=(
            jax.ShapeDtypeStruct((features, half), bf16),
            jax.ShapeDtypeStruct((features, half), bf16),
            jax.ShapeDtypeStruct((half, features), bf16),
        ),
        in_specs=[wide] * (2 * n_slots)
        + [pl.BlockSpec((rows, half), lambda f: (0, 0))] * n_slots
        + [pl.BlockSpec((rows, 2 * half), lambda f: (0, 0))] * n_slots,
        out_specs=(
            pl.BlockSpec((tile, half), lambda f: (f, 0)),
            pl.BlockSpec((tile, half), lambda f: (f, 0)),
            pl.BlockSpec((half, tile), lambda f: (0, f)),
        ),
        compiler_params=pltpu.CompilerParams(vmem_limit_bytes=40 << 20),
        cost_estimate=pl.CostEstimate(
            flops=6 * n_slots * rows * features * half,
            bytes_accessed=6 * features * half + 4 * n_slots * rows * features,
            transcendentals=0,
        ),
    )(*xs, *gs, *hids, *dgus)


def add(left, right):
    return (left.astype(jnp.float32) + right.astype(jnp.float32)).astype(jnp.bfloat16)


def dense_shards(tokens, grad_out, routes, route_weight, w_gate, w_up, w_down):
    n_node, n_local = lax.axis_size("node"), lax.axis_size("local")
    experts = n_node * n_local // 2
    n_z = n_node // 2
    features = tokens.shape[1]
    axes = ("node", "local")
    device = lax.axis_index("node") * n_local + lax.axis_index("local")
    expert = jnp.full((1,), device // 2, jnp.int32)

    def exchange(value, step):
        pairs = [(d, d ^ step((d // n_local) % 2)) for d in range(n_node * n_local)]
        return lax.ppermute(value, axes, pairs)

    first = lambda core: 1 + core
    second = lambda core: 2 - core
    sibling = lambda core: n_local

    block = pack(tokens, grad_out, routes, route_weight, experts)
    slots = [block] + [
        exchange(block, lambda core, z=z: z * 2 * n_local) for z in range(1, n_z)
    ]
    weights = (w_gate[0], w_up[0], w_down[0])
    results = []
    for own in slots:
        one = exchange(own, first)
        two = exchange(own, second)
        both = exchange(one, second)
        plane = [own, one, two, both]
        others = [exchange(part, sibling) for part in plane]
        results.append(forward(expert, plane + others, *weights, experts))
    rows = tokens.shape[0]
    arrived = []
    for z in list(range(1, n_z)) + [0]:
        _, _, keep, send, _, _ = results[z]
        total = add(keep, exchange(send, sibling))
        total = add(total[: 2 * rows], exchange(total[2 * rows :], second))
        total = add(total[:rows], exchange(total[rows:], first))
        arrived.append(exchange(total, lambda core: z * 2 * n_local) if z else total)
    final = sum(part.astype(jnp.float32) for part in arrived).astype(jnp.bfloat16)
    xs, gs, _, _, hids, dgus = (list(column) for column in zip(*results))
    grad_wg, grad_wu, grad_wd = weight_grads(xs, gs, hids, dgus)
    return (
        final[:, :features],
        final[:, features:],
        grad_wg[None],
        grad_wu[None],
        grad_wd[None],
    )


def solution(mesh):
    n_node, n_local, n_tp = (mesh.shape[name] for name in ("node", "local", "tp"))

    def shards(tokens, grad_out, routes, *rest):
        experts = n_node * n_local // 2
        grid = n_tp == 1 and n_local == 4 and n_node in (4, 8)
        if grid and 2 * routes.shape[1] >= experts:
            return dense_shards(tokens, grad_out, routes, *rest)
        return sparse_shards(tokens, grad_out, routes, *rest)

    return jax.shard_map(
        shards,
        mesh=mesh,
        in_specs=(
            P(("node", "local"), "tp"),
            P(("node", "local"), "tp"),
            P(("node", "local"), None),
            P(("node", "local"), None),
            P(("node", "local"), "tp", None),
            P(("node", "local"), "tp", None),
            P(("node", "local"), None, "tp"),
        ),
        out_specs=(
            P(("node", "local"), "tp"),
            P(("node", "local"), "tp"),
            P(("node", "local"), "tp", None),
            P(("node", "local"), "tp", None),
            P(("node", "local"), None, "tp"),
        ),
        check_vma=False,
    )
```

time: 479 us -> 158 us (0.33)
  waiting for transfers between devices: 366 us -> 70.5 us
  matrix products: 38 us -> 0 us
  Pallas kernels: 0 us -> 32.3 us
  local copies, waits for them, and re-layouts: 34.3 us -> 14.4 us
    all_to_all x8 -> x0, waiting for transfers between devices: 366 us -> none  [the longest x1 70.8 us: shards(): lax.all_to_all(twice_rows, 'node', split_axis=0, concat_axis=2, tiled=True)]
    ppermute x0 -> x46, waiting for transfers between devices: none -> 70.5 us  [exchange(): return lax.ppermute(value, axes, pairs)]
    dot_general x14 -> x0, matrix products: 38 us -> none  [the longest x1 5.17 us: shards(): lax.dot_general(got_rows, d_gate, contract_first, preferred_element_type=...]
    all_to_all x8 -> x0, starting transfers between devices: 37 us -> none  [the longest x1 6.45 us: shards(): lax.all_to_all(twice_rows, 'node', split_axis=0, concat_axis=2, tiled=True)]
    ppermute x0 -> x46, starting transfers between devices: none -> 35.2 us  [exchange(): return lax.ppermute(value, axes, pairs)]
    pallas_call x0 -> x6, Pallas kernels: none -> 32.3 us  [the longest x4 21.5 us: forward(): pl.pallas_call(functools.partial(forward_kernel, experts, len(blocks)), o...]
    all_to_all x4 -> x0, local copies, waits for them, and re-layouts: 18.6 us -> none  [the longest x1 5.32 us: shards(): lax.all_to_all(back_sum, 'node', split_axis=2, concat_axis=0, tiled=True)]
    unnamed x34 -> x42, local copies, waits for them, and re-layouts: 2.93 us -> 13.5 us
  transfers between devices with their start and end apart: 8 -> 46, of which waited for: 8 -> 16; matrix products, arithmetic and copies ran while one was open for 13% -> 3% of each run, Pallas kernels for 0% -> 19%
where the time goes in v1:
time: 158 us
  waiting for transfers between devices  70.5 us (45%)
  starting transfers between devices  35.2 us (22%)
  Pallas kernels  32.3 us (20%)
  local copies, waits for them, and re-layouts  14.4 us (9%)
  other arithmetic  4.29 us (3%)
    ppermute x46, waiting for transfers between devices, exchange(): return lax.ppermute(value, axes, pairs)  70.5 us
    ppermute x46, starting transfers between devices, exchange(): return lax.ppermute(value, axes, pairs)  35.2 us
    pallas_call x4, Pallas kernels, forward(): pl.pallas_call(functools.partial(forward_kernel, experts, len(blocks)), o...  21.5 us
    unnamed x42, local copies, waits for them, and re-layouts  13.5 us
    pallas_call x1, Pallas kernels, weight_grads(): pl.pallas_call(functools.partial(grads_kernel, n_slots), grid=(features /...  8.97 us
    convert_element_type x11, other arithmetic, add(): (left.astype(jnp.float32) + right.astype(jnp.float32)).astype(jnp.bfloat16)  4.11 us
  transfers between devices with their start and end apart: 46, of which 16 were waited for; matrix products, arithmetic and copies ran while one was open for 3% of the time, Pallas kernels for 19%

profile of v1, /device:TPU:0, one launch (start us, length us, event | category | flops | bytes accessed | tf_op | source)
XLA Modules:
  0.0 157.7 jit_solution(15620748374055414523)
XLA Ops:
  0.6 1.4 copy.12.route_ref
  3.4 1.8 %shard_map.110.refs_0_ = bf16[32,4224]{1,0:T(8,128)(2,1)} custom-call(bf16[32,2048]{1,0:T(8,128)(2,1)} %tok_ref.1, bf16[32,2048]{1,0:T(8,128)(2,1)} %grad_ref.1, s32[32,8]{1,0:T(8,128)} %copy.12.route_ref, f32[32,8]{1,0:T(8,128)} %copy.13.weight_ref), custom_call_target="tpu_custom_call" | custom-call | tf_op jit(solution)/shard_map/pallas_call | solution.py:129
  5.2 5.0 %collective-permute-start.24 = (bf16[32,4224]{1,0:T(8,128)(2,1)}, bf16[32,4224]{1,0:T(8,128)(2,1)S(1)}, u32[]{:S(2)}, u32[]{:S(2)}) collective-permute-start(bf16[32,4224]{1,0:T(8,128)(2,1)} %shard_map.110.refs_0_), channel_id=1, source_target_pairs={{0,24},{1,25},{2,26},{3,27},{4,28},{5,29},{6,30},{7,31},{8,16},{9,... | collective-permute-start | bytes 811016 | tf_op jit(solution)/shard_map/ppermute | solution.py:295
  10.8 1.7 %collective-permute-start.36 = (bf16[32,4224]{1,0:T(8,128)(2,1)}, bf16[32,4224]{1,0:T(8,128)(2,1)S(1)}, u32[]{:S(2)}, u32[]{:S(2)}) collective-permute-start(bf16[32,4224]{1,0:T(8,128)(2,1)} %shard_map.110.refs_0_), channel_id=1, source_target_pairs={{0,1},{1,0},{2,3},{3,2},{4,6},{5,7},{6,4},{7,5},{8,9},{9,8},{10,11... | collective-permute-start | bytes 811016 | tf_op jit(solution)/shard_map/ppermute | solution.py:295
  12.5 1.5 collective-permute-start.37
  14.0 3.9 %collective-permute-done.24.refs_0_ = bf16[32,4224]{1,0:T(8,128)(2,1)S(1)} collective-permute-done((bf16[32,4224]{1,0:T(8,128)(2,1)}, bf16[32,4224]{1,0:T(8,128)(2,1)S(1)}, u32[]{:S(2)}, u32[]{:S(2)}) %collective-permute-start.24) | collective-permute-done | bytes 270368 | tf_op jit(solution)/shard_map/ppermute | solution.py:295
  17.9 15.6 %collective-permute-done.12.refs_0_ = bf16[32,4224]{1,0:T(8,128)(2,1)S(1)} collective-permute-done((bf16[32,4224]{1,0:T(8,128)(2,1)}, bf16[32,4224]{1,0:T(8,128)(2,1)S(1)}, u32[]{:S(2)}, u32[]{:S(2)}) %collective-permute-start.12) | collective-permute-done | bytes 270368 | tf_op jit(solution)/shard_map/ppermute | solution.py:295
  33.5 1.5 collective-permute-start.25
  35.0 1.5 collective-permute-start.26
  38.3 4.5 %collective-permute-done.25.refs_1_ = bf16[32,4224]{1,0:T(8,128)(2,1)S(1)} collective-permute-done((bf16[32,4224]{1,0:T(8,128)(2,1)S(1)}, bf16[32,4224]{1,0:T(8,128)(2,1)S(1)}, u32[]{:S(2)}, u32[]{:S(2)}) %collective-permute-start.25) | collective-permute-done | bytes 270368 | tf_op jit(solution)/shard_map/ppermute | solution.py:295
  43.3 2.5 %collective-permute-start.38 = (bf16[32,4224]{1,0:T(8,128)(2,1)S(1)}, bf16[32,4224]{1,0:T(8,128)(2,1)}, u32[]{:S(2)}, u32[]{:S(2)}) collective-permute-start(bf16[32,4224]{1,0:T(8,128)(2,1)S(1)} %collective-permute-done.36.refs_1_), channel_id=1, source_target_pairs={{0,2},{1,3},{2,0},{3,1},{4,5},{5,4},{6,7},{7,6},{8,10},{9,11},{10,... | collective-permute-start | bytes 811016 | tf_op jit(solution)/shard_map/ppermute | solution.py:295
  46.4 2.2 %collective-permute-done.13.refs_1_ = bf16[32,4224]{1,0:T(8,128)(2,1)S(1)} collective-permute-done((bf16[32,4224]{1,0:T(8,128)(2,1)S(1)}, bf16[32,4224]{1,0:T(8,128)(2,1)S(1)}, u32[]{:S(2)}, u32[]{:S(2)}) %collective-permute-start.13) | collective-permute-done | bytes 270368 | tf_op jit(solution)/shard_map/ppermute | solution.py:295
  49.7 3.4 %collective-permute-done.38.refs_3_ = bf16[32,4224]{1,0:T(8,128)(2,1)} collective-permute-done((bf16[32,4224]{1,0:T(8,128)(2,1)S(1)}, bf16[32,4224]{1,0:T(8,128)(2,1)}, u32[]{:S(2)}, u32[]{:S(2)}) %collective-permute-start.38) | collective-permute-done | bytes 270368 | tf_op jit(solution)/shard_map/ppermute | solution.py:295
  53.1 2.0 %collective-permute-done.1.refs_1_ = bf16[32,4224]{1,0:T(8,128)(2,1)S(1)} collective-permute-done((bf16[32,4224]{1,0:T(8,128)(2,1)S(1)}, bf16[32,4224]{1,0:T(8,128)(2,1)S(1)}, u32[]{:S(2)}, u32[]{:S(2)}) %collective-permute-start.1) | collective-permute-done | bytes 270368 | tf_op jit(solution)/shard_map/ppermute | solution.py:295
  58.9 1.4 copy-done.1
  60.3 1.4 copy-done.3
  61.7 1.4 copy-done.5
  64.1 5.8 %shard_map.114 = (bf16[256,2048]{1,0:T(8,128)(2,1)S(1)}, bf16[256,2048]{1,0:T(8,128)(2,1)S(1)}, bf16[128,4096]{1,0:T(8,128)(2,1)S(1)}, bf16[128,4096]{1,0:T(8,12...) custom-call(s32[1]{0:T(128)} %bitcast.expert_ref, bf16[32,4224]{1,0:T(8,128)(2,1)S(1)} %copy-done, ...), custom_call_target="tpu_custom_call" | custom-call | flops 2415919104 | bytes 13107200 | tf_op jit(solution)/shard_map/pallas_call | solution.py:208
  74.6 3.2 %collective-permute-done.3.refs_3_ = bf16[32,4224]{1,0:T(8,128)(2,1)S(1)} collective-permute-done((bf16[32,4224]{1,0:T(8,128)(2,1)S(1)}, bf16[32,4224]{1,0:T(8,128)(2,1)S(1)}, u32[]{:S(2)}, u32[]{:S(2)}) %collective-permute-start.3) | collective-permute-done | bytes 270368 | tf_op jit(solution)/shard_map/ppermute | solution.py:295
  78.4 5.3 %shard_map.113 = (bf16[256,2048]{1,0:T(8,128)(2,1)S(1)}, bf16[256,2048]{1,0:T(8,128)(2,1)S(1)}, bf16[128,4096]{1,0:T(8,128)(2,1)S(1)}, bf16[128,4096]{1,0:T(8,12...) custom-call(s32[1]{0:T(128)} %bitcast.expert_ref, ...), custom_call_target="tpu_custom_call" | custom-call | flops 2415919104 | bytes 13107200 | tf_op jit(solution)/shard_map/pallas_call | solution.py:208
  84.8 5.1 %shard_map.112 = (bf16[256,2048]{1,0:T(8,128)(2,1)S(1)}, bf16[256,2048]{1,0:T(8,128)(2,1)S(1)}, bf16[128,4096]{1,0:T(8,128)(2,1)S(1)}, bf16[128,4096]{1,0:T(8,12...) custom-call(s32[1]{0:T(128)} %bitcast.expert_ref, ...), custom_call_target="tpu_custom_call" | custom-call | flops 2415919104 | bytes 13107200 | tf_op jit(solution)/shard_map/pallas_call | solution.py:208
  92.4 5.3 %shard_map.111 = (bf16[256,2048]{1,0:T(8,128)(2,1)S(1)}, bf16[256,2048]{1,0:T(8,128)(2,1)S(1)}, bf16[128,4096]{1,0:T(8,128)(2,1)S(1)}, bf16[128,4096]{1,0:T(8,12...) custom-call(s32[1]{0:T(128)} %bitcast.expert_ref, ...), custom_call_target="tpu_custom_call" | custom-call | flops 2415919104 | bytes 13107200 | tf_op jit(solution)/shard_map/pallas_call | solution.py:208
  98.2 1.5 add_convert_fusion
  100.9 1.5 add_convert_fusion.1
  106.1 2.8 %collective-permute-done.44 = bf16[64,4096]{1,0:T(8,128)(2,1)S(1)} collective-permute-done((bf16[64,4096]{1,0:T(8,128)(2,1)S(1)}, bf16[64,4096]{1,0:T(8,128)(2,1)S(1)}, u32[]{:S(2)}, u32[]{:S(2)}) %collective-permute-start.44) | collective-permute-done | bytes 524320 | tf_op jit(solution)/shard_map/ppermute | solution.py:295
  110.4 7.0 %collective-permute-done.33 = bf16[64,4096]{1,0:T(8,128)(2,1)S(1)} collective-permute-done((bf16[64,4096]{1,0:T(8,128)(2,1)S(1)}, bf16[64,4096]{1,0:T(8,128)(2,1)S(1)}, u32[]{:S(2)}, u32[]{:S(2)}) %collective-permute-start.33) | collective-permute-done | bytes 524320 | tf_op jit(solution)/shard_map/ppermute | solution.py:295
  118.8 7.0 %collective-permute-done.21 = bf16[64,4096]{1,0:T(8,128)(2,1)S(1)} collective-permute-done((bf16[64,4096]{1,0:T(8,128)(2,1)S(1)}, bf16[64,4096]{1,0:T(8,128)(2,1)S(1)}, u32[]{:S(2)}, u32[]{:S(2)}) %collective-permute-start.21) | collective-permute-done | bytes 524320 | tf_op jit(solution)/shard_map/ppermute | solution.py:295
  127.2 7.0 %collective-permute-done.9 = bf16[64,4096]{1,0:T(8,128)(2,1)S(1)} collective-permute-done((bf16[64,4096]{1,0:T(8,128)(2,1)S(1)}, bf16[64,4096]{1,0:T(8,128)(2,1)S(1)}, u32[]{:S(2)}, u32[]{:S(2)}) %collective-permute-start.9) | collective-permute-done | bytes 524320 | tf_op jit(solution)/shard_map/ppermute | solution.py:295
  135.7 2.4 %collective-permute-start.35 = (bf16[32,4096]{1,0:T(8,128)(2,1)S(1)}, bf16[32,4096]{1,0:T(8,128)(2,1)S(1)}, u32[]{:S(2)}, u32[]{:S(2)}) collective-permute-start(bf16[32,4096]{1,0:T(8,128)(2,1)S(1)} %add_convert_fusion.10), channel_id=1, source_target_pairs={{0,24},{1,25},{2,26},{3,27},{4,28},{5,29},{6,30},{7,31},{8,16},{9,... | collective-permute-start | bytes 786440 | tf_op jit(solution)/shard_map/ppermute | solution.py:295
  138.2 2.6 %collective-permute-done.10 = bf16[32,4096]{1,0:T(8,128)(2,1)S(1)} collective-permute-done((bf16[32,4096]{1,0:T(8,128)(2,1)S(1)}, bf16[32,4096]{1,0:T(8,128)(2,1)S(1)}, u32[]{:S(2)}, u32[]{:S(2)}) %collective-permute-start.10) | collective-permute-done | bytes 262176 | tf_op jit(solution)/shard_map/ppermute | solution.py:295
  141.1 9.0 %shard_map.115 = (bf16[2048,384]{1,0:T(8,128)(2,1)}, bf16[2048,384]{1,0:T(8,128)(2,1)}, bf16[384,2048]{1,0:T(8,128)(2,1)}) custom-call(bf16[256,2048]{1,0:T(8,128)(2,1)S(1)} %get-tuple-element.40.refs_0_, bf16[256,2048]{1,0:T(8,128)(2,1)S(1)} %get-tuple-element.41.refs_1_, bf16[256,2048]{1,0:T(8,128)(2,1)S(1)} %copy-done.15, ...), custom_call_target="tpu_custom_call" | custom-call | flops 4831838208 | bytes 13107200 | tf_op jit(solution)/shard_map/pallas_call | solution.py:255
  150.0 6.8 %collective-permute-done.23 = bf16[32,4096]{1,0:T(8,128)(2,1)S(1)} collective-permute-done((bf16[32,4096]{1,0:T(8,128)(2,1)S(1)}, bf16[32,4096]{1,0:T(8,128)(2,1)S(1)}, u32[]{:S(2)}, u32[]{:S(2)}) %collective-permute-start.23) | collective-permute-done | bytes 262176 | tf_op jit(solution)/shard_map/ppermute | solution.py:295
  (129 shorter events, 31.8 us)
Async XLA Ops:
  5.2 12.7 %collective-permute-start.24 = (bf16[32,4224]{1,0:T(8,128)(2,1)}, bf16[32,4224]{1,0:T(8,128)(2,1)S(1)}, u32[]{:S(2)}, u32[]{:S(2)}) collective-permute-start(bf16[32,4224]{1,0:T(8,128)(2,1)} %shard_map.110.refs_0_), channel_id=1, source_target_pairs={{0,24},{1,25},{2,26},{3,27},{4,28},{5,29},{6,30},{7,31},{8,16},{9,... | collective-permute-start | bytes 811016 | tf_op jit(solution)/shard_map/ppermute | solution.py:295
  10.2 23.2 %collective-permute-start.12 = (bf16[32,4224]{1,0:T(8,128)(2,1)}, bf16[32,4224]{1,0:T(8,128)(2,1)S(1)}, u32[]{:S(2)}, u32[]{:S(2)}) collective-permute-start(bf16[32,4224]{1,0:T(8,128)(2,1)} %shard_map.110.refs_0_), channel_id=1, source_target_pairs={{0,16},{1,17},{2,18},{3,19},{4,20},{5,21},{6,22},{7,23},{8,24},{9,... | collective-permute-start | bytes 811016 | tf_op jit(solution)/shard_map/ppermute | solution.py:295
  10.2 24.7 %collective-permute-start = (bf16[32,4224]{1,0:T(8,128)(2,1)}, bf16[32,4224]{1,0:T(8,128)(2,1)S(1)}, u32[]{:S(2)}, u32[]{:S(2)}) collective-permute-start(bf16[32,4224]{1,0:T(8,128)(2,1)} %shard_map.110.refs_0_), channel_id=1, source_target_pairs={{0,8},{1,9},{2,10},{3,11},{4,12},{5,13},{6,14},{7,15},{8,0},{9,1},... | collective-permute-start | bytes 811016 | tf_op jit(solution)/shard_map/ppermute | solution.py:295
  10.8 25.7 %collective-permute-start.36 = (bf16[32,4224]{1,0:T(8,128)(2,1)}, bf16[32,4224]{1,0:T(8,128)(2,1)S(1)}, u32[]{:S(2)}, u32[]{:S(2)}) collective-permute-start(bf16[32,4224]{1,0:T(8,128)(2,1)} %shard_map.110.refs_0_), channel_id=1, source_target_pairs={{0,1},{1,0},{2,3},{3,2},{4,6},{5,7},{6,4},{7,5},{8,9},{9,8},{10,11... | collective-permute-start | bytes 811016 | tf_op jit(solution)/shard_map/ppermute | solution.py:295
  12.5 24.0 %collective-permute-start.37 = (bf16[32,4224]{1,0:T(8,128)(2,1)}, bf16[32,4224]{1,0:T(8,128)(2,1)S(1)}, u32[]{:S(2)}, u32[]{:S(2)}) collective-permute-start(bf16[32,4224]{1,0:T(8,128)(2,1)} %shard_map.110.refs_0_), channel_id=1, source_target_pairs={{0,2},{1,3},{2,0},{3,1},{4,5},{5,4},{6,7},{7,6},{8,10},{9,11},{10,... | collective-permute-start | bytes 811016 | tf_op jit(solution)/shard_map/ppermute | solution.py:295
  17.9 19.2 %collective-permute-start.39 = (bf16[32,4224]{1,0:T(8,128)(2,1)}, bf16[32,4224]{1,0:T(8,128)(2,1)S(1)}, u32[]{:S(2)}, u32[]{:S(2)}) collective-permute-start(bf16[32,4224]{1,0:T(8,128)(2,1)} %shard_map.110.refs_0_), channel_id=1, source_target_pairs={{0,4},{1,5},{2,6},{3,7},{4,0},{5,1},{6,2},{7,3},{8,12},{9,13},{10,... | collective-permute-start | bytes 811016 | tf_op jit(solution)/shard_map/ppermute | solution.py:295
  33.5 9.3 %collective-permute-start.25 = (bf16[32,4224]{1,0:T(8,128)(2,1)S(1)}, bf16[32,4224]{1,0:T(8,128)(2,1)S(1)}, u32[]{:S(2)}, u32[]{:S(2)}) collective-permute-start(bf16[32,4224]{1,0:T(8,128)(2,1)S(1)} %collective-permute-done.24.refs_0_), channel_id=1, source_target_pairs={{0,1},{1,0},{2,3},{3,2},{4,6},{5,7},{6,4},{7,5},{8,9},{9,8},{10,11... | collective-permute-start | bytes 811016 | tf_op jit(solution)/shard_map/ppermute | solution.py:295
  36.5 9.3 %collective-permute-start.28 = (bf16[32,4224]{1,0:T(8,128)(2,1)S(1)}, bf16[32,4224]{1,0:T(8,128)(2,1)S(1)}, u32[]{:S(2)}, u32[]{:S(2)}) collective-permute-start(bf16[32,4224]{1,0:T(8,128)(2,1)S(1)} %collective-permute-done.24.refs_0_), channel_id=1, source_target_pairs={{0,4},{1,5},{2,6},{3,7},{4,0},{5,1},{6,2},{7,3},{8,12},{9,13},{10,... | collective-permute-start | bytes 811016 | tf_op jit(solution)/shard_map/ppermute | solution.py:295
  36.5 12.1 %collective-permute-start.13 = (bf16[32,4224]{1,0:T(8,128)(2,1)S(1)}, bf16[32,4224]{1,0:T(8,128)(2,1)S(1)}, u32[]{:S(2)}, u32[]{:S(2)}) collective-permute-start(bf16[32,4224]{1,0:T(8,128)(2,1)S(1)} %collective-permute-done.12.refs_0_), channel_id=1, source_target_pairs={{0,1},{1,0},{2,3},{3,2},{4,6},{5,7},{6,4},{7,5},{8,9},{9,8},{10,11... | collective-permute-start | bytes 811016 | tf_op jit(solution)/shard_map/ppermute | solution.py:295
  37.8 11.4 %collective-permute-start.14 = (bf16[32,4224]{1,0:T(8,128)(2,1)S(1)}, bf16[32,4224]{1,0:T(8,128)(2,1)S(1)}, u32[]{:S(2)}, u32[]{:S(2)}) collective-permute-start(bf16[32,4224]{1,0:T(8,128)(2,1)S(1)} %collective-permute-done.12.refs_0_), channel_id=1, source_target_pairs={{0,2},{1,3},{2,0},{3,1},{4,5},{5,4},{6,7},{7,6},{8,10},{9,11},{10,... | collective-permute-start | bytes 811016 | tf_op jit(solution)/shard_map/ppermute | solution.py:295
  43.3 9.8 %collective-permute-start.38 = (bf16[32,4224]{1,0:T(8,128)(2,1)S(1)}, bf16[32,4224]{1,0:T(8,128)(2,1)}, u32[]{:S(2)}, u32[]{:S(2)}) collective-permute-start(bf16[32,4224]{1,0:T(8,128)(2,1)S(1)} %collective-permute-done.36.refs_1_), channel_id=1, source_target_pairs={{0,2},{1,3},{2,0},{3,1},{4,5},{5,4},{6,7},{7,6},{8,10},{9,11},{10,... | collective-permute-start | bytes 811016 | tf_op jit(solution)/shard_map/ppermute | solution.py:295
  45.8 9.4 %collective-permute-start.1 = (bf16[32,4224]{1,0:T(8,128)(2,1)S(1)}, bf16[32,4224]{1,0:T(8,128)(2,1)S(1)}, u32[]{:S(2)}, u32[]{:S(2)}) collective-permute-start(bf16[32,4224]{1,0:T(8,128)(2,1)S(1)} %collective-permute-done.refs_0_), channel_id=1, source_target_pairs={{0,1},{1,0},{2,3},{3,2},{4,6},{5,7},{6,4},{7,5},{8,9},{9,8},{10,11... | collective-permute-start | bytes 811016 | tf_op jit(solution)/shard_map/ppermute | solution.py:295
  55.2 15.7 %collective-permute-start.27 = (bf16[32,4224]{1,0:T(8,128)(2,1)S(1)}, bf16[32,4224]{1,0:T(8,128)(2,1)}, u32[]{:S(2)}, u32[]{:S(2)}) collective-permute-start(bf16[32,4224]{1,0:T(8,128)(2,1)S(1)} %collective-permute-done.25.refs_1_), channel_id=1, source_target_pairs={{0,2},{1,3},{2,0},{3,1},{4,5},{5,4},{6,7},{7,6},{8,10},{9,11},{10,... | collective-permute-start | bytes 811016 | tf_op jit(solution)/shard_map/ppermute | solution.py:295
  55.9 15.3 %collective-permute-start.29 = (bf16[32,4224]{1,0:T(8,128)(2,1)S(1)}, bf16[32,4224]{1,0:T(8,128)(2,1)S(1)}, u32[]{:S(2)}, u32[]{:S(2)}) collective-permute-start(bf16[32,4224]{1,0:T(8,128)(2,1)S(1)} %collective-permute-done.25.refs_1_), channel_id=1, source_target_pairs={{0,4},{1,5},{2,6},{3,7},{4,0},{5,1},{6,2},{7,3},{8,12},{9,13},{10,... | collective-permute-start | bytes 811016 | tf_op jit(solution)/shard_map/ppermute | solution.py:295
  56.6 16.0 %collective-permute-start.15 = (bf16[32,4224]{1,0:T(8,128)(2,1)S(1)}, bf16[32,4224]{1,0:T(8,128)(2,1)S(1)}, u32[]{:S(2)}, u32[]{:S(2)}) collective-permute-start(bf16[32,4224]{1,0:T(8,128)(2,1)S(1)} %collective-permute-done.13.refs_1_), channel_id=1, source_target_pairs={{0,2},{1,3},{2,0},{3,1},{4,5},{5,4},{6,7},{7,6},{8,10},{9,11},{10,... | collective-permute-start | bytes 811016 | tf_op jit(solution)/shard_map/ppermute | solution.py:295
  57.4 15.1 %collective-permute-start.17 = (bf16[32,4224]{1,0:T(8,128)(2,1)S(1)}, bf16[32,4224]{1,0:T(8,128)(2,1)S(1)}, u32[]{:S(2)}, u32[]{:S(2)}) collective-permute-start(bf16[32,4224]{1,0:T(8,128)(2,1)S(1)} %collective-permute-done.13.refs_1_), channel_id=1, source_target_pairs={{0,4},{1,5},{2,6},{3,7},{4,0},{5,1},{6,2},{7,3},{8,12},{9,13},{10,... | collective-permute-start | bytes 811016 | tf_op jit(solution)/shard_map/ppermute | solution.py:295
  57.8 13.6 %collective-permute-start.30 = (bf16[32,4224]{1,0:T(8,128)(2,1)S(1)}, bf16[32,4224]{1,0:T(8,128)(2,1)S(1)}, u32[]{:S(2)}, u32[]{:S(2)}) collective-permute-start(bf16[32,4224]{1,0:T(8,128)(2,1)S(1)} %collective-permute-done.26.refs_2_), channel_id=1, source_target_pairs={{0,4},{1,5},{2,6},{3,7},{4,0},{5,1},{6,2},{7,3},{8,12},{9,13},{10,... | collective-permute-start | bytes 811016 | tf_op jit(solution)/shard_map/ppermute | solution.py:295
  70.9 27.3 %collective-permute-start.43 = (bf16[128,4096]{1,0:T(8,128)(2,1)S(1)}, bf16[128,4096]{1,0:T(8,128)(2,1)}, u32[]{:S(2)}, u32[]{:S(2)}) collective-permute-start(bf16[128,4096]{1,0:T(8,128)(2,1)S(1)} %get-tuple-element.39), channel_id=1, source_target_pairs={{0,4},{1,5},{2,6},{3,7},{4,0},{5,1},{6,2},{7,3},{8,12},{9,13},{10,... | collective-permute-start | bytes 3145736 | tf_op jit(solution)/shard_map/ppermute | solution.py:295
  74.3 17.6 %collective-permute-start.4 = (bf16[32,4224]{1,0:T(8,128)(2,1)S(1)}, bf16[32,4224]{1,0:T(8,128)(2,1)S(1)}, u32[]{:S(2)}, u32[]{:S(2)}) collective-permute-start(bf16[32,4224]{1,0:T(8,128)(2,1)S(1)} %collective-permute-done.refs_0_), channel_id=1, source_target_pairs={{0,4},{1,5},{2,6},{3,7},{4,0},{5,1},{6,2},{7,3},{8,12},{9,13},{10,... | collective-permute-start | bytes 811016 | tf_op jit(solution)/shard_map/ppermute | solution.py:295
  77.9 14.4 %collective-permute-start.5 = (bf16[32,4224]{1,0:T(8,128)(2,1)S(1)}, bf16[32,4224]{1,0:T(8,128)(2,1)S(1)}, u32[]{:S(2)}, u32[]{:S(2)}) collective-permute-start(bf16[32,4224]{1,0:T(8,128)(2,1)S(1)} %collective-permute-done.1.refs_1_), channel_id=1, source_target_pairs={{0,4},{1,5},{2,6},{3,7},{4,0},{5,1},{6,2},{7,3},{8,12},{9,13},{10,... | collective-permute-start | bytes 811016 | tf_op jit(solution)/shard_map/ppermute | solution.py:295
  77.9 14.5 %collective-permute-start.6 = (bf16[32,4224]{1,0:T(8,128)(2,1)S(1)}, bf16[32,4224]{1,0:T(8,128)(2,1)S(1)}, u32[]{:S(2)}, u32[]{:S(2)}) collective-permute-start(bf16[32,4224]{1,0:T(8,128)(2,1)S(1)} %collective-permute-done.2.refs_2_), channel_id=1, source_target_pairs={{0,4},{1,5},{2,6},{3,7},{4,0},{5,1},{6,2},{7,3},{8,12},{9,13},{10,... | collective-permute-start | bytes 811016 | tf_op jit(solution)/shard_map/ppermute | solution.py:295
  78.4 14.0 %collective-permute-start.7 = (bf16[32,4224]{1,0:T(8,128)(2,1)S(1)}, bf16[32,4224]{1,0:T(8,128)(2,1)S(1)}, u32[]{:S(2)}, u32[]{:S(2)}) collective-permute-start(bf16[32,4224]{1,0:T(8,128)(2,1)S(1)} %collective-permute-done.3.refs_3_), channel_id=1, source_target_pairs={{0,4},{1,5},{2,6},{3,7},{4,0},{5,1},{6,2},{7,3},{8,12},{9,13},{10,... | collective-permute-start | bytes 811016 | tf_op jit(solution)/shard_map/ppermute | solution.py:295
  92.3 11.1 %collective-permute-start.20 = (bf16[128,4096]{1,0:T(8,128)(2,1)S(1)}, bf16[128,4096]{1,0:T(8,128)(2,1)S(1)}, u32[]{:S(2)}, u32[]{:S(2)}) collective-permute-start(bf16[128,4096]{1,0:T(8,128)(2,1)S(1)} %get-tuple-element.35), channel_id=1, source_target_pairs={{0,4},{1,5},{2,6},{3,7},{4,0},{5,1},{6,2},{7,3},{8,12},{9,13},{10,... | collective-permute-start | bytes 3145736 | tf_op jit(solution)/shard_map/ppermute | solution.py:295
  102.4 14.9 %collective-permute-start.33 = (bf16[64,4096]{1,0:T(8,128)(2,1)S(1)}, bf16[64,4096]{1,0:T(8,128)(2,1)S(1)}, u32[]{:S(2)}, u32[]{:S(2)}) collective-permute-start(bf16[64,4096]{1,0:T(8,128)(2,1)S(1)} %slice.81), channel_id=1, source_target_pairs={{0,2},{1,3},{2,0},{3,1},{4,5},{5,4},{6,7},{7,6},{8,10},{9,11},{10,... | collective-permute-start | bytes 1572872 | tf_op jit(solution)/shard_map/ppermute | solution.py:295
  103.7 22.1 %collective-permute-start.21 = (bf16[64,4096]{1,0:T(8,128)(2,1)S(1)}, bf16[64,4096]{1,0:T(8,128)(2,1)S(1)}, u32[]{:S(2)}, u32[]{:S(2)}) collective-permute-start(bf16[64,4096]{1,0:T(8,128)(2,1)S(1)} %slice.77), channel_id=1, source_target_pairs={{0,2},{1,3},{2,0},{3,1},{4,5},{5,4},{6,7},{7,6},{8,10},{9,11},{10,... | collective-permute-start | bytes 1572872 | tf_op jit(solution)/shard_map/ppermute | solution.py:295
  105.2 29.0 %collective-permute-start.9 = (bf16[64,4096]{1,0:T(8,128)(2,1)S(1)}, bf16[64,4096]{1,0:T(8,128)(2,1)S(1)}, u32[]{:S(2)}, u32[]{:S(2)}) collective-permute-start(bf16[64,4096]{1,0:T(8,128)(2,1)S(1)} %slice.73), channel_id=1, source_target_pairs={{0,2},{1,3},{2,0},{3,1},{4,5},{5,4},{6,7},{7,6},{8,10},{9,11},{10,... | collective-permute-start | bytes 1572872 | tf_op jit(solution)/shard_map/ppermute | solution.py:295
  109.1 40.9 %collective-permute-start.45 = (bf16[32,4096]{1,0:T(8,128)(2,1)S(1)}, bf16[32,4096]{1,0:T(8,128)(2,1)S(1)}, u32[]{:S(2)}, u32[]{:S(2)}) collective-permute-start(bf16[32,4096]{1,0:T(8,128)(2,1)S(1)} %slice.87), channel_id=1, source_target_pairs={{0,1},{1,0},{2,3},{3,2},{4,6},{5,7},{6,4},{7,5},{8,9},{9,8},{10,11... | collective-permute-start | bytes 786440 | tf_op jit(solution)/shard_map/ppermute | solution.py:295
  117.5 18.1 %collective-permute-start.34 = (bf16[32,4096]{1,0:T(8,128)(2,1)S(1)}, bf16[32,4096]{1,0:T(8,128)(2,1)S(1)}, u32[]{:S(2)}, u32[]{:S(2)}) collective-permute-start(bf16[32,4096]{1,0:T(8,128)(2,1)S(1)} %slice.83), channel_id=1, source_target_pairs={{0,1},{1,0},{2,3},{3,2},{4,6},{5,7},{6,4},{7,5},{8,9},{9,8},{10,11... | collective-permute-start | bytes 786440 | tf_op jit(solution)/shard_map/ppermute | solution.py:295
  126.0 12.1 %collective-permute-start.22 = (bf16[32,4096]{1,0:T(8,128)(2,1)S(1)}, bf16[32,4096]{1,0:T(8,128)(2,1)S(1)}, u32[]{:S(2)}, u32[]{:S(2)}) collective-permute-start(bf16[32,4096]{1,0:T(8,128)(2,1)S(1)} %slice.79), channel_id=1, source_target_pairs={{0,1},{1,0},{2,3},{3,2},{4,6},{5,7},{6,4},{7,5},{8,9},{9,8},{10,11... | collective-permute-start | bytes 786440 | tf_op jit(solution)/shard_map/ppermute | solution.py:295
  135.7 14.3 %collective-permute-start.35 = (bf16[32,4096]{1,0:T(8,128)(2,1)S(1)}, bf16[32,4096]{1,0:T(8,128)(2,1)S(1)}, u32[]{:S(2)}, u32[]{:S(2)}) collective-permute-start(bf16[32,4096]{1,0:T(8,128)(2,1)S(1)} %add_convert_fusion.10), channel_id=1, source_target_pairs={{0,24},{1,25},{2,26},{3,27},{4,28},{5,29},{6,30},{7,31},{8,16},{9,... | collective-permute-start | bytes 786440 | tf_op jit(solution)/shard_map/ppermute | solution.py:295
  138.2 18.7 %collective-permute-start.23 = (bf16[32,4096]{1,0:T(8,128)(2,1)S(1)}, bf16[32,4096]{1,0:T(8,128)(2,1)S(1)}, u32[]{:S(2)}, u32[]{:S(2)}) collective-permute-start(bf16[32,4096]{1,0:T(8,128)(2,1)S(1)} %add_convert_fusion.11), channel_id=1, source_target_pairs={{0,16},{1,17},{2,18},{3,19},{4,20},{5,21},{6,22},{7,23},{8,24},{9,... | collective-permute-start | bytes 786440 | tf_op jit(solution)/shard_map/ppermute | solution.py:295
  140.9 15.9 %collective-permute-start.11 = (bf16[32,4096]{1,0:T(8,128)(2,1)S(1)}, bf16[32,4096]{1,0:T(8,128)(2,1)S(1)}, u32[]{:S(2)}, u32[]{:S(2)}) collective-permute-start(bf16[32,4096]{1,0:T(8,128)(2,1)S(1)} %add_convert_fusion.12), channel_id=1, source_target_pairs={{0,8},{1,9},{2,10},{3,11},{4,12},{5,13},{6,14},{7,15},{8,0},{9,1},... | collective-permute-start | bytes 786440 | tf_op jit(solution)/shard_map/ppermute | solution.py:295
  (34 other events, 202.5 us)

commit v2 on v1

--- a/solution.py
+++ b/solution.py
@@ -8,6 +8,7 @@
 from jax.sharding import PartitionSpec as P
 
 LANES = 128
+VMEM_BYTES = 32 << 20
 CONTRACT_LAST = (((1,), (1,)), ((), ()))
 CONTRACT_FIRST = (((0,), (0,)), ((), ()))
 
@@ -114,8 +115,9 @@
     lane = lax.broadcasted_iota(jnp.int32, (rows, LANES), 1)
     expert = lane % experts
     dense = jnp.zeros((rows, LANES), jnp.float32)
-    for k in range(route_ref.shape[1]):
-        dense += jnp.where(route_ref[:, k : k + 1] == expert, weight_ref[:, k : k + 1], 0.0)
+    chosen, share = jnp.transpose(route_ref[...]), jnp.transpose(weight_ref[...])
+    for k in range(chosen.shape[1]):
+        dense += jnp.where(chosen[:, k : k + 1] == expert, share[:, k : k + 1], 0.0)
     high = dense.astype(jnp.bfloat16).astype(jnp.float32)
     middle = (dense - high).astype(jnp.bfloat16).astype(jnp.float32)
     low = dense - high - middle
@@ -129,156 +131,237 @@
     return pl.pallas_call(
         functools.partial(pack_kernel, experts),
         out_shape=jax.ShapeDtypeStruct((rows, 2 * features + LANES), jnp.bfloat16),
-    )(tokens, grad_out, routes, route_weight)
-
-
-def forward_kernel(
-    experts, n_blocks, expert_ref, *refs
-):
-    blocks = refs[:n_blocks]
-    wg_ref, wu_ref, wd_ref = refs[n_blocks : n_blocks + 3]
-    x_ref, g_ref, keep_ref, send_ref, hid_ref, dgu_ref = refs[n_blocks + 3 : n_blocks + 9]
-    wgu, wd, rw, sems, wsems = refs[n_blocks + 9 :]
+    )(tokens, grad_out, routes.T, route_weight.T)
+
+
+def place_copies(pieces, columns, held, sems):
+    copies, row = [], 0
+    for i, piece in enumerate(pieces):
+        place = pl.ds(row, piece.shape[0])
+        copies.append(pltpu.make_async_copy(piece.at[:, columns], held.at[place], sems.at[i]))
+        row += piece.shape[0]
+    return copies
+
+
+def forward_kernel(experts, n_pieces, expert_ref, *refs):
+    pieces = refs[:n_pieces]
+    wg_ref, wu_ref, wd_ref = refs[n_pieces : n_pieces + 3]
+    keep_ref, send_ref, hid_ref, dgu_ref = refs[n_pieces + 3 : n_pieces + 7]
+    x, g, rw, wgu, wd, hid, dgu, out, back = refs[n_pieces + 7 : n_pieces + 16]
+    x_sems, g_sems, r_sems, w_sems, o_sems = refs[n_pieces + 16 :]
     features, half = wg_ref.shape
-    rows = blocks[0].shape[0]
-    w_copies = [
-        pltpu.make_async_copy(wg_ref, wgu.at[:, :half], wsems.at[0]),
-        pltpu.make_async_copy(wu_ref, wgu.at[:, half:], wsems.at[1]),
-        pltpu.make_async_copy(wd_ref, wd, wsems.at[2]),
-    ]
-    x_copies, g_copies, r_copies = [], [], []
-    for i, block in enumerate(blocks):
-        place = pl.ds(i * rows, rows)
-        x_copies.append(
-            pltpu.make_async_copy(block.at[:, :features], x_ref.at[place], sems.at[0, i])
+    own = keep_ref.shape[0]
+    cut = features // 2
+    w_copies, d_copies = [], []
+    for i in range(2):
+        rows = pl.ds(i * cut, cut)
+        w_copies += [
+            pltpu.make_async_copy(wg_ref.at[rows], wgu.at[rows, :half], w_sems.at[2 * i]),
+            pltpu.make_async_copy(wu_ref.at[rows], wgu.at[rows, half:], w_sems.at[2 * i + 1]),
+        ]
+        d_copies.append(
+            pltpu.make_async_copy(wd_ref.at[:, rows], wd.at[:, rows], w_sems.at[4 + i])
         )
-        g_copies.append(
-            pltpu.make_async_copy(
-                block.at[:, features : 2 * features], g_ref.at[place], sems.at[1, i]
-            )
-        )
-        r_copies.append(
-            pltpu.make_async_copy(block.at[:, 2 * features :], rw.at[place], sems.at[2, i])
-        )
-    for copy in w_copies[:2] + x_copies + r_copies + w_copies[2:] + g_copies:
+    x_copies = place_copies(pieces, pl.ds(0, features), x, x_sems)
+    g_copies = place_copies(pieces, pl.ds(features, features), g, g_sems)
+    r_copies = place_copies(pieces, pl.ds(2 * features, LANES), rw, r_sems)
+    for copy in d_copies + g_copies + r_copies + w_copies + x_copies:
         copy.start()
-    for copy in w_copies[:2] + x_copies + r_copies:
-        copy.wait()
-    gate_up = jnp.dot(x_ref[...], wgu[...], preferred_element_type=jnp.float32)
-    for copy in w_copies[2:] + g_copies:
+    for copy in d_copies + g_copies + r_copies:
         copy.wait()
     lane = lax.broadcasted_iota(jnp.int32, rw.shape, 1)
     chosen = (lane % experts == expert_ref[0]) & (lane < 3 * experts)
     weight = jnp.sum(jnp.where(chosen, rw[...].astype(jnp.float32), 0.0), axis=1, keepdims=True)
     d_hidden = (
-        lax.dot_general(g_ref[...], wd[...], CONTRACT_LAST, preferred_element_type=jnp.float32)
+        lax.dot_general(g[...], wd[...], CONTRACT_LAST, preferred_element_type=jnp.float32)
         * weight
     )
+    for copy in w_copies + x_copies:
+        copy.wait()
+    gate_up = jnp.dot(x[...], wgu[...], preferred_element_type=jnp.float32)
     gate, up_val = gate_up[:, :half], gate_up[:, half:]
     sig_gate = jax.nn.sigmoid(gate)
     activated = gate * sig_gate
-    hid_ref[...] = (weight * (activated * up_val)).astype(jnp.bfloat16)
-    dgu_ref[:, :half] = (
-        d_hidden * up_val * sig_gate * (1.0 + gate * (1.0 - sig_gate))
-    ).astype(jnp.bfloat16)
-    dgu_ref[:, half:] = (d_hidden * activated).astype(jnp.bfloat16)
-    out = jnp.dot(hid_ref[...], wd[...], preferred_element_type=jnp.float32).astype(jnp.bfloat16)
-    own = keep_ref.shape[0]
-    keep_ref[:, :features] = out[:own]
-    send_ref[:, :features] = out[own:]
-    back = lax.dot_general(
-        dgu_ref[...], wgu[...], CONTRACT_LAST, preferred_element_type=jnp.float32
-    ).astype(jnp.bfloat16)
-    keep_ref[:, features:] = back[:own]
-    send_ref[:, features:] = back[own:]
-
-
-def forward(expert, blocks, weight_g, weight_u, weight_d, experts):
-    rows = blocks[0].shape[0] * len(blocks)
+    hid[...] = (weight * (activated * up_val)).astype(jnp.bfloat16)
+    dgu[:, :half] = (d_hidden * up_val * sig_gate * (1.0 + gate * (1.0 - sig_gate))).astype(
+        jnp.bfloat16
+    )
+    dgu[:, half:] = (d_hidden * activated).astype(jnp.bfloat16)
+    sends = [
+        pltpu.make_async_copy(hid, hid_ref, o_sems.at[0]),
+        pltpu.make_async_copy(dgu, dgu_ref, o_sems.at[1]),
+    ]
+
+    def leave(part, column):
+        sends.append(
+            pltpu.make_async_copy(
+                part.at[own:], send_ref.at[:, column], o_sems.at[len(sends)]
+            )
+        )
+        sends.append(
+            pltpu.make_async_copy(
+                part.at[:own], keep_ref.at[:, column], o_sems.at[len(sends)]
+            )
+        )
+        sends[-2].start()
+        sends[-1].start()
+
+    sends[0].start()
+    sends[1].start()
+    out[...] = jnp.dot(hid[...], wd[...], preferred_element_type=jnp.float32).astype(jnp.bfloat16)
+    leave(out, pl.ds(0, features))
+    for i in range(2):
+        columns = pl.ds(i * cut, cut)
+        back[i] = lax.dot_general(
+            dgu[...], wgu[columns], CONTRACT_LAST, preferred_element_type=jnp.float32
+        ).astype(jnp.bfloat16)
+        leave(back.at[i], pl.ds(features + i * cut, cut))
+    for copy in sends:
+        copy.wait()
+
+
+def forward(expert, pieces, weight_g, weight_u, weight_d, experts):
+    rows = sum(piece.shape[0] for piece in pieces)
     features, half = weight_g.shape
     bf16 = jnp.bfloat16
     out_shape = (
-        jax.ShapeDtypeStruct((rows, features), bf16),
-        jax.ShapeDtypeStruct((rows, features), bf16),
         jax.ShapeDtypeStruct((rows // 2, 2 * features), bf16),
         jax.ShapeDtypeStruct((rows // 2, 2 * features), bf16),
         jax.ShapeDtypeStruct((rows, half), bf16),
         jax.ShapeDtypeStruct((rows, 2 * half), bf16),
     )
     return pl.pallas_call(
-        functools.partial(forward_kernel, experts, len(blocks)),
+        functools.partial(forward_kernel, experts, len(pieces)),
         out_shape=out_shape,
         in_specs=[pl.BlockSpec(memory_space=pltpu.SMEM)]
-        + [pl.BlockSpec(memory_space=pl.ANY)] * (len(blocks) + 3),
-        out_specs=tuple(pl.BlockSpec(memory_space=pltpu.VMEM) for _ in out_shape),
+        + [pl.BlockSpec(memory_space=pl.ANY)] * (len(pieces) + 3),
+        out_specs=tuple(pl.BlockSpec(memory_space=pl.ANY) for _ in out_shape),
         scratch_shapes=[
+            pltpu.VMEM((rows, features), bf16),
+            pltpu.VMEM((rows, features), bf16),
+            pltpu.VMEM((rows, LANES), bf16),
             pltpu.VMEM((features, 2 * half), bf16),
             pltpu.VMEM((half, features), bf16),
-            pltpu.VMEM((rows, LANES), bf16),
-            pltpu.SemaphoreType.DMA((3, len(blocks))),
-            pltpu.SemaphoreType.DMA((3,)),
+            pltpu.VMEM((rows, half), bf16),
+            pltpu.VMEM((rows, 2 * half), bf16),
+            pltpu.VMEM((rows, features), bf16),
+            pltpu.VMEM((2, rows, features // 2), bf16),
+            pltpu.SemaphoreType.DMA((len(pieces),)),
+            pltpu.SemaphoreType.DMA((len(pieces),)),
+            pltpu.SemaphoreType.DMA((len(pieces),)),
+            pltpu.SemaphoreType.DMA((6,)),
+            pltpu.SemaphoreType.DMA((8,)),
         ],
-        compiler_params=pltpu.CompilerParams(vmem_limit_bytes=40 << 20),
+        compiler_params=pltpu.CompilerParams(vmem_limit_bytes=VMEM_BYTES),
         cost_estimate=pl.CostEstimate(
-            flops=12 * rows * features * half,
-            bytes_accessed=6 * features * half + 16 * rows * features,
+            flops=12 * 20 * rows * features * half,
+            bytes_accessed=6 * features * half + 8 * rows * features,
             transcendentals=rows * half,
         ),
-    )(expert, *blocks, weight_g, weight_u, weight_d)
-
-
-def grads_kernel(n_slots, *refs):
-    xs, gs, hids, dgus = (refs[i * n_slots : (i + 1) * n_slots] for i in range(4))
-    gg_ref, gu_ref, gd_ref = refs[4 * n_slots :]
-    half = gg_ref.shape[1]
-
-    def product(lefts, rights):
-        return sum(
-            lax.dot_general(
-                left[...], right[...], CONTRACT_FIRST, preferred_element_type=jnp.float32
-            )
-            for left, right in zip(lefts, rights)
+    )(expert, *pieces, weight_g, weight_u, weight_d)
+
+
+def grads_kernel(n_pieces, n_slots, tile, *refs):
+    pieces, refs = refs[:n_pieces], refs[n_pieces:]
+    hids, dgus, refs = refs[:n_slots], refs[n_slots : 2 * n_slots], refs[2 * n_slots :]
+    gg_ref, gu_ref, gd_ref, x, g, hid, dgu, gg, gu, gd, x_sems, g_sems, a_sems, o_sems = refs
+    features, half = gg_ref.shape
+    every = pl.ds(0, half)
+    first = place_copies(dgus, pl.ds(0, 2 * half), dgu, a_sems.at[0])
+    first += place_copies(pieces, pl.ds(0, features), x, x_sems)
+    then = place_copies(hids, every, hid, a_sems.at[1])
+    then += place_copies(pieces, pl.ds(features, features), g, g_sems)
+    for copy in first + then:
+        copy.start()
+    for copy in first:
+        copy.wait()
+    sends = []
+
+    def leave(held, place, ref):
+        sends.append(
+            pltpu.make_async_copy(held.at[place], ref.at[place], o_sems.at[len(sends)])
+        )
+        sends[-1].start()
+
+    for i in range(features // tile):
+        rows = pl.ds(i * tile, tile)
+        grad_gu = lax.dot_general(
+            x[:, rows], dgu[...], CONTRACT_FIRST, preferred_element_type=jnp.float32
         ).astype(jnp.bfloat16)
-
-    grad_gu = product(xs, dgus)
-    gg_ref[...] = grad_gu[:, :half]
-    gu_ref[...] = grad_gu[:, half:]
-    gd_ref[...] = product(hids, gs)
-
-
-def weight_grads(xs, gs, hids, dgus):
-    features, half, rows = xs[0].shape[1], hids[0].shape[1], xs[0].shape[0]
-    tile = 256
+        gg[rows] = grad_gu[:, :half]
+        gu[rows] = grad_gu[:, half:]
+        leave(gg, rows, gg_ref)
+        leave(gu, rows, gu_ref)
+    for copy in then:
+        copy.wait()
+    for i in range(half // LANES):
+        rows = pl.ds(i * LANES, LANES)
+        gd[rows] = lax.dot_general(
+            hid[:, rows], g[...], CONTRACT_FIRST, preferred_element_type=jnp.float32
+        ).astype(jnp.bfloat16)
+        leave(gd, rows, gd_ref)
+    for copy in sends:
+        copy.wait()
+
+
+def weight_grads(pieces, hids, dgus):
+    features, half = pieces[0].shape[1] // 2 // LANES * LANES, hids[0].shape[1]
+    rows = sum(piece.shape[0] for piece in pieces)
+    tile = min(256, features)
     bf16 = jnp.bfloat16
-    n_slots = len(xs)
-    wide = pl.BlockSpec((rows, tile), lambda f: (0, f))
+    out_shape = (
+        jax.ShapeDtypeStruct((features, half), bf16),
+        jax.ShapeDtypeStruct((features, half), bf16),
+        jax.ShapeDtypeStruct((half, features), bf16),
+    )
     return pl.pallas_call(
-        functools.partial(grads_kernel, n_slots),
-        grid=(features // tile,),
-        out_shape=(
-            jax.ShapeDtypeStruct((features, half), bf16),
-            jax.ShapeDtypeStruct((features, half), bf16),
-            jax.ShapeDtypeStruct((half, features), bf16),
-        ),
-        in_specs=[wide] * (2 * n_slots)
-        + [pl.BlockSpec((rows, half), lambda f: (0, 0))] * n_slots
-        + [pl.BlockSpec((rows, 2 * half), lambda f: (0, 0))] * n_slots,
-        out_specs=(
-            pl.BlockSpec((tile, half), lambda f: (f, 0)),
-            pl.BlockSpec((tile, half), lambda f: (f, 0)),
-            pl.BlockSpec((half, tile), lambda f: (0, f)),
-        ),
-        compiler_params=pltpu.CompilerParams(vmem_limit_bytes=40 << 20),
+        functools.partial(grads_kernel, len(pieces), len(hids), tile),
+        out_shape=out_shape,
+        in_specs=[pl.BlockSpec(memory_space=pl.ANY)] * (len(pieces) + 2 * len(hids)),
+        out_specs=tuple(pl.BlockSpec(memory_space=pl.ANY) for _ in out_shape),
+        scratch_shapes=[
+            pltpu.VMEM((rows, features), bf16),
+            pltpu.VMEM((rows, features), bf16),
+            pltpu.VMEM((rows, half), bf16),
+            pltpu.VMEM((rows, 2 * half), bf16),
+            pltpu.VMEM((features, half), bf16),
+            pltpu.VMEM((features, half), bf16),
+            pltpu.VMEM((half, features), bf16),
+            pltpu.SemaphoreType.DMA((len(pieces),)),
+            pltpu.SemaphoreType.DMA((len(pieces),)),
+            pltpu.SemaphoreType.DMA((2, len(hids))),
+            pltpu.SemaphoreType.DMA((2 * (features // tile) + half // LANES,)),
+        ],
+        compiler_params=pltpu.CompilerParams(vmem_limit_bytes=VMEM_BYTES),
         cost_estimate=pl.CostEstimate(
-            flops=6 * n_slots * rows * features * half,
-            bytes_accessed=6 * features * half + 4 * n_slots * rows * features,
+            flops=6 * 20 * rows * features * half,
+            bytes_accessed=6 * features * half + 4 * rows * features,
             transcendentals=0,
         ),
-    )(*xs, *gs, *hids, *dgus)
+    )(*pieces, *hids, *dgus)
 
 
 def add(left, right):
     return (left.astype(jnp.float32) + right.astype(jnp.float32)).astype(jnp.bfloat16)
+
+
+def after(value, *earlier):
+    return lax.optimization_barrier((value,) + earlier)[0]
+
+
+def tick_kernel(in_ref, out_ref):
+    pass
+
+
+def tick(token):
+    return pl.pallas_call(
+        tick_kernel,
+        out_shape=jax.ShapeDtypeStruct(token.shape, token.dtype),
+        in_specs=[pl.BlockSpec(memory_space=pl.ANY)],
+        out_specs=pl.BlockSpec(memory_space=pl.ANY),
+        input_output_aliases={0: 0},
+        cost_estimate=pl.CostEstimate(flops=50_000_000_000, bytes_accessed=0, transcendentals=0),
+    )(token)
 
 
 def dense_shards(tokens, grad_out, routes, route_weight, w_gate, w_up, w_down):
@@ -298,30 +381,108 @@
     second = lambda core: 2 - core
     sibling = lambda core: n_local
 
+    def along(z):
+        return lambda core: z * 2 * n_local
+
+    rows = tokens.shape[0]
+    weights = (w_gate[0], w_up[0], w_down[0])
     block = pack(tokens, grad_out, routes, route_weight, experts)
-    slots = [block] + [
-        exchange(block, lambda core, z=z: z * 2 * n_local) for z in range(1, n_z)
-    ]
-    weights = (w_gate[0], w_up[0], w_down[0])
-    results = []
-    for own in slots:
-        one = exchange(own, first)
-        two = exchange(own, second)
-        both = exchange(one, second)
-        plane = [own, one, two, both]
-        others = [exchange(part, sibling) for part in plane]
-        results.append(forward(expert, plane + others, *weights, experts))
-    rows = tokens.shape[0]
-    arrived = []
-    for z in list(range(1, n_z)) + [0]:
-        _, _, keep, send, _, _ = results[z]
-        total = add(keep, exchange(send, sibling))
-        total = add(total[: 2 * rows], exchange(total[2 * rows :], second))
-        total = add(total[:rows], exchange(total[rows:], first))
-        arrived.append(exchange(total, lambda core: z * 2 * n_local) if z else total)
+    now = [jnp.zeros((8, LANES), jnp.float32)]
+
+    def start(value, step):
+        return exchange(after(value, now[0]), step)
+
+    def wait(value):
+        value, now[0] = lax.optimization_barrier((value, now[0]))
+        return value
+
+    def turn():
+        now[0] = tick(now[0])
+
+    pairs, twos, taken, results, sums = {}, {}, {}, {}, {}
+
+    def spread(z, one, own):
+        pairs[z] = wait(jnp.concatenate([own, wait(one)]))
+        return start(pairs[z], second), start(pairs[z], sibling)
+
+    def across(z, two):
+        twos[z] = wait(two)
+        return start(twos[z], sibling)
+
+    def compute(z, pair_there, two_there):
+        taken[z] = [pairs[z], twos[z], pair_there, two_there]
+        results[z] = forward(expert, [after(t, now[0]) for t in taken[z]], *weights, experts)
+        results[z] = [wait(t) for t in results[z]]
+        return start(results[z][1], sibling)
+
+    def fold(z, there):
+        sums[z] = wait(add(results[z][0], wait(there)))
+        return start(sums[z][2 * rows :], second)
+
+    def fold_second(z, there):
+        sums[z] = wait(add(sums[z][: 2 * rows], wait(there)))
+        return start(sums[z][rows:], first)
+
+    def fold_first(z, there):
+        sums[z] = wait(add(sums[z][:rows], wait(there)))
+        return start(sums[z], along(z)) if z else sums[z]
+
+    one0 = start(block, first)
+    far1 = start(block, along(1))
+    far2 = start(block, along(2))
+    turn()
+    two0, pt0 = spread(0, one0, block)
+    turn()
+    far1 = wait(far1)
+    one1 = start(far1, first)
+    turn()
+    tt0 = across(0, two0)
+    far2 = wait(far2)
+    one2 = start(far2, first)
+    far3 = start(block, along(3))
+    turn()
+    two1, pt1 = spread(1, one1, far1)
+    turn()
+    back0 = compute(0, pt0, tt0)
+    two2, pt2 = spread(2, one2, far2)
+    tt1 = across(1, two1)
+    turn()
+    back1 = compute(1, pt1, tt1)
+    far3 = wait(far3)
+    one3 = start(far3, first)
+    tt2 = across(2, two2)
+    back0 = fold(0, back0)
+    turn()
+    two3, pt3 = spread(3, one3, far3)
+    back2 = compute(2, pt2, tt2)
+    back1 = fold(1, back1)
+    turn()
+    tt3 = across(3, two3)
+    turn()
+    back2 = fold(2, back2)
+    back0 = fold_second(0, back0)
+    turn()
+    back3 = compute(3, pt3, tt3)
+    back1 = fold_second(1, back1)
+    turn()
+    back3 = fold(3, back3)
+    back2 = fold_second(2, back2)
+    turn()
+    back1 = fold_first(1, back1)
+    back2 = fold_first(2, back2)
+    back3 = fold_second(3, back3)
+    turn()
+    back3 = fold_first(3, back3)
+    back0 = fold_first(0, back0)
+    order = [0, 1, 2, 3]
+    grad_wg, grad_wu, grad_wd = weight_grads(
+        [after(piece, now[0]) for z in order for piece in taken[z]],
+        [results[z][2] for z in order],
+        [results[z][3] for z in order],
+    )
+    grad_wg = wait(grad_wg)
+    arrived = (back0, wait(back2), wait(back1), wait(back3))
     final = sum(part.astype(jnp.float32) for part in arrived).astype(jnp.bfloat16)
-    xs, gs, _, _, hids, dgus = (list(column) for column in zip(*results))
-    grad_wg, grad_wu, grad_wd = weight_grads(xs, gs, hids, dgus)
     return (
         final[:, :features],
         final[:, features:],

time: 158 us -> 127 us (0.80)
  waiting for transfers between devices: 70.5 us -> 49 us
  local copies, waits for them, and re-layouts: 14.4 us -> 4 us
  Pallas kernels: 32.3 us -> 34.3 us
    ppermute x46 -> x34, waiting for transfers between devices: 70.5 us -> 49 us  [exchange(): return lax.ppermute(value, axes, pairs)]
    unnamed x42 -> x28, local copies, waits for them, and re-layouts: 13.5 us -> 3.07 us
    convert_element_type x11 -> x12, other arithmetic: 4.11 us -> 1.76 us  [add(): (left.astype(jnp.float32) + right.astype(jnp.float32)).astype(jnp.bfloat16)]
    pallas_call x5, Pallas kernels: 30.5 us -> 32.3 us  [the longest x4 23 us: forward(): pl.pallas_call(functools.partial(forward_kernel, experts, len(pieces)), o...]
    ppermute x46 -> x34, starting transfers between devices: 35.2 us -> 35.1 us  [exchange(): return lax.ppermute(value, axes, pairs)]
  transfers between devices with their start and end apart: 46 -> 34, of which waited for: 16 -> 12; matrix products, arithmetic and copies ran while one was open for 3% -> 2% of each run, Pallas kernels for 19% -> 26%
where the time goes in v2:
time: 127 us; the launch traced here: 126 us
  waiting for transfers between devices  49 us (39%)
  starting transfers between devices  35.1 us (28%)
  Pallas kernels  34.3 us (27%)
  local copies, waits for them, and re-layouts  4 us (3%)
  other arithmetic  3.03 us (2%)
    ppermute x34, waiting for transfers between devices, exchange(): return lax.ppermute(value, axes, pairs)  49 us
    ppermute x34, starting transfers between devices, exchange(): return lax.ppermute(value, axes, pairs)  35.1 us
    pallas_call x4, Pallas kernels, forward(): pl.pallas_call(functools.partial(forward_kernel, experts, len(pieces)), o...  23 us
    pallas_call x1, Pallas kernels, weight_grads(): pl.pallas_call(functools.partial(grads_kernel, len(pieces), len(hids), ti...  9.29 us
    unnamed x28, local copies, waits for them, and re-layouts  3.07 us
  transfers between devices with their start and end apart: 34, of which 12 were waited for; matrix products, arithmetic and copies ran while one was open for 2% of the time, Pallas kernels for 26%

profile of v2, /device:TPU:0, one launch (start us, length us, event | category | flops | bytes accessed | tf_op | source)
XLA Modules:
  0.0 126.5 jit_solution(13065313716536279966)
XLA Ops:
  0.6 2.0 %shard_map.110 = bf16[32,4224]{1,0:T(8,128)(2,1)} custom-call(bf16[32,2048]{1,0:T(8,128)(2,1)} %tok_ref.1, bf16[32,2048]{1,0:T(8,128)(2,1)} %grad_ref.1, s32[8,32]{1,0:T(8,128)} %bitcast.21, f32[8,32]{1,0:T(8,128)} %bitcast.22), custom_call_target="tpu_custom_call" | custom-call | tf_op jit(solution)/shard_map/pallas_call | solution.py:131
  2.7 2.9 %collective-permute-start = (bf16[32,4224]{1,0:T(8,128)(2,1)}, bf16[32,4224]{1,0:T(8,128)(2,1)S(1)}, u32[]{:S(2)}, u32[]{:S(2)}) collective-permute-start(bf16[32,4224]{1,0:T(8,128)(2,1)} %shard_map.110), channel_id=1, source_target_pairs={{0,1},{1,0},{2,3},{3,2},{4,6},{5,7},{6,4},{7,5},{8,9},{9,8},{10,11... | collective-permute-start | bytes 811016 | tf_op jit(solution)/shard_map/ppermute | solution.py:378
  5.6 2.6 %collective-permute-start.3 = (bf16[32,4224]{1,0:T(8,128)(2,1)}, bf16[32,4224]{1,0:T(8,128)(2,1)S(1)}, u32[]{:S(2)}, u32[]{:S(2)}) collective-permute-start(bf16[32,4224]{1,0:T(8,128)(2,1)} %shard_map.110), channel_id=1, source_target_pairs={{0,16},{1,17},{2,18},{3,19},{4,20},{5,21},{6,22},{7,23},{8,24},{9,... | collective-permute-start | bytes 811016 | tf_op jit(solution)/shard_map/ppermute | solution.py:378
  8.2 1.6 %collective-permute-start.1 = (bf16[32,4224]{1,0:T(8,128)(2,1)}, bf16[32,4224]{1,0:T(8,128)(2,1)S(1)}, u32[]{:S(2)}, u32[]{:S(2)}) collective-permute-start(bf16[32,4224]{1,0:T(8,128)(2,1)} %shard_map.110), channel_id=1, source_target_pairs={{0,8},{1,9},{2,10},{3,11},{4,12},{5,13},{6,14},{7,15},{8,0},{9,1},... | collective-permute-start | bytes 811016 | tf_op jit(solution)/shard_map/ppermute | solution.py:378
  11.4 2.0 %collective-permute-start.4 = (bf16[64,4224]{1,0:T(8,128)(2,1)S(1)}, bf16[64,4224]{1,0:T(8,128)(2,1)S(1)}, u32[]{:S(2)}, u32[]{:S(2)}) collective-permute-start(bf16[64,4224]{1,0:T(8,128)(2,1)S(1)} %pad_maximum_fusion.refs_0_), channel_id=1, source_target_pairs={{0,2},{1,3},{2,0},{3,1},{4,5},{5,4},{6,7},{7,6},{8,10},{9,11},{10,... | collective-permute-start | bytes 1622024 | tf_op jit(solution)/shard_map/ppermute | solution.py:378
  13.4 7.4 %collective-permute-done.1 = bf16[32,4224]{1,0:T(8,128)(2,1)S(1)} collective-permute-done((bf16[32,4224]{1,0:T(8,128)(2,1)}, bf16[32,4224]{1,0:T(8,128)(2,1)S(1)}, u32[]{:S(2)}, u32[]{:S(2)}) %collective-permute-start.1) | collective-permute-done | bytes 270368 | tf_op jit(solution)/shard_map/ppermute | solution.py:378
  20.8 1.5 %collective-permute-start.2 = (bf16[32,4224]{1,0:T(8,128)(2,1)S(1)}, bf16[32,4224]{1,0:T(8,128)(2,1)S(1)}, u32[]{:S(2)}, u32[]{:S(2)}) collective-permute-start(bf16[32,4224]{1,0:T(8,128)(2,1)S(1)} %collective-permute-done.1), channel_id=1, source_target_pairs={{0,1},{1,0},{2,3},{3,2},{4,6},{5,7},{6,4},{7,5},{8,9},{9,8},{10,11... | collective-permute-start | bytes 811016 | tf_op jit(solution)/shard_map/ppermute | solution.py:378
  22.3 5.0 %collective-permute-done.2 = bf16[32,4224]{1,0:T(8,128)(2,1)S(1)} collective-permute-done((bf16[32,4224]{1,0:T(8,128)(2,1)S(1)}, bf16[32,4224]{1,0:T(8,128)(2,1)S(1)}, u32[]{:S(2)}, u32[]{:S(2)}) %collective-permute-start.2) | collective-permute-done | bytes 270368 | tf_op jit(solution)/shard_map/ppermute | solution.py:378
  27.9 1.2 collective-permute-start.12
  29.6 1.1 collective-permute-start.10
  30.8 1.6 %copy-done.3 = bf16[1,2048,384]{2,1,0:T(8,128)(2,1)S(1)} copy-done((bf16[1,2048,384]{2,1,0:T(8,128)(2,1)S(1)}, bf16[1,2048,384]{2,1,0:T(8,128)(2,1)}, u32[]{:S(2)}) %copy-start.3) | copy-done | bytes 1572888
  32.4 1.4 %copy-done.5 = bf16[1,384,2048]{2,1,0:T(8,128)(2,1)S(1)} copy-done((bf16[1,384,2048]{2,1,0:T(8,128)(2,1)S(1)}, bf16[1,384,2048]{2,1,0:T(8,128)(2,1)}, u32[]{:S(2)}) %copy-start.5) | copy-done | bytes 1572888
  33.8 5.7 %shard_map.111 = (bf16[128,4096]{1,0:T(8,128)(2,1)S(1)}, bf16[128,4096]{1,0:T(8,128)(2,1)S(1)}, bf16[256,384]{1,0:T(8,128)(2,1)S(1)}, bf16[256,768]{1,0:T(8,128)(2,1)S(1)}) custom-call(s32[1]{0:T(128)} %bitcast.expert_ref, bf16[64,4224]{1,0:T(8,128)(2,1)S(1)} %pad_maximum_fusion.refs_0_, bf16[64,4224]{1,0:T(8,128)(2,1)S(1)} %collective-permute-done.4.refs_1_, ...), custom_call_target="tpu_custom_call" | custom-call | flops 48318382080 | bytes 8912896 | tf_op jit(solution)/shard_map/pallas_call | solution.py:233
  41.6 5.7 %shard_map.112 = (bf16[128,4096]{1,0:T(8,128)(2,1)S(1)}, bf16[128,4096]{1,0:T(8,128)(2,1)S(1)}, bf16[256,384]{1,0:T(8,128)(2,1)S(1)}, bf16[256,768]{1,0:T(8,128)(2,1)S(1)}) custom-call(s32[1]{0:T(128)} %bitcast.expert_ref, bf16[64,4224]{1,0:T(8,128)(2,1)S(1)} %pad_maximum_fusion.1.refs_0_.refs_4_, ...), custom_call_target="tpu_custom_call" | custom-call | flops 48318382080 | bytes 8912896 | tf_op jit(solution)/shard_map/pallas_call | solution.py:233
  47.4 1.7 %collective-permute-done.9.refs_1_.refs_9_ = bf16[64,4224]{1,0:T(8,128)(2,1)S(1)} collective-permute-done((bf16[64,4224]{1,0:T(8,128)(2,1)S(1)}, bf16[64,4224]{1,0:T(8,128)(2,1)S(1)}, u32[]{:S(2)}, u32[]{:S(2)}) %collective-permute-start.9) | collective-permute-done | bytes 540704 | tf_op jit(solution)/shard_map/ppermute | solution.py:378
  49.1 1.5 %collective-permute-start.15 = (bf16[32,4224]{1,0:T(8,128)(2,1)S(1)}, bf16[32,4224]{1,0:T(8,128)(2,1)S(1)}, u32[]{:S(2)}, u32[]{:S(2)}) collective-permute-start(bf16[32,4224]{1,0:T(8,128)(2,1)S(1)} %collective-permute-done.10), channel_id=1, source_target_pairs={{0,1},{1,0},{2,3},{3,2},{4,6},{5,7},{6,4},{7,5},{8,9},{9,8},{10,11... | collective-permute-start | bytes 811016 | tf_op jit(solution)/shard_map/ppermute | solution.py:378
  50.9 4.7 %collective-permute-done.15 = bf16[32,4224]{1,0:T(8,128)(2,1)S(1)} collective-permute-done((bf16[32,4224]{1,0:T(8,128)(2,1)S(1)}, bf16[32,4224]{1,0:T(8,128)(2,1)S(1)}, u32[]{:S(2)}, u32[]{:S(2)}) %collective-permute-start.15) | collective-permute-done | bytes 270368 | tf_op jit(solution)/shard_map/ppermute | solution.py:378
  56.6 1.1 collective-permute-start.14
  57.7 5.9 %shard_map.113 = (bf16[128,4096]{1,0:T(8,128)(2,1)S(1)}, bf16[128,4096]{1,0:T(8,128)(2,1)S(1)}, bf16[256,384]{1,0:T(8,128)(2,1)S(1)}, bf16[256,768]{1,0:T(8,128)(2,1)S(1)}) custom-call(s32[1]{0:T(128)} %bitcast.expert_ref, bf16[64,4224]{1,0:T(8,128)(2,1)S(1)} %pad_maximum_fusion.2.refs_0_.refs_8_, ...), custom_call_target="tpu_custom_call" | custom-call | flops 48318382080 | bytes 8912896 | tf_op jit(solution)/shard_map/pallas_call | solution.py:233
  64.2 1.6 %collective-permute-start.25 = (bf16[64,4096]{1,0:T(8,128)(2,1)S(1)}, bf16[64,4096]{1,0:T(8,128)(2,1)S(1)}, u32[]{:S(2)}, u32[]{:S(2)}) collective-permute-start(bf16[64,4096]{1,0:T(8,128)(2,1)S(1)} %slice.59), channel_id=1, source_target_pairs={{0,2},{1,3},{2,0},{3,1},{4,5},{5,4},{6,7},{7,6},{8,10},{9,11},{10,... | collective-permute-start | bytes 1572872 | tf_op jit(solution)/shard_map/ppermute | solution.py:378
  66.6 4.1 %collective-permute-done.14 = bf16[64,4096]{1,0:T(8,128)(2,1)S(1)} collective-permute-done((bf16[64,4096]{1,0:T(8,128)(2,1)S(1)}, bf16[64,4096]{1,0:T(8,128)(2,1)S(1)}, u32[]{:S(2)}, u32[]{:S(2)}) %collective-permute-start.14) | collective-permute-done | bytes 524320 | tf_op jit(solution)/shard_map/ppermute | solution.py:378
  70.8 5.7 %shard_map.114 = (bf16[128,4096]{1,0:T(8,128)(2,1)S(1)}, bf16[128,4096]{1,0:T(8,128)(2,1)S(1)}, bf16[256,384]{1,0:T(8,128)(2,1)S(1)}, bf16[256,768]{1,0:T(8,128)(2,1)S(1)}) custom-call(s32[1]{0:T(128)} %bitcast.expert_ref, bf16[64,4224]{1,0:T(8,128)(2,1)S(1)} %pad_maximum_fusion.3.refs_0_.refs_12_, ...), custom_call_target="tpu_custom_call" | custom-call | flops 48318382080 | bytes 8912896 | tf_op jit(solution)/shard_map/pallas_call | solution.py:233
  80.2 1.2 collective-permute-start.26
  81.4 9.6 %collective-permute-done.27 = bf16[64,4096]{1,0:T(8,128)(2,1)S(1)} collective-permute-done((bf16[64,4096]{1,0:T(8,128)(2,1)S(1)}, bf16[64,4096]{1,0:T(8,128)(2,1)S(1)}, u32[]{:S(2)}, u32[]{:S(2)}) %collective-permute-start.27) | collective-permute-done | bytes 524320 | tf_op jit(solution)/shard_map/ppermute | solution.py:378
  91.2 2.0 %collective-permute-start.28 = (bf16[32,4096]{1,0:T(8,128)(2,1)S(1)}, bf16[32,4096]{1,0:T(8,128)(2,1)S(1)}, u32[]{:S(2)}, u32[]{:S(2)}) collective-permute-start(bf16[32,4096]{1,0:T(8,128)(2,1)S(1)} %slice.65), channel_id=1, source_target_pairs={{0,1},{1,0},{2,3},{3,2},{4,6},{5,7},{6,4},{7,5},{8,9},{9,8},{10,11... | collective-permute-start | bytes 786440 | tf_op jit(solution)/shard_map/ppermute | solution.py:378
  93.3 1.5 %collective-permute-start.32 = (bf16[32,4096]{1,0:T(8,128)(2,1)S(1)}, bf16[32,4096]{1,0:T(8,128)(2,1)S(1)}, u32[]{:S(2)}, u32[]{:S(2)}) collective-permute-start(bf16[32,4096]{1,0:T(8,128)(2,1)S(1)} %add_convert_fusion.12), channel_id=1, source_target_pairs={{0,8},{1,9},{2,10},{3,11},{4,12},{5,13},{6,14},{7,15},{8,0},{9,1},... | collective-permute-start | bytes 786440 | tf_op jit(solution)/shard_map/ppermute | solution.py:378
  94.7 4.9 %collective-permute-done.28 = bf16[32,4096]{1,0:T(8,128)(2,1)S(1)} collective-permute-done((bf16[32,4096]{1,0:T(8,128)(2,1)S(1)}, bf16[32,4096]{1,0:T(8,128)(2,1)S(1)}, u32[]{:S(2)}, u32[]{:S(2)}) %collective-permute-start.28) | collective-permute-done | bytes 262176 | tf_op jit(solution)/shard_map/ppermute | solution.py:378
  99.8 1.8 %collective-permute-start.31 = (bf16[32,4096]{1,0:T(8,128)(2,1)S(1)}, bf16[32,4096]{1,0:T(8,128)(2,1)S(1)}, u32[]{:S(2)}, u32[]{:S(2)}) collective-permute-start(bf16[32,4096]{1,0:T(8,128)(2,1)S(1)} %add_convert_fusion.11), channel_id=1, source_target_pairs={{0,16},{1,17},{2,18},{3,19},{4,20},{5,21},{6,22},{7,23},{8,24},{9,... | collective-permute-start | bytes 786440 | tf_op jit(solution)/shard_map/ppermute | solution.py:378
  101.8 1.6 %collective-permute-start.30 = (bf16[32,4096]{1,0:T(8,128)(2,1)S(1)}, bf16[32,4096]{1,0:T(8,128)(2,1)S(1)}, u32[]{:S(2)}, u32[]{:S(2)}) collective-permute-start(bf16[32,4096]{1,0:T(8,128)(2,1)S(1)} %slice.69), channel_id=1, source_target_pairs={{0,1},{1,0},{2,3},{3,2},{4,6},{5,7},{6,4},{7,5},{8,9},{9,8},{10,11... | collective-permute-start | bytes 786440 | tf_op jit(solution)/shard_map/ppermute | solution.py:378
  103.3 10.1 %collective-permute-done.31 = bf16[32,4096]{1,0:T(8,128)(2,1)S(1)} collective-permute-done((bf16[32,4096]{1,0:T(8,128)(2,1)S(1)}, bf16[32,4096]{1,0:T(8,128)(2,1)S(1)}, u32[]{:S(2)}, u32[]{:S(2)}) %collective-permute-start.31) | collective-permute-done | bytes 262176 | tf_op jit(solution)/shard_map/ppermute | solution.py:378
  113.6 2.7 %collective-permute-start.33 = (bf16[32,4096]{1,0:T(8,128)(2,1)S(1)}, bf16[32,4096]{1,0:T(8,128)(2,1)S(1)}, u32[]{:S(2)}, u32[]{:S(2)}) collective-permute-start(bf16[32,4096]{1,0:T(8,128)(2,1)S(1)} %add_convert_fusion.10), channel_id=1, source_target_pairs={{0,24},{1,25},{2,26},{3,27},{4,28},{5,29},{6,30},{7,31},{8,16},{9,... | collective-permute-start | bytes 786440 | tf_op jit(solution)/shard_map/ppermute | solution.py:378
  116.3 9.3 %shard_map.115 = (bf16[2048,384]{1,0:T(8,128)(2,1)}, bf16[2048,384]{1,0:T(8,128)(2,1)}, bf16[384,2048]{1,0:T(8,128)(2,1)}) custom-call(bf16[64,4224]{1,0:T(8,128)(2,1)S(1)} %copy-done.1, bf16[64,4224]{1,0:T(8,128)(2,1)S(1)} %copy-done.8, bf16[64,4224]{1,0:T(8,128)(2,1)S(1)} %copy-done.10, bf16[64,4224]{1,0:T(8,128)(2,1)S(1)} %copy-done.12, ...), custom_call_target="tpu_custom_call" | custom-call | flops 96636764160 | bytes 13107200 | tf_op jit(solution)/shard_map/pallas_call | solution.py:317
  (96 shorter events, 12.7 us)
Async XLA Ops:
  2.7 7.7 %collective-permute-start = (bf16[32,4224]{1,0:T(8,128)(2,1)}, bf16[32,4224]{1,0:T(8,128)(2,1)S(1)}, u32[]{:S(2)}, u32[]{:S(2)}) collective-permute-start(bf16[32,4224]{1,0:T(8,128)(2,1)} %shard_map.110), channel_id=1, source_target_pairs={{0,1},{1,0},{2,3},{3,2},{4,6},{5,7},{6,4},{7,5},{8,9},{9,8},{10,11... | collective-permute-start | bytes 811016 | tf_op jit(solution)/shard_map/ppermute | solution.py:378
  5.6 16.7 %collective-permute-start.3 = (bf16[32,4224]{1,0:T(8,128)(2,1)}, bf16[32,4224]{1,0:T(8,128)(2,1)S(1)}, u32[]{:S(2)}, u32[]{:S(2)}) collective-permute-start(bf16[32,4224]{1,0:T(8,128)(2,1)} %shard_map.110), channel_id=1, source_target_pairs={{0,16},{1,17},{2,18},{3,19},{4,20},{5,21},{6,22},{7,23},{8,24},{9,... | collective-permute-start | bytes 811016 | tf_op jit(solution)/shard_map/ppermute | solution.py:378
  8.2 12.6 %collective-permute-start.1 = (bf16[32,4224]{1,0:T(8,128)(2,1)}, bf16[32,4224]{1,0:T(8,128)(2,1)S(1)}, u32[]{:S(2)}, u32[]{:S(2)}) collective-permute-start(bf16[32,4224]{1,0:T(8,128)(2,1)} %shard_map.110), channel_id=1, source_target_pairs={{0,8},{1,9},{2,10},{3,11},{4,12},{5,13},{6,14},{7,15},{8,0},{9,1},... | collective-permute-start | bytes 811016 | tf_op jit(solution)/shard_map/ppermute | solution.py:378
  11.4 10.9 %collective-permute-start.4 = (bf16[64,4224]{1,0:T(8,128)(2,1)S(1)}, bf16[64,4224]{1,0:T(8,128)(2,1)S(1)}, u32[]{:S(2)}, u32[]{:S(2)}) collective-permute-start(bf16[64,4224]{1,0:T(8,128)(2,1)S(1)} %pad_maximum_fusion.refs_0_), channel_id=1, source_target_pairs={{0,2},{1,3},{2,0},{3,1},{4,5},{5,4},{6,7},{7,6},{8,10},{9,11},{10,... | collective-permute-start | bytes 1622024 | tf_op jit(solution)/shard_map/ppermute | solution.py:378
  13.4 15.7 %collective-permute-start.5 = (bf16[64,4224]{1,0:T(8,128)(2,1)S(1)}, bf16[64,4224]{1,0:T(8,128)(2,1)S(1)}, u32[]{:S(2)}, u32[]{:S(2)}) collective-permute-start(bf16[64,4224]{1,0:T(8,128)(2,1)S(1)} %pad_maximum_fusion.refs_0_), channel_id=1, source_target_pairs={{0,4},{1,5},{2,6},{3,7},{4,0},{5,1},{6,2},{7,3},{8,12},{9,13},{10,... | collective-permute-start | bytes 1622024 | tf_op jit(solution)/shard_map/ppermute | solution.py:378
  20.8 6.5 %collective-permute-start.2 = (bf16[32,4224]{1,0:T(8,128)(2,1)S(1)}, bf16[32,4224]{1,0:T(8,128)(2,1)S(1)}, u32[]{:S(2)}, u32[]{:S(2)}) collective-permute-start(bf16[32,4224]{1,0:T(8,128)(2,1)S(1)} %collective-permute-done.1), channel_id=1, source_target_pairs={{0,1},{1,0},{2,3},{3,2},{4,6},{5,7},{6,4},{7,5},{8,9},{9,8},{10,11... | collective-permute-start | bytes 811016 | tf_op jit(solution)/shard_map/ppermute | solution.py:378
  27.3 3.5 %collective-permute-start.6 = (bf16[64,4224]{1,0:T(8,128)(2,1)S(1)}, bf16[64,4224]{1,0:T(8,128)(2,1)S(1)}, u32[]{:S(2)}, u32[]{:S(2)}) collective-permute-start(bf16[64,4224]{1,0:T(8,128)(2,1)S(1)} %collective-permute-done.4.refs_1_), channel_id=1, source_target_pairs={{0,4},{1,5},{2,6},{3,7},{4,0},{5,1},{6,2},{7,3},{8,12},{9,13},{10,... | collective-permute-start | bytes 1622024 | tf_op jit(solution)/shard_map/ppermute | solution.py:378
  27.4 12.3 %collective-permute-start.11 = (bf16[64,4224]{1,0:T(8,128)(2,1)S(1)}, bf16[64,4224]{1,0:T(8,128)(2,1)S(1)}, u32[]{:S(2)}, u32[]{:S(2)}) collective-permute-start(bf16[64,4224]{1,0:T(8,128)(2,1)S(1)} %pad_maximum_fusion.1.refs_0_.refs_4_), channel_id=1, source_target_pairs={{0,2},{1,3},{2,0},{3,1},{4,5},{5,4},{6,7},{7,6},{8,10},{9,11},{10,... | collective-permute-start | bytes 1622024 | tf_op jit(solution)/shard_map/ppermute | solution.py:378
  27.9 13.5 %collective-permute-start.12 = (bf16[64,4224]{1,0:T(8,128)(2,1)S(1)}, bf16[64,4224]{1,0:T(8,128)(2,1)S(1)}, u32[]{:S(2)}, u32[]{:S(2)}) collective-permute-start(bf16[64,4224]{1,0:T(8,128)(2,1)S(1)} %pad_maximum_fusion.1.refs_0_.refs_4_), channel_id=1, source_target_pairs={{0,4},{1,5},{2,6},{3,7},{4,0},{5,1},{6,2},{7,3},{8,12},{9,13},{10,... | collective-permute-start | bytes 1622024 | tf_op jit(solution)/shard_map/ppermute | solution.py:378
  29.1 10.4 %collective-permute-start.8 = (bf16[32,4224]{1,0:T(8,128)(2,1)S(1)}, bf16[32,4224]{1,0:T(8,128)(2,1)S(1)}, u32[]{:S(2)}, u32[]{:S(2)}) collective-permute-start(bf16[32,4224]{1,0:T(8,128)(2,1)S(1)} %collective-permute-done.3), channel_id=1, source_target_pairs={{0,1},{1,0},{2,3},{3,2},{4,6},{5,7},{6,4},{7,5},{8,9},{9,8},{10,11... | collective-permute-start | bytes 811016 | tf_op jit(solution)/shard_map/ppermute | solution.py:378
  29.6 17.7 %collective-permute-start.10 = (bf16[32,4224]{1,0:T(8,128)(2,1)S(1)}, bf16[32,4224]{1,0:T(8,128)(2,1)S(1)}, u32[]{:S(2)}, u32[]{:S(2)}) collective-permute-start(bf16[32,4224]{1,0:T(8,128)(2,1)S(1)} %copy-done.13), channel_id=1, source_target_pairs={{0,24},{1,25},{2,26},{3,27},{4,28},{5,29},{6,30},{7,31},{8,16},{9,... | collective-permute-start | bytes 811016 | tf_op jit(solution)/shard_map/ppermute | solution.py:378
  39.7 9.4 %collective-permute-start.9 = (bf16[64,4224]{1,0:T(8,128)(2,1)S(1)}, bf16[64,4224]{1,0:T(8,128)(2,1)S(1)}, u32[]{:S(2)}, u32[]{:S(2)}) collective-permute-start(bf16[64,4224]{1,0:T(8,128)(2,1)S(1)} %pad_maximum_fusion.2.refs_0_.refs_8_), channel_id=1, source_target_pairs={{0,2},{1,3},{2,0},{3,1},{4,5},{5,4},{6,7},{7,6},{8,10},{9,11},{10,... | collective-permute-start | bytes 1622024 | tf_op jit(solution)/shard_map/ppermute | solution.py:378
  40.6 15.9 %collective-permute-start.16 = (bf16[64,4224]{1,0:T(8,128)(2,1)S(1)}, bf16[64,4224]{1,0:T(8,128)(2,1)S(1)}, u32[]{:S(2)}, u32[]{:S(2)}) collective-permute-start(bf16[64,4224]{1,0:T(8,128)(2,1)S(1)} %pad_maximum_fusion.2.refs_0_.refs_8_), channel_id=1, source_target_pairs={{0,4},{1,5},{2,6},{3,7},{4,0},{5,1},{6,2},{7,3},{8,12},{9,13},{10,... | collective-permute-start | bytes 1622024 | tf_op jit(solution)/shard_map/ppermute | solution.py:378
  41.4 9.1 %collective-permute-start.7 = (bf16[128,4096]{1,0:T(8,128)(2,1)S(1)}, bf16[128,4096]{1,0:T(8,128)(2,1)S(1)}, u32[]{:S(2)}, u32[]{:S(2)}) collective-permute-start(bf16[128,4096]{1,0:T(8,128)(2,1)S(1)} %get-tuple-element.222), channel_id=1, source_target_pairs={{0,4},{1,5},{2,6},{3,7},{4,0},{5,1},{6,2},{7,3},{8,12},{9,13},{10,... | collective-permute-start | bytes 3145736 | tf_op jit(solution)/shard_map/ppermute | solution.py:378
  49.1 14.7 %collective-permute-start.20 = (bf16[128,4096]{1,0:T(8,128)(2,1)S(1)}, bf16[128,4096]{1,0:T(8,128)(2,1)S(1)}, u32[]{:S(2)}, u32[]{:S(2)}) collective-permute-start(bf16[128,4096]{1,0:T(8,128)(2,1)S(1)} %get-tuple-element.274), channel_id=1, source_target_pairs={{0,4},{1,5},{2,6},{3,7},{4,0},{5,1},{6,2},{7,3},{8,12},{9,13},{10,... | collective-permute-start | bytes 3145736 | tf_op jit(solution)/shard_map/ppermute | solution.py:378
  49.1 6.5 %collective-permute-start.15 = (bf16[32,4224]{1,0:T(8,128)(2,1)S(1)}, bf16[32,4224]{1,0:T(8,128)(2,1)S(1)}, u32[]{:S(2)}, u32[]{:S(2)}) collective-permute-start(bf16[32,4224]{1,0:T(8,128)(2,1)S(1)} %collective-permute-done.10), channel_id=1, source_target_pairs={{0,1},{1,0},{2,3},{3,2},{4,6},{5,7},{6,4},{7,5},{8,9},{9,8},{10,11... | collective-permute-start | bytes 811016 | tf_op jit(solution)/shard_map/ppermute | solution.py:378
  50.6 7.2 %collective-permute-start.17 = (bf16[64,4224]{1,0:T(8,128)(2,1)S(1)}, bf16[64,4224]{1,0:T(8,128)(2,1)S(1)}, u32[]{:S(2)}, u32[]{:S(2)}) collective-permute-start(bf16[64,4224]{1,0:T(8,128)(2,1)S(1)} %collective-permute-done.9.refs_1_.refs_9_), channel_id=1, source_target_pairs={{0,4},{1,5},{2,6},{3,7},{4,0},{5,1},{6,2},{7,3},{8,12},{9,13},{10,... | collective-permute-start | bytes 1622024 | tf_op jit(solution)/shard_map/ppermute | solution.py:378
  55.6 10.1 %collective-permute-start.19 = (bf16[64,4224]{1,0:T(8,128)(2,1)S(1)}, bf16[64,4224]{1,0:T(8,128)(2,1)S(1)}, u32[]{:S(2)}, u32[]{:S(2)}) collective-permute-start(bf16[64,4224]{1,0:T(8,128)(2,1)S(1)} %pad_maximum_fusion.3.refs_0_.refs_12_), channel_id=1, source_target_pairs={{0,2},{1,3},{2,0},{3,1},{4,5},{5,4},{6,7},{7,6},{8,10},{9,11},{10,... | collective-permute-start | bytes 1622024 | tf_op jit(solution)/shard_map/ppermute | solution.py:378
  56.6 14.2 %collective-permute-start.22 = (bf16[64,4224]{1,0:T(8,128)(2,1)S(1)}, bf16[64,4224]{1,0:T(8,128)(2,1)S(1)}, u32[]{:S(2)}, u32[]{:S(2)}) collective-permute-start(bf16[64,4224]{1,0:T(8,128)(2,1)S(1)} %pad_maximum_fusion.3.refs_0_.refs_12_), channel_id=1, source_target_pairs={{0,4},{1,5},{2,6},{3,7},{4,0},{5,1},{6,2},{7,3},{8,12},{9,13},{10,... | collective-permute-start | bytes 1622024 | tf_op jit(solution)/shard_map/ppermute | solution.py:378
  56.6 14.1 %collective-permute-start.14 = (bf16[64,4096]{1,0:T(8,128)(2,1)S(1)}, bf16[64,4096]{1,0:T(8,128)(2,1)S(1)}, u32[]{:S(2)}, u32[]{:S(2)}) collective-permute-start(bf16[64,4096]{1,0:T(8,128)(2,1)S(1)} %slice.55), channel_id=1, source_target_pairs={{0,2},{1,3},{2,0},{3,1},{4,5},{5,4},{6,7},{7,6},{8,10},{9,11},{10,... | collective-permute-start | bytes 1572872 | tf_op jit(solution)/shard_map/ppermute | solution.py:378
  64.2 12.4 %collective-permute-start.25 = (bf16[64,4096]{1,0:T(8,128)(2,1)S(1)}, bf16[64,4096]{1,0:T(8,128)(2,1)S(1)}, u32[]{:S(2)}, u32[]{:S(2)}) collective-permute-start(bf16[64,4096]{1,0:T(8,128)(2,1)S(1)} %slice.59), channel_id=1, source_target_pairs={{0,2},{1,3},{2,0},{3,1},{4,5},{5,4},{6,7},{7,6},{8,10},{9,11},{10,... | collective-permute-start | bytes 1572872 | tf_op jit(solution)/shard_map/ppermute | solution.py:378
  65.7 5.1 %collective-permute-start.23 = (bf16[64,4224]{1,0:T(8,128)(2,1)S(1)}, bf16[64,4224]{1,0:T(8,128)(2,1)S(1)}, u32[]{:S(2)}, u32[]{:S(2)}) collective-permute-start(bf16[64,4224]{1,0:T(8,128)(2,1)S(1)} %collective-permute-done.19.refs_1_.refs_13_), channel_id=1, source_target_pairs={{0,4},{1,5},{2,6},{3,7},{4,0},{5,1},{6,2},{7,3},{8,12},{9,13},{10,... | collective-permute-start | bytes 1622024 | tf_op jit(solution)/shard_map/ppermute | solution.py:378
  76.7 3.2 %collective-permute-start.24 = (bf16[128,4096]{1,0:T(8,128)(2,1)S(1)}, bf16[128,4096]{1,0:T(8,128)(2,1)S(1)}, u32[]{:S(2)}, u32[]{:S(2)}) collective-permute-start(bf16[128,4096]{1,0:T(8,128)(2,1)S(1)} %get-tuple-element.302), channel_id=1, source_target_pairs={{0,4},{1,5},{2,6},{3,7},{4,0},{5,1},{6,2},{7,3},{8,12},{9,13},{10,... | collective-permute-start | bytes 3145736 | tf_op jit(solution)/shard_map/ppermute | solution.py:378
  76.8 14.2 %collective-permute-start.27 = (bf16[64,4096]{1,0:T(8,128)(2,1)S(1)}, bf16[64,4096]{1,0:T(8,128)(2,1)S(1)}, u32[]{:S(2)}, u32[]{:S(2)}) collective-permute-start(bf16[64,4096]{1,0:T(8,128)(2,1)S(1)} %slice.63), channel_id=1, source_target_pairs={{0,2},{1,3},{2,0},{3,1},{4,5},{5,4},{6,7},{7,6},{8,10},{9,11},{10,... | collective-permute-start | bytes 1572872 | tf_op jit(solution)/shard_map/ppermute | solution.py:378
  77.8 15.4 %collective-permute-start.29 = (bf16[32,4096]{1,0:T(8,128)(2,1)S(1)}, bf16[32,4096]{1,0:T(8,128)(2,1)S(1)}, u32[]{:S(2)}, u32[]{:S(2)}) collective-permute-start(bf16[32,4096]{1,0:T(8,128)(2,1)S(1)} %slice.67), channel_id=1, source_target_pairs={{0,1},{1,0},{2,3},{3,2},{4,6},{5,7},{6,4},{7,5},{8,9},{9,8},{10,11... | collective-permute-start | bytes 786440 | tf_op jit(solution)/shard_map/ppermute | solution.py:378
  78.9 34.6 %collective-permute-start.21 = (bf16[32,4096]{1,0:T(8,128)(2,1)S(1)}, bf16[32,4096]{1,0:T(8,128)(2,1)S(1)}, u32[]{:S(2)}, u32[]{:S(2)}) collective-permute-start(bf16[32,4096]{1,0:T(8,128)(2,1)S(1)} %slice.57), channel_id=1, source_target_pairs={{0,1},{1,0},{2,3},{3,2},{4,6},{5,7},{6,4},{7,5},{8,9},{9,8},{10,11... | collective-permute-start | bytes 786440 | tf_op jit(solution)/shard_map/ppermute | solution.py:378
  80.2 21.4 %collective-permute-start.26 = (bf16[64,4096]{1,0:T(8,128)(2,1)S(1)}, bf16[64,4096]{1,0:T(8,128)(2,1)S(1)}, u32[]{:S(2)}, u32[]{:S(2)}) collective-permute-start(bf16[64,4096]{1,0:T(8,128)(2,1)S(1)} %slice.61), channel_id=1, source_target_pairs={{0,2},{1,3},{2,0},{3,1},{4,5},{5,4},{6,7},{7,6},{8,10},{9,11},{10,... | collective-permute-start | bytes 1572872 | tf_op jit(solution)/shard_map/ppermute | solution.py:378
  91.2 8.4 %collective-permute-start.28 = (bf16[32,4096]{1,0:T(8,128)(2,1)S(1)}, bf16[32,4096]{1,0:T(8,128)(2,1)S(1)}, u32[]{:S(2)}, u32[]{:S(2)}) collective-permute-start(bf16[32,4096]{1,0:T(8,128)(2,1)S(1)} %slice.65), channel_id=1, source_target_pairs={{0,1},{1,0},{2,3},{3,2},{4,6},{5,7},{6,4},{7,5},{8,9},{9,8},{10,11... | collective-permute-start | bytes 786440 | tf_op jit(solution)/shard_map/ppermute | solution.py:378
  93.3 8.3 %collective-permute-start.32 = (bf16[32,4096]{1,0:T(8,128)(2,1)S(1)}, bf16[32,4096]{1,0:T(8,128)(2,1)S(1)}, u32[]{:S(2)}, u32[]{:S(2)}) collective-permute-start(bf16[32,4096]{1,0:T(8,128)(2,1)S(1)} %add_convert_fusion.12), channel_id=1, source_target_pairs={{0,8},{1,9},{2,10},{3,11},{4,12},{5,13},{6,14},{7,15},{8,0},{9,1},... | collective-permute-start | bytes 786440 | tf_op jit(solution)/shard_map/ppermute | solution.py:378
  99.8 13.7 %collective-permute-start.31 = (bf16[32,4096]{1,0:T(8,128)(2,1)S(1)}, bf16[32,4096]{1,0:T(8,128)(2,1)S(1)}, u32[]{:S(2)}, u32[]{:S(2)}) collective-permute-start(bf16[32,4096]{1,0:T(8,128)(2,1)S(1)} %add_convert_fusion.11), channel_id=1, source_target_pairs={{0,16},{1,17},{2,18},{3,19},{4,20},{5,21},{6,22},{7,23},{8,24},{9,... | collective-permute-start | bytes 786440 | tf_op jit(solution)/shard_map/ppermute | solution.py:378
  101.8 11.7 %collective-permute-start.30 = (bf16[32,4096]{1,0:T(8,128)(2,1)S(1)}, bf16[32,4096]{1,0:T(8,128)(2,1)S(1)}, u32[]{:S(2)}, u32[]{:S(2)}) collective-permute-start(bf16[32,4096]{1,0:T(8,128)(2,1)S(1)} %slice.69), channel_id=1, source_target_pairs={{0,1},{1,0},{2,3},{3,2},{4,6},{5,7},{6,4},{7,5},{8,9},{9,8},{10,11... | collective-permute-start | bytes 786440 | tf_op jit(solution)/shard_map/ppermute | solution.py:378
  113.6 12.0 %collective-permute-start.33 = (bf16[32,4096]{1,0:T(8,128)(2,1)S(1)}, bf16[32,4096]{1,0:T(8,128)(2,1)S(1)}, u32[]{:S(2)}, u32[]{:S(2)}) collective-permute-start(bf16[32,4096]{1,0:T(8,128)(2,1)S(1)} %add_convert_fusion.10), channel_id=1, source_target_pairs={{0,24},{1,25},{2,26},{3,27},{4,28},{5,29},{6,30},{7,31},{8,16},{9,... | collective-permute-start | bytes 786440 | tf_op jit(solution)/shard_map/ppermute | solution.py:378
  (16 other events, 209.0 us)

commit v3 on v2

--- a/solution.py
+++ b/solution.py
@@ -134,6 +134,37 @@
     )(tokens, grad_out, routes.T, route_weight.T)
 
 
+def stage_kernel(wg_ref, wu_ref, wd_ref, wgu_ref, wd_held_ref, sems):
+    half = wg_ref.shape[1]
+    copies = [
+        pltpu.make_async_copy(wg_ref, wgu_ref.at[:, :half], sems.at[0]),
+        pltpu.make_async_copy(wu_ref, wgu_ref.at[:, half:], sems.at[1]),
+        pltpu.make_async_copy(wd_ref, wd_held_ref, sems.at[2]),
+    ]
+    for copy in copies:
+        copy.start()
+    for copy in copies:
+        copy.wait()
+
+
+def stage(weight_g, weight_u, weight_d):
+    features, half = weight_g.shape
+    return pl.pallas_call(
+        stage_kernel,
+        out_shape=(
+            jax.ShapeDtypeStruct((features, 2 * half), jnp.bfloat16),
+            jax.ShapeDtypeStruct((half, features), jnp.bfloat16),
+        ),
+        in_specs=[pl.BlockSpec(memory_space=pl.ANY)] * 3,
+        out_specs=(pl.BlockSpec(memory_space=pltpu.VMEM),) * 2,
+        scratch_shapes=[pltpu.SemaphoreType.DMA((3,))],
+        compiler_params=pltpu.CompilerParams(vmem_limit_bytes=VMEM_BYTES),
+        cost_estimate=pl.CostEstimate(
+            flops=0, bytes_accessed=12 * features * half, transcendentals=0
+        ),
+    )(weight_g, weight_u, weight_d)
+
+
 def place_copies(pieces, columns, held, sems):
     copies, row = [], 0
     for i, piece in enumerate(pieces):
@@ -145,29 +176,19 @@
 
 def forward_kernel(experts, n_pieces, expert_ref, *refs):
     pieces = refs[:n_pieces]
-    wg_ref, wu_ref, wd_ref = refs[n_pieces : n_pieces + 3]
-    keep_ref, send_ref, hid_ref, dgu_ref = refs[n_pieces + 3 : n_pieces + 7]
-    x, g, rw, wgu, wd, hid, dgu, out, back = refs[n_pieces + 7 : n_pieces + 16]
-    x_sems, g_sems, r_sems, w_sems, o_sems = refs[n_pieces + 16 :]
-    features, half = wg_ref.shape
+    wgu, wd = refs[n_pieces : n_pieces + 2]
+    keep_ref, send_ref, hid_ref, dgu_ref = refs[n_pieces + 2 : n_pieces + 6]
+    x, g, rw, hid, dgu, out, back = refs[n_pieces + 6 : n_pieces + 13]
+    x_sems, g_sems, r_sems, o_sems = refs[n_pieces + 13 :]
+    half, features = wd.shape
     own = keep_ref.shape[0]
     cut = features // 2
-    w_copies, d_copies = [], []
-    for i in range(2):
-        rows = pl.ds(i * cut, cut)
-        w_copies += [
-            pltpu.make_async_copy(wg_ref.at[rows], wgu.at[rows, :half], w_sems.at[2 * i]),
-            pltpu.make_async_copy(wu_ref.at[rows], wgu.at[rows, half:], w_sems.at[2 * i + 1]),
-        ]
-        d_copies.append(
-            pltpu.make_async_copy(wd_ref.at[:, rows], wd.at[:, rows], w_sems.at[4 + i])
-        )
     x_copies = place_copies(pieces, pl.ds(0, features), x, x_sems)
     g_copies = place_copies(pieces, pl.ds(features, features), g, g_sems)
     r_copies = place_copies(pieces, pl.ds(2 * features, LANES), rw, r_sems)
-    for copy in d_copies + g_copies + r_copies + w_copies + x_copies:
+    for copy in g_copies + r_copies + x_copies:
         copy.start()
-    for copy in d_copies + g_copies + r_copies:
+    for copy in g_copies + r_copies:
         copy.wait()
     lane = lax.broadcasted_iota(jnp.int32, rw.shape, 1)
     chosen = (lane % experts == expert_ref[0]) & (lane < 3 * experts)
@@ -176,7 +197,7 @@
         lax.dot_general(g[...], wd[...], CONTRACT_LAST, preferred_element_type=jnp.float32)
         * weight
     )
-    for copy in w_copies + x_copies:
+    for copy in x_copies:
         copy.wait()
     gate_up = jnp.dot(x[...], wgu[...], preferred_element_type=jnp.float32)
     gate, up_val = gate_up[:, :half], gate_up[:, half:]
@@ -220,9 +241,9 @@
         copy.wait()
 
 
-def forward(expert, pieces, weight_g, weight_u, weight_d, experts):
+def forward(expert, pieces, weight_gu, weight_d, experts):
     rows = sum(piece.shape[0] for piece in pieces)
-    features, half = weight_g.shape
+    half, features = weight_d.shape
     bf16 = jnp.bfloat16
     out_shape = (
         jax.ShapeDtypeStruct((rows // 2, 2 * features), bf16),
@@ -234,14 +255,13 @@
         functools.partial(forward_kernel, experts, len(pieces)),
         out_shape=out_shape,
         in_specs=[pl.BlockSpec(memory_space=pltpu.SMEM)]
-        + [pl.BlockSpec(memory_space=pl.ANY)] * (len(pieces) + 3),
+        + [pl.BlockSpec(memory_space=pl.ANY)] * len(pieces)
+        + [pl.BlockSpec(memory_space=pltpu.VMEM)] * 2,
         out_specs=tuple(pl.BlockSpec(memory_space=pl.ANY) for _ in out_shape),
         scratch_shapes=[
             pltpu.VMEM((rows, features), bf16),
             pltpu.VMEM((rows, features), bf16),
             pltpu.VMEM((rows, LANES), bf16),
-            pltpu.VMEM((features, 2 * half), bf16),
-            pltpu.VMEM((half, features), bf16),
             pltpu.VMEM((rows, half), bf16),
             pltpu.VMEM((rows, 2 * half), bf16),
             pltpu.VMEM((rows, features), bf16),
@@ -249,7 +269,6 @@
             pltpu.SemaphoreType.DMA((len(pieces),)),
             pltpu.SemaphoreType.DMA((len(pieces),)),
             pltpu.SemaphoreType.DMA((len(pieces),)),
-            pltpu.SemaphoreType.DMA((6,)),
             pltpu.SemaphoreType.DMA((8,)),
         ],
         compiler_params=pltpu.CompilerParams(vmem_limit_bytes=VMEM_BYTES),
@@ -258,7 +277,7 @@
             bytes_accessed=6 * features * half + 8 * rows * features,
             transcendentals=rows * half,
         ),
-    )(expert, *pieces, weight_g, weight_u, weight_d)
+    )(expert, *pieces, weight_gu, weight_d)
 
 
 def grads_kernel(n_pieces, n_slots, tile, *refs):
@@ -385,7 +404,6 @@
         return lambda core: z * 2 * n_local
 
     rows = tokens.shape[0]
-    weights = (w_gate[0], w_up[0], w_down[0])
     block = pack(tokens, grad_out, routes, route_weight, experts)
     now = [jnp.zeros((8, LANES), jnp.float32)]
 
@@ -432,48 +450,50 @@
     far2 = start(block, along(2))
     turn()
     two0, pt0 = spread(0, one0, block)
+    weights = stage(after(w_gate, now[0])[0], w_up[0], w_down[0])
+    weights = [wait(w) for w in weights]
     turn()
     far1 = wait(far1)
     one1 = start(far1, first)
+    far3 = start(block, along(3))
     turn()
     tt0 = across(0, two0)
+    two1, pt1 = spread(1, one1, far1)
+    turn()
     far2 = wait(far2)
     one2 = start(far2, first)
-    far3 = start(block, along(3))
-    turn()
-    two1, pt1 = spread(1, one1, far1)
-    turn()
     back0 = compute(0, pt0, tt0)
     two2, pt2 = spread(2, one2, far2)
-    tt1 = across(1, two1)
-    turn()
-    back1 = compute(1, pt1, tt1)
+    turn()
     far3 = wait(far3)
     one3 = start(far3, first)
+    tt1 = across(1, two1)
+    turn()
+    back1 = compute(1, pt1, tt1)
+    two3, pt3 = spread(3, one3, far3)
     tt2 = across(2, two2)
-    back0 = fold(0, back0)
-    turn()
-    two3, pt3 = spread(3, one3, far3)
+    turn()
     back2 = compute(2, pt2, tt2)
     back1 = fold(1, back1)
-    turn()
     tt3 = across(3, two3)
     turn()
     back2 = fold(2, back2)
+    back0 = fold(0, back0)
+    back3 = compute(3, pt3, tt3)
+    turn()
     back0 = fold_second(0, back0)
-    turn()
-    back3 = compute(3, pt3, tt3)
-    back1 = fold_second(1, back1)
-    turn()
     back3 = fold(3, back3)
     back2 = fold_second(2, back2)
+    back1 = fold_second(1, back1)
+    turn()
+    back2 = fold_first(2, back2)
+    turn()
+    back3 = fold_second(3, back3)
     turn()
     back1 = fold_first(1, back1)
-    back2 = fold_first(2, back2)
-    back3 = fold_second(3, back3)
+    back0 = fold_first(0, back0)
     turn()
     back3 = fold_first(3, back3)
-    back0 = fold_first(0, back0)
     order = [0, 1, 2, 3]
     grad_wg, grad_wu, grad_wd = weight_grads(
         [after(piece, now[0]) for z in order for piece in taken[z]],

time: 127 us -> 116 us (0.913)
  waiting for transfers between devices: 49 us -> 42.8 us
  starting transfers between devices: 35.1 us -> 32.5 us
  Pallas kernels: 34.3 us -> 32.5 us
    ppermute x34, waiting for transfers between devices: 49 us -> 42.8 us  [exchange(): return lax.ppermute(value, axes, pairs)]
    ppermute x34, starting transfers between devices: 35.1 us -> 32.5 us  [exchange(): return lax.ppermute(value, axes, pairs)]
    pallas_call x4, Pallas kernels: 23 us -> 20.7 us  [forward(): pl.pallas_call(functools.partial(forward_kernel, experts, len(pieces)), o...]
    unnamed x28 -> x24, local copies, waits for them, and re-layouts: 3.07 us -> 2.86 us
  transfers between devices with their start and end apart: 34 -> 34, of which waited for: 12 -> 16; matrix products, arithmetic and copies ran while one was open for 2% -> 3% of each run, Pallas kernels for 26% -> 26%
where the time goes in v3:
time: 116 us
  waiting for transfers between devices  42.8 us (37%)
  Pallas kernels  32.5 us (28%)
  starting transfers between devices  32.5 us (28%)
  local copies, waits for them, and re-layouts  3.8 us (3%)
  other arithmetic  2.98 us (3%)
    ppermute x34, waiting for transfers between devices, exchange(): return lax.ppermute(value, axes, pairs)  42.8 us
    ppermute x34, starting transfers between devices, exchange(): return lax.ppermute(value, axes, pairs)  32.5 us
    pallas_call x4, Pallas kernels, forward(): pl.pallas_call(functools.partial(forward_kernel, experts, len(pieces)), o...  20.7 us
    pallas_call x1, Pallas kernels, weight_grads(): pl.pallas_call(functools.partial(grads_kernel, len(pieces), len(hids), ti...  9.29 us
    unnamed x24, local copies, waits for them, and re-layouts  2.86 us
  transfers between devices with their start and end apart: 34, of which 16 were waited for; matrix products, arithmetic and copies ran while one was open for 3% of the time, Pallas kernels for 26%

profile of v3, /device:TPU:0, one launch (start us, length us, event | category | flops | bytes accessed | tf_op | source)
XLA Modules:
  0.0 115.6 jit_solution(10816699170862467048)
XLA Ops:
  0.6 2.0 %shard_map.110 = bf16[32,4224]{1,0:T(8,128)(2,1)} custom-call(bf16[32,2048]{1,0:T(8,128)(2,1)} %tok_ref.1, bf16[32,2048]{1,0:T(8,128)(2,1)} %grad_ref.1, s32[8,32]{1,0:T(8,128)} %bitcast.12, f32[8,32]{1,0:T(8,128)} %bitcast.13), custom_call_target="tpu_custom_call" | custom-call | tf_op jit(solution)/shard_map/pallas_call | solution.py:131
  2.7 2.9 %collective-permute-start = (bf16[32,4224]{1,0:T(8,128)(2,1)}, bf16[32,4224]{1,0:T(8,128)(2,1)S(1)}, u32[]{:S(2)}, u32[]{:S(2)}) collective-permute-start(bf16[32,4224]{1,0:T(8,128)(2,1)} %shard_map.110), channel_id=1, source_target_pairs={{0,1},{1,0},{2,3},{3,2},{4,6},{5,7},{6,4},{7,5},{8,9},{9,8},{10,11... | collective-permute-start | bytes 811016 | tf_op jit(solution)/shard_map/ppermute | solution.py:397
  5.6 1.6 %collective-permute-start.2 = (bf16[32,4224]{1,0:T(8,128)(2,1)}, bf16[32,4224]{1,0:T(8,128)(2,1)S(1)}, u32[]{:S(2)}, u32[]{:S(2)}) collective-permute-start(bf16[32,4224]{1,0:T(8,128)(2,1)} %shard_map.110), channel_id=1, source_target_pairs={{0,8},{1,9},{2,10},{3,11},{4,12},{5,13},{6,14},{7,15},{8,0},{9,1},... | collective-permute-start | bytes 811016 | tf_op jit(solution)/shard_map/ppermute | solution.py:397
  7.2 2.6 %collective-permute-start.1 = (bf16[32,4224]{1,0:T(8,128)(2,1)}, bf16[32,4224]{1,0:T(8,128)(2,1)S(1)}, u32[]{:S(2)}, u32[]{:S(2)}) collective-permute-start(bf16[32,4224]{1,0:T(8,128)(2,1)} %shard_map.110), channel_id=1, source_target_pairs={{0,16},{1,17},{2,18},{3,19},{4,20},{5,21},{6,22},{7,23},{8,24},{9,... | collective-permute-start | bytes 811016 | tf_op jit(solution)/shard_map/ppermute | solution.py:397
  11.3 2.1 %collective-permute-start.4 = (bf16[64,4224]{1,0:T(8,128)(2,1)S(1)}, bf16[64,4224]{1,0:T(8,128)(2,1)S(1)}, u32[]{:S(2)}, u32[]{:S(2)}) collective-permute-start(bf16[64,4224]{1,0:T(8,128)(2,1)S(1)} %pad_maximum_fusion.refs_0_), channel_id=1, source_target_pairs={{0,2},{1,3},{2,0},{3,1},{4,5},{5,4},{6,7},{7,6},{8,10},{9,11},{10,... | collective-permute-start | bytes 1622024 | tf_op jit(solution)/shard_map/ppermute | solution.py:397
  13.4 1.4 %copy-done.1 = bf16[1,2048,384]{2,1,0:T(8,128)(2,1)S(1)} copy-done((bf16[1,2048,384]{2,1,0:T(8,128)(2,1)S(1)}, bf16[1,2048,384]{2,1,0:T(8,128)(2,1)}, u32[]{:S(2)}) %copy-start.1) | copy-done | bytes 1572888
  14.8 1.4 %copy-done.2 = bf16[1,384,2048]{2,1,0:T(8,128)(2,1)S(1)} copy-done((bf16[1,384,2048]{2,1,0:T(8,128)(2,1)S(1)}, bf16[1,384,2048]{2,1,0:T(8,128)(2,1)}, u32[]{:S(2)}) %copy-start.2) | copy-done | bytes 1572888
  16.7 2.8 %collective-permute-done.2 = bf16[32,4224]{1,0:T(8,128)(2,1)S(1)} collective-permute-done((bf16[32,4224]{1,0:T(8,128)(2,1)}, bf16[32,4224]{1,0:T(8,128)(2,1)S(1)}, u32[]{:S(2)}, u32[]{:S(2)}) %collective-permute-start.2) | collective-permute-done | bytes 270368 | tf_op jit(solution)/shard_map/ppermute | solution.py:397
  19.5 1.5 %collective-permute-start.3 = (bf16[32,4224]{1,0:T(8,128)(2,1)S(1)}, bf16[32,4224]{1,0:T(8,128)(2,1)S(1)}, u32[]{:S(2)}, u32[]{:S(2)}) collective-permute-start(bf16[32,4224]{1,0:T(8,128)(2,1)S(1)} %collective-permute-done.2), channel_id=1, source_target_pairs={{0,1},{1,0},{2,3},{3,2},{4,6},{5,7},{6,4},{7,5},{8,9},{9,8},{10,11... | collective-permute-start | bytes 811016 | tf_op jit(solution)/shard_map/ppermute | solution.py:397
  21.0 2.5 %collective-permute-start.10 = (bf16[32,4224]{1,0:T(8,128)(2,1)S(1)}, bf16[32,4224]{1,0:T(8,128)(2,1)S(1)}, u32[]{:S(2)}, u32[]{:S(2)}) collective-permute-start(bf16[32,4224]{1,0:T(8,128)(2,1)S(1)} %copy-done.11), channel_id=1, source_target_pairs={{0,24},{1,25},{2,26},{3,27},{4,28},{5,29},{6,30},{7,31},{8,16},{9,... | collective-permute-start | bytes 811016 | tf_op jit(solution)/shard_map/ppermute | solution.py:397
  23.5 2.5 %collective-permute-done.3 = bf16[32,4224]{1,0:T(8,128)(2,1)S(1)} collective-permute-done((bf16[32,4224]{1,0:T(8,128)(2,1)S(1)}, bf16[32,4224]{1,0:T(8,128)(2,1)S(1)}, u32[]{:S(2)}, u32[]{:S(2)}) %collective-permute-start.3) | collective-permute-done | bytes 270368 | tf_op jit(solution)/shard_map/ppermute | solution.py:397
  26.5 1.3 %collective-permute-start.13 = (bf16[64,4224]{1,0:T(8,128)(2,1)S(1)}, bf16[64,4224]{1,0:T(8,128)(2,1)S(1)}, u32[]{:S(2)}, u32[]{:S(2)}) collective-permute-start(bf16[64,4224]{1,0:T(8,128)(2,1)S(1)} %pad_maximum_fusion.1.refs_0_.refs_4_), channel_id=1, source_target_pairs={{0,4},{1,5},{2,6},{3,7},{4,0},{5,1},{6,2},{7,3},{8,12},{9,13},{10,... | collective-permute-start | bytes 1622024 | tf_op jit(solution)/shard_map/ppermute | solution.py:397
  28.3 5.1 %shard_map.112 = (bf16[128,4096]{1,0:T(8,128)(2,1)S(1)}, bf16[128,4096]{1,0:T(8,128)(2,1)S(1)}, bf16[256,384]{1,0:T(8,128)(2,1)S(1)}, bf16[256,768]{1,0:T(8,128)(2,1)S(1)}) custom-call(s32[1]{0:T(128)} %bitcast.expert_ref, bf16[64,4224]{1,0:T(8,128)(2,1)S(1)} %pad_maximum_fusion.refs_0_, bf16[64,4224]{1,0:T(8,128)(2,1)S(1)} %collective-permute-done.4.refs_1_, ...), custom_call_target="tpu_custom_call" | custom-call | flops 48318382080 | bytes 8912896 | tf_op jit(solution)/shard_map/pallas_call | solution.py:254
  33.5 3.7 %collective-permute-done.8 = bf16[32,4224]{1,0:T(8,128)(2,1)S(1)} collective-permute-done((bf16[32,4224]{1,0:T(8,128)(2,1)S(1)}, bf16[32,4224]{1,0:T(8,128)(2,1)S(1)}, u32[]{:S(2)}, u32[]{:S(2)}) %collective-permute-start.8) | collective-permute-done | bytes 270368 | tf_op jit(solution)/shard_map/ppermute | solution.py:397
  38.8 1.3 %collective-permute-start.15 = (bf16[64,4224]{1,0:T(8,128)(2,1)S(1)}, bf16[64,4224]{1,0:T(8,128)(2,1)S(1)}, u32[]{:S(2)}, u32[]{:S(2)}) collective-permute-start(bf16[64,4224]{1,0:T(8,128)(2,1)S(1)} %pad_maximum_fusion.2.refs_0_.refs_8_), channel_id=1, source_target_pairs={{0,4},{1,5},{2,6},{3,7},{4,0},{5,1},{6,2},{7,3},{8,12},{9,13},{10,... | collective-permute-start | bytes 1622024 | tf_op jit(solution)/shard_map/ppermute | solution.py:397
  40.7 5.1 %shard_map.113 = (bf16[128,4096]{1,0:T(8,128)(2,1)S(1)}, bf16[128,4096]{1,0:T(8,128)(2,1)S(1)}, bf16[256,384]{1,0:T(8,128)(2,1)S(1)}, bf16[256,768]{1,0:T(8,128)(2,1)S(1)}) custom-call(s32[1]{0:T(128)} %bitcast.expert_ref, bf16[64,4224]{1,0:T(8,128)(2,1)S(1)} %pad_maximum_fusion.1.refs_0_.refs_4_, ...), custom_call_target="tpu_custom_call" | custom-call | flops 48318382080 | bytes 8912896 | tf_op jit(solution)/shard_map/pallas_call | solution.py:254
  45.8 3.7 %collective-permute-done.11 = bf16[32,4224]{1,0:T(8,128)(2,1)S(1)} collective-permute-done((bf16[32,4224]{1,0:T(8,128)(2,1)S(1)}, bf16[32,4224]{1,0:T(8,128)(2,1)S(1)}, u32[]{:S(2)}, u32[]{:S(2)}) %collective-permute-start.11) | collective-permute-done | bytes 270368 | tf_op jit(solution)/shard_map/ppermute | solution.py:397
  51.0 1.3 %collective-permute-start.21 = (bf16[64,4224]{1,0:T(8,128)(2,1)S(1)}, bf16[64,4224]{1,0:T(8,128)(2,1)S(1)}, u32[]{:S(2)}, u32[]{:S(2)}) collective-permute-start(bf16[64,4224]{1,0:T(8,128)(2,1)S(1)} %pad_maximum_fusion.3.refs_0_.refs_12_), channel_id=1, source_target_pairs={{0,4},{1,5},{2,6},{3,7},{4,0},{5,1},{6,2},{7,3},{8,12},{9,13},{10,... | collective-permute-start | bytes 1622024 | tf_op jit(solution)/shard_map/ppermute | solution.py:397
  52.6 5.3 %shard_map.114 = (bf16[128,4096]{1,0:T(8,128)(2,1)S(1)}, bf16[128,4096]{1,0:T(8,128)(2,1)S(1)}, bf16[256,384]{1,0:T(8,128)(2,1)S(1)}, bf16[256,768]{1,0:T(8,128)(2,1)S(1)}) custom-call(s32[1]{0:T(128)} %bitcast.expert_ref, bf16[64,4224]{1,0:T(8,128)(2,1)S(1)} %pad_maximum_fusion.2.refs_0_.refs_8_, ...), custom_call_target="tpu_custom_call" | custom-call | flops 48318382080 | bytes 8912896 | tf_op jit(solution)/shard_map/pallas_call | solution.py:254
  58.5 1.5 %collective-permute-done.18.refs_1_.refs_13_ = bf16[64,4224]{1,0:T(8,128)(2,1)S(1)} collective-permute-done((bf16[64,4224]{1,0:T(8,128)(2,1)S(1)}, bf16[64,4224]{1,0:T(8,128)(2,1)S(1)}, u32[]{:S(2)}, u32[]{:S(2)}) %collective-permute-start.18) | collective-permute-done | bytes 540704 | tf_op jit(solution)/shard_map/ppermute | solution.py:397
  61.2 1.6 %collective-permute-start.20 = (bf16[64,4096]{1,0:T(8,128)(2,1)S(1)}, bf16[64,4096]{1,0:T(8,128)(2,1)S(1)}, u32[]{:S(2)}, u32[]{:S(2)}) collective-permute-start(bf16[64,4096]{1,0:T(8,128)(2,1)S(1)} %slice.55), channel_id=1, source_target_pairs={{0,2},{1,3},{2,0},{3,1},{4,5},{5,4},{6,7},{7,6},{8,10},{9,11},{10,... | collective-permute-start | bytes 1572872 | tf_op jit(solution)/shard_map/ppermute | solution.py:397
  62.8 5.1 %shard_map.115 = (bf16[128,4096]{1,0:T(8,128)(2,1)S(1)}, bf16[128,4096]{1,0:T(8,128)(2,1)S(1)}, bf16[256,384]{1,0:T(8,128)(2,1)S(1)}, bf16[256,768]{1,0:T(8,128)(2,1)S(1)}) custom-call(s32[1]{0:T(128)} %bitcast.expert_ref, bf16[64,4224]{1,0:T(8,128)(2,1)S(1)} %pad_maximum_fusion.3.refs_0_.refs_12_, ...), custom_call_target="tpu_custom_call" | custom-call | flops 48318382080 | bytes 8912896 | tf_op jit(solution)/shard_map/pallas_call | solution.py:254
  68.6 6.3 %collective-permute-done.20 = bf16[64,4096]{1,0:T(8,128)(2,1)S(1)} collective-permute-done((bf16[64,4096]{1,0:T(8,128)(2,1)S(1)}, bf16[64,4096]{1,0:T(8,128)(2,1)S(1)}, u32[]{:S(2)}, u32[]{:S(2)}) %collective-permute-start.20) | collective-permute-done | bytes 524320 | tf_op jit(solution)/shard_map/ppermute | solution.py:397
  75.1 1.6 %collective-permute-start.23 = (bf16[32,4096]{1,0:T(8,128)(2,1)S(1)}, bf16[32,4096]{1,0:T(8,128)(2,1)S(1)}, u32[]{:S(2)}, u32[]{:S(2)}) collective-permute-start(bf16[32,4096]{1,0:T(8,128)(2,1)S(1)} %slice.57), channel_id=1, source_target_pairs={{0,1},{1,0},{2,3},{3,2},{4,6},{5,7},{6,4},{7,5},{8,9},{9,8},{10,11... | collective-permute-start | bytes 786440 | tf_op jit(solution)/shard_map/ppermute | solution.py:397
  76.9 6.5 %collective-permute-done.25 = bf16[64,4096]{1,0:T(8,128)(2,1)S(1)} collective-permute-done((bf16[64,4096]{1,0:T(8,128)(2,1)S(1)}, bf16[64,4096]{1,0:T(8,128)(2,1)S(1)}, u32[]{:S(2)}, u32[]{:S(2)}) %collective-permute-start.25) | collective-permute-done | bytes 524320 | tf_op jit(solution)/shard_map/ppermute | solution.py:397
  83.5 1.6 %collective-permute-start.29 = (bf16[32,4096]{1,0:T(8,128)(2,1)S(1)}, bf16[32,4096]{1,0:T(8,128)(2,1)S(1)}, u32[]{:S(2)}, u32[]{:S(2)}) collective-permute-start(bf16[32,4096]{1,0:T(8,128)(2,1)S(1)} %slice.67), channel_id=1, source_target_pairs={{0,1},{1,0},{2,3},{3,2},{4,6},{5,7},{6,4},{7,5},{8,9},{9,8},{10,11... | collective-permute-start | bytes 786440 | tf_op jit(solution)/shard_map/ppermute | solution.py:397
  86.2 6.6 %collective-permute-done.29 = bf16[32,4096]{1,0:T(8,128)(2,1)S(1)} collective-permute-done((bf16[32,4096]{1,0:T(8,128)(2,1)S(1)}, bf16[32,4096]{1,0:T(8,128)(2,1)S(1)}, u32[]{:S(2)}, u32[]{:S(2)}) %collective-permute-start.29) | collective-permute-done | bytes 262176 | tf_op jit(solution)/shard_map/ppermute | solution.py:397
  93.6 1.9 %collective-permute-done.28 = bf16[64,4096]{1,0:T(8,128)(2,1)S(1)} collective-permute-done((bf16[64,4096]{1,0:T(8,128)(2,1)S(1)}, bf16[64,4096]{1,0:T(8,128)(2,1)S(1)}, u32[]{:S(2)}, u32[]{:S(2)}) %collective-permute-start.28) | collective-permute-done | bytes 524320 | tf_op jit(solution)/shard_map/ppermute | solution.py:397
  96.0 1.7 %collective-permute-start.32 = (bf16[32,4096]{1,0:T(8,128)(2,1)S(1)}, bf16[32,4096]{1,0:T(8,128)(2,1)S(1)}, u32[]{:S(2)}, u32[]{:S(2)}) collective-permute-start(bf16[32,4096]{1,0:T(8,128)(2,1)S(1)} %slice.69), channel_id=1, source_target_pairs={{0,1},{1,0},{2,3},{3,2},{4,6},{5,7},{6,4},{7,5},{8,9},{9,8},{10,11... | collective-permute-start | bytes 786440 | tf_op jit(solution)/shard_map/ppermute | solution.py:397
  98.5 4.1 %collective-permute-done.30 = bf16[32,4096]{1,0:T(8,128)(2,1)S(1)} collective-permute-done((bf16[32,4096]{1,0:T(8,128)(2,1)S(1)}, bf16[32,4096]{1,0:T(8,128)(2,1)S(1)}, u32[]{:S(2)}, u32[]{:S(2)}) %collective-permute-start.30) | collective-permute-done | bytes 262176 | tf_op jit(solution)/shard_map/ppermute | solution.py:397
  102.8 2.6 %collective-permute-start.33 = (bf16[32,4096]{1,0:T(8,128)(2,1)S(1)}, bf16[32,4096]{1,0:T(8,128)(2,1)S(1)}, u32[]{:S(2)}, u32[]{:S(2)}) collective-permute-start(bf16[32,4096]{1,0:T(8,128)(2,1)S(1)} %add_convert_fusion.9), channel_id=1, source_target_pairs={{0,24},{1,25},{2,26},{3,27},{4,28},{5,29},{6,30},{7,31},{8,16},{9,... | collective-permute-start | bytes 786440 | tf_op jit(solution)/shard_map/ppermute | solution.py:397
  105.4 9.3 %shard_map.116 = (bf16[2048,384]{1,0:T(8,128)(2,1)}, bf16[2048,384]{1,0:T(8,128)(2,1)}, bf16[384,2048]{1,0:T(8,128)(2,1)}) custom-call(bf16[64,4224]{1,0:T(8,128)(2,1)S(1)} %copy-done.4, bf16[64,4224]{1,0:T(8,128)(2,1)S(1)} %copy-done.6, bf16[64,4224]{1,0:T(8,128)(2,1)S(1)} %copy-done.8, bf16[64,4224]{1,0:T(8,128)(2,1)S(1)} %copy-done.10, ...), custom_call_target="tpu_custom_call" | custom-call | flops 96636764160 | bytes 13107200 | tf_op jit(solution)/shard_map/pallas_call | solution.py:336
  (93 shorter events, 14.0 us)
Async XLA Ops:
  2.7 7.6 %collective-permute-start = (bf16[32,4224]{1,0:T(8,128)(2,1)}, bf16[32,4224]{1,0:T(8,128)(2,1)S(1)}, u32[]{:S(2)}, u32[]{:S(2)}) collective-permute-start(bf16[32,4224]{1,0:T(8,128)(2,1)} %shard_map.110), channel_id=1, source_target_pairs={{0,1},{1,0},{2,3},{3,2},{4,6},{5,7},{6,4},{7,5},{8,9},{9,8},{10,11... | collective-permute-start | bytes 811016 | tf_op jit(solution)/shard_map/ppermute | solution.py:397
  5.6 13.8 %collective-permute-start.2 = (bf16[32,4224]{1,0:T(8,128)(2,1)}, bf16[32,4224]{1,0:T(8,128)(2,1)S(1)}, u32[]{:S(2)}, u32[]{:S(2)}) collective-permute-start(bf16[32,4224]{1,0:T(8,128)(2,1)} %shard_map.110), channel_id=1, source_target_pairs={{0,8},{1,9},{2,10},{3,11},{4,12},{5,13},{6,14},{7,15},{8,0},{9,1},... | collective-permute-start | bytes 811016 | tf_op jit(solution)/shard_map/ppermute | solution.py:397
  7.2 18.9 %collective-permute-start.1 = (bf16[32,4224]{1,0:T(8,128)(2,1)}, bf16[32,4224]{1,0:T(8,128)(2,1)S(1)}, u32[]{:S(2)}, u32[]{:S(2)}) collective-permute-start(bf16[32,4224]{1,0:T(8,128)(2,1)} %shard_map.110), channel_id=1, source_target_pairs={{0,16},{1,17},{2,18},{3,19},{4,20},{5,21},{6,22},{7,23},{8,24},{9,... | collective-permute-start | bytes 811016 | tf_op jit(solution)/shard_map/ppermute | solution.py:397
  11.3 12.2 %collective-permute-start.4 = (bf16[64,4224]{1,0:T(8,128)(2,1)S(1)}, bf16[64,4224]{1,0:T(8,128)(2,1)S(1)}, u32[]{:S(2)}, u32[]{:S(2)}) collective-permute-start(bf16[64,4224]{1,0:T(8,128)(2,1)S(1)} %pad_maximum_fusion.refs_0_), channel_id=1, source_target_pairs={{0,2},{1,3},{2,0},{3,1},{4,5},{5,4},{6,7},{7,6},{8,10},{9,11},{10,... | collective-permute-start | bytes 1622024 | tf_op jit(solution)/shard_map/ppermute | solution.py:397
  13.4 14.4 %collective-permute-start.5 = (bf16[64,4224]{1,0:T(8,128)(2,1)S(1)}, bf16[64,4224]{1,0:T(8,128)(2,1)S(1)}, u32[]{:S(2)}, u32[]{:S(2)}) collective-permute-start(bf16[64,4224]{1,0:T(8,128)(2,1)S(1)} %pad_maximum_fusion.refs_0_), channel_id=1, source_target_pairs={{0,4},{1,5},{2,6},{3,7},{4,0},{5,1},{6,2},{7,3},{8,12},{9,13},{10,... | collective-permute-start | bytes 1622024 | tf_op jit(solution)/shard_map/ppermute | solution.py:397
  19.5 6.5 %collective-permute-start.3 = (bf16[32,4224]{1,0:T(8,128)(2,1)S(1)}, bf16[32,4224]{1,0:T(8,128)(2,1)S(1)}, u32[]{:S(2)}, u32[]{:S(2)}) collective-permute-start(bf16[32,4224]{1,0:T(8,128)(2,1)S(1)} %collective-permute-done.2), channel_id=1, source_target_pairs={{0,1},{1,0},{2,3},{3,2},{4,6},{5,7},{6,4},{7,5},{8,9},{9,8},{10,11... | collective-permute-start | bytes 811016 | tf_op jit(solution)/shard_map/ppermute | solution.py:397
  21.0 16.3 %collective-permute-start.10 = (bf16[32,4224]{1,0:T(8,128)(2,1)S(1)}, bf16[32,4224]{1,0:T(8,128)(2,1)S(1)}, u32[]{:S(2)}, u32[]{:S(2)}) collective-permute-start(bf16[32,4224]{1,0:T(8,128)(2,1)S(1)} %copy-done.11), channel_id=1, source_target_pairs={{0,24},{1,25},{2,26},{3,27},{4,28},{5,29},{6,30},{7,31},{8,16},{9,... | collective-permute-start | bytes 811016 | tf_op jit(solution)/shard_map/ppermute | solution.py:397
  26.0 2.3 %collective-permute-start.6 = (bf16[64,4224]{1,0:T(8,128)(2,1)S(1)}, bf16[64,4224]{1,0:T(8,128)(2,1)S(1)}, u32[]{:S(2)}, u32[]{:S(2)}) collective-permute-start(bf16[64,4224]{1,0:T(8,128)(2,1)S(1)} %collective-permute-done.4.refs_1_), channel_id=1, source_target_pairs={{0,4},{1,5},{2,6},{3,7},{4,0},{5,1},{6,2},{7,3},{8,12},{9,13},{10,... | collective-permute-start | bytes 1622024 | tf_op jit(solution)/shard_map/ppermute | solution.py:397
  26.1 12.3 %collective-permute-start.12 = (bf16[64,4224]{1,0:T(8,128)(2,1)S(1)}, bf16[64,4224]{1,0:T(8,128)(2,1)S(1)}, u32[]{:S(2)}, u32[]{:S(2)}) collective-permute-start(bf16[64,4224]{1,0:T(8,128)(2,1)S(1)} %pad_maximum_fusion.1.refs_0_.refs_4_), channel_id=1, source_target_pairs={{0,2},{1,3},{2,0},{3,1},{4,5},{5,4},{6,7},{7,6},{8,10},{9,11},{10,... | collective-permute-start | bytes 1622024 | tf_op jit(solution)/shard_map/ppermute | solution.py:397
  26.5 13.6 %collective-permute-start.13 = (bf16[64,4224]{1,0:T(8,128)(2,1)S(1)}, bf16[64,4224]{1,0:T(8,128)(2,1)S(1)}, u32[]{:S(2)}, u32[]{:S(2)}) collective-permute-start(bf16[64,4224]{1,0:T(8,128)(2,1)S(1)} %pad_maximum_fusion.1.refs_0_.refs_4_), channel_id=1, source_target_pairs={{0,4},{1,5},{2,6},{3,7},{4,0},{5,1},{6,2},{7,3},{8,12},{9,13},{10,... | collective-permute-start | bytes 1622024 | tf_op jit(solution)/shard_map/ppermute | solution.py:397
  27.8 9.4 %collective-permute-start.8 = (bf16[32,4224]{1,0:T(8,128)(2,1)S(1)}, bf16[32,4224]{1,0:T(8,128)(2,1)S(1)}, u32[]{:S(2)}, u32[]{:S(2)}) collective-permute-start(bf16[32,4224]{1,0:T(8,128)(2,1)S(1)} %collective-permute-done.1), channel_id=1, source_target_pairs={{0,1},{1,0},{2,3},{3,2},{4,6},{5,7},{6,4},{7,5},{8,9},{9,8},{10,11... | collective-permute-start | bytes 811016 | tf_op jit(solution)/shard_map/ppermute | solution.py:397
  38.4 12.3 %collective-permute-start.9 = (bf16[64,4224]{1,0:T(8,128)(2,1)S(1)}, bf16[64,4224]{1,0:T(8,128)(2,1)S(1)}, u32[]{:S(2)}, u32[]{:S(2)}) collective-permute-start(bf16[64,4224]{1,0:T(8,128)(2,1)S(1)} %pad_maximum_fusion.2.refs_0_.refs_8_), channel_id=1, source_target_pairs={{0,2},{1,3},{2,0},{3,1},{4,5},{5,4},{6,7},{7,6},{8,10},{9,11},{10,... | collective-permute-start | bytes 1622024 | tf_op jit(solution)/shard_map/ppermute | solution.py:397
  38.8 13.6 %collective-permute-start.15 = (bf16[64,4224]{1,0:T(8,128)(2,1)S(1)}, bf16[64,4224]{1,0:T(8,128)(2,1)S(1)}, u32[]{:S(2)}, u32[]{:S(2)}) collective-permute-start(bf16[64,4224]{1,0:T(8,128)(2,1)S(1)} %pad_maximum_fusion.2.refs_0_.refs_8_), channel_id=1, source_target_pairs={{0,4},{1,5},{2,6},{3,7},{4,0},{5,1},{6,2},{7,3},{8,12},{9,13},{10,... | collective-permute-start | bytes 1622024 | tf_op jit(solution)/shard_map/ppermute | solution.py:397
  40.1 9.4 %collective-permute-start.11 = (bf16[32,4224]{1,0:T(8,128)(2,1)S(1)}, bf16[32,4224]{1,0:T(8,128)(2,1)S(1)}, u32[]{:S(2)}, u32[]{:S(2)}) collective-permute-start(bf16[32,4224]{1,0:T(8,128)(2,1)S(1)} %collective-permute-done.10), channel_id=1, source_target_pairs={{0,1},{1,0},{2,3},{3,2},{4,6},{5,7},{6,4},{7,5},{8,9},{9,8},{10,11... | collective-permute-start | bytes 811016 | tf_op jit(solution)/shard_map/ppermute | solution.py:397
  40.6 20.2 %collective-permute-start.7 = (bf16[128,4096]{1,0:T(8,128)(2,1)S(1)}, bf16[128,4096]{1,0:T(8,128)(2,1)S(1)}, u32[]{:S(2)}, u32[]{:S(2)}) collective-permute-start(bf16[128,4096]{1,0:T(8,128)(2,1)S(1)} %get-tuple-element.236), channel_id=1, source_target_pairs={{0,4},{1,5},{2,6},{3,7},{4,0},{5,1},{6,2},{7,3},{8,12},{9,13},{10,... | collective-permute-start | bytes 3145736 | tf_op jit(solution)/shard_map/ppermute | solution.py:397
  50.6 9.4 %collective-permute-start.18 = (bf16[64,4224]{1,0:T(8,128)(2,1)S(1)}, bf16[64,4224]{1,0:T(8,128)(2,1)S(1)}, u32[]{:S(2)}, u32[]{:S(2)}) collective-permute-start(bf16[64,4224]{1,0:T(8,128)(2,1)S(1)} %pad_maximum_fusion.3.refs_0_.refs_12_), channel_id=1, source_target_pairs={{0,2},{1,3},{2,0},{3,1},{4,5},{5,4},{6,7},{7,6},{8,10},{9,11},{10,... | collective-permute-start | bytes 1622024 | tf_op jit(solution)/shard_map/ppermute | solution.py:397
  51.0 11.8 %collective-permute-start.21 = (bf16[64,4224]{1,0:T(8,128)(2,1)S(1)}, bf16[64,4224]{1,0:T(8,128)(2,1)S(1)}, u32[]{:S(2)}, u32[]{:S(2)}) collective-permute-start(bf16[64,4224]{1,0:T(8,128)(2,1)S(1)} %pad_maximum_fusion.3.refs_0_.refs_12_), channel_id=1, source_target_pairs={{0,4},{1,5},{2,6},{3,7},{4,0},{5,1},{6,2},{7,3},{8,12},{9,13},{10,... | collective-permute-start | bytes 1622024 | tf_op jit(solution)/shard_map/ppermute | solution.py:397
  52.4 5.9 %collective-permute-start.19 = (bf16[128,4096]{1,0:T(8,128)(2,1)S(1)}, bf16[128,4096]{1,0:T(8,128)(2,1)S(1)}, u32[]{:S(2)}, u32[]{:S(2)}) collective-permute-start(bf16[128,4096]{1,0:T(8,128)(2,1)S(1)} %get-tuple-element.283), channel_id=1, source_target_pairs={{0,4},{1,5},{2,6},{3,7},{4,0},{5,1},{6,2},{7,3},{8,12},{9,13},{10,... | collective-permute-start | bytes 3145736 | tf_op jit(solution)/shard_map/ppermute | solution.py:397
  57.9 2.7 %collective-permute-start.17 = (bf16[128,4096]{1,0:T(8,128)(2,1)S(1)}, bf16[128,4096]{1,0:T(8,128)(2,1)S(1)}, u32[]{:S(2)}, u32[]{:S(2)}) collective-permute-start(bf16[128,4096]{1,0:T(8,128)(2,1)S(1)} %get-tuple-element.279), channel_id=1, source_target_pairs={{0,4},{1,5},{2,6},{3,7},{4,0},{5,1},{6,2},{7,3},{8,12},{9,13},{10,... | collective-permute-start | bytes 3145736 | tf_op jit(solution)/shard_map/ppermute | solution.py:397
  60.0 2.8 %collective-permute-start.22 = (bf16[64,4224]{1,0:T(8,128)(2,1)S(1)}, bf16[64,4224]{1,0:T(8,128)(2,1)S(1)}, u32[]{:S(2)}, u32[]{:S(2)}) collective-permute-start(bf16[64,4224]{1,0:T(8,128)(2,1)S(1)} %collective-permute-done.18.refs_1_.refs_13_), channel_id=1, source_target_pairs={{0,4},{1,5},{2,6},{3,7},{4,0},{5,1},{6,2},{7,3},{8,12},{9,13},{10,... | collective-permute-start | bytes 1622024 | tf_op jit(solution)/shard_map/ppermute | solution.py:397
  60.0 25.0 %collective-permute-start.24 = (bf16[64,4096]{1,0:T(8,128)(2,1)S(1)}, bf16[64,4096]{1,0:T(8,128)(2,1)S(1)}, u32[]{:S(2)}, u32[]{:S(2)}) collective-permute-start(bf16[64,4096]{1,0:T(8,128)(2,1)S(1)} %slice.59), channel_id=1, source_target_pairs={{0,2},{1,3},{2,0},{3,1},{4,5},{5,4},{6,7},{7,6},{8,10},{9,11},{10,... | collective-permute-start | bytes 1572872 | tf_op jit(solution)/shard_map/ppermute | solution.py:397
  61.2 13.7 %collective-permute-start.20 = (bf16[64,4096]{1,0:T(8,128)(2,1)S(1)}, bf16[64,4096]{1,0:T(8,128)(2,1)S(1)}, u32[]{:S(2)}, u32[]{:S(2)}) collective-permute-start(bf16[64,4096]{1,0:T(8,128)(2,1)S(1)} %slice.55), channel_id=1, source_target_pairs={{0,2},{1,3},{2,0},{3,1},{4,5},{5,4},{6,7},{7,6},{8,10},{9,11},{10,... | collective-permute-start | bytes 1572872 | tf_op jit(solution)/shard_map/ppermute | solution.py:397
  68.0 8.7 %collective-permute-start.26 = (bf16[128,4096]{1,0:T(8,128)(2,1)S(1)}, bf16[128,4096]{1,0:T(8,128)(2,1)S(1)}, u32[]{:S(2)}, u32[]{:S(2)}) collective-permute-start(bf16[128,4096]{1,0:T(8,128)(2,1)S(1)} %get-tuple-element.320), channel_id=1, source_target_pairs={{0,4},{1,5},{2,6},{3,7},{4,0},{5,1},{6,2},{7,3},{8,12},{9,13},{10,... | collective-permute-start | bytes 3145736 | tf_op jit(solution)/shard_map/ppermute | solution.py:397
  68.0 15.3 %collective-permute-start.25 = (bf16[64,4096]{1,0:T(8,128)(2,1)S(1)}, bf16[64,4096]{1,0:T(8,128)(2,1)S(1)}, u32[]{:S(2)}, u32[]{:S(2)}) collective-permute-start(bf16[64,4096]{1,0:T(8,128)(2,1)S(1)} %slice.61), channel_id=1, source_target_pairs={{0,2},{1,3},{2,0},{3,1},{4,5},{5,4},{6,7},{7,6},{8,10},{9,11},{10,... | collective-permute-start | bytes 1572872 | tf_op jit(solution)/shard_map/ppermute | solution.py:397
  75.1 20.9 %collective-permute-start.23 = (bf16[32,4096]{1,0:T(8,128)(2,1)S(1)}, bf16[32,4096]{1,0:T(8,128)(2,1)S(1)}, u32[]{:S(2)}, u32[]{:S(2)}) collective-permute-start(bf16[32,4096]{1,0:T(8,128)(2,1)S(1)} %slice.57), channel_id=1, source_target_pairs={{0,1},{1,0},{2,3},{3,2},{4,6},{5,7},{6,4},{7,5},{8,9},{9,8},{10,11... | collective-permute-start | bytes 786440 | tf_op jit(solution)/shard_map/ppermute | solution.py:397
  83.5 9.3 %collective-permute-start.29 = (bf16[32,4096]{1,0:T(8,128)(2,1)S(1)}, bf16[32,4096]{1,0:T(8,128)(2,1)S(1)}, u32[]{:S(2)}, u32[]{:S(2)}) collective-permute-start(bf16[32,4096]{1,0:T(8,128)(2,1)S(1)} %slice.67), channel_id=1, source_target_pairs={{0,1},{1,0},{2,3},{3,2},{4,6},{5,7},{6,4},{7,5},{8,9},{9,8},{10,11... | collective-permute-start | bytes 786440 | tf_op jit(solution)/shard_map/ppermute | solution.py:397
  85.2 10.3 %collective-permute-start.28 = (bf16[64,4096]{1,0:T(8,128)(2,1)S(1)}, bf16[64,4096]{1,0:T(8,128)(2,1)S(1)}, u32[]{:S(2)}, u32[]{:S(2)}) collective-permute-start(bf16[64,4096]{1,0:T(8,128)(2,1)S(1)} %slice.65), channel_id=1, source_target_pairs={{0,2},{1,3},{2,0},{3,1},{4,5},{5,4},{6,7},{7,6},{8,10},{9,11},{10,... | collective-permute-start | bytes 1572872 | tf_op jit(solution)/shard_map/ppermute | solution.py:397
  85.8 10.1 %collective-permute-start.27 = (bf16[32,4096]{1,0:T(8,128)(2,1)S(1)}, bf16[32,4096]{1,0:T(8,128)(2,1)S(1)}, u32[]{:S(2)}, u32[]{:S(2)}) collective-permute-start(bf16[32,4096]{1,0:T(8,128)(2,1)S(1)} %slice.63), channel_id=1, source_target_pairs={{0,1},{1,0},{2,3},{3,2},{4,6},{5,7},{6,4},{7,5},{8,9},{9,8},{10,11... | collective-permute-start | bytes 786440 | tf_op jit(solution)/shard_map/ppermute | solution.py:397
  92.9 9.8 %collective-permute-start.30 = (bf16[32,4096]{1,0:T(8,128)(2,1)S(1)}, bf16[32,4096]{1,0:T(8,128)(2,1)S(1)}, u32[]{:S(2)}, u32[]{:S(2)}) collective-permute-start(bf16[32,4096]{1,0:T(8,128)(2,1)S(1)} %add_convert_fusion.12), channel_id=1, source_target_pairs={{0,16},{1,17},{2,18},{3,19},{4,20},{5,21},{6,22},{7,23},{8,24},{9,... | collective-permute-start | bytes 786440 | tf_op jit(solution)/shard_map/ppermute | solution.py:397
  96.0 6.7 %collective-permute-start.32 = (bf16[32,4096]{1,0:T(8,128)(2,1)S(1)}, bf16[32,4096]{1,0:T(8,128)(2,1)S(1)}, u32[]{:S(2)}, u32[]{:S(2)}) collective-permute-start(bf16[32,4096]{1,0:T(8,128)(2,1)S(1)} %slice.69), channel_id=1, source_target_pairs={{0,1},{1,0},{2,3},{3,2},{4,6},{5,7},{6,4},{7,5},{8,9},{9,8},{10,11... | collective-permute-start | bytes 786440 | tf_op jit(solution)/shard_map/ppermute | solution.py:397
  97.7 17.0 %collective-permute-start.31 = (bf16[32,4096]{1,0:T(8,128)(2,1)S(1)}, bf16[32,4096]{1,0:T(8,128)(2,1)S(1)}, u32[]{:S(2)}, u32[]{:S(2)}) collective-permute-start(bf16[32,4096]{1,0:T(8,128)(2,1)S(1)} %add_convert_fusion.11), channel_id=1, source_target_pairs={{0,8},{1,9},{2,10},{3,11},{4,12},{5,13},{6,14},{7,15},{8,0},{9,1},... | collective-permute-start | bytes 786440 | tf_op jit(solution)/shard_map/ppermute | solution.py:397
  102.8 11.9 %collective-permute-start.33 = (bf16[32,4096]{1,0:T(8,128)(2,1)S(1)}, bf16[32,4096]{1,0:T(8,128)(2,1)S(1)}, u32[]{:S(2)}, u32[]{:S(2)}) collective-permute-start(bf16[32,4096]{1,0:T(8,128)(2,1)S(1)} %add_convert_fusion.9), channel_id=1, source_target_pairs={{0,24},{1,25},{2,26},{3,27},{4,28},{5,29},{6,30},{7,31},{8,16},{9,... | collective-permute-start | bytes 786440 | tf_op jit(solution)/shard_map/ppermute | solution.py:397
  (14 other events, 101.3 us)

commit v4 on v3

--- a/solution.py
+++ b/solution.py
@@ -353,7 +353,7 @@
         ],
         compiler_params=pltpu.CompilerParams(vmem_limit_bytes=VMEM_BYTES),
         cost_estimate=pl.CostEstimate(
-            flops=6 * 20 * rows * features * half,
+            flops=1,
             bytes_accessed=6 * features * half + 4 * rows * features,
             transcendentals=0,
         ),
@@ -383,6 +383,24 @@
     )(token)
 
 
+def total_kernel(*refs):
+    parts, (mixed_ref, grad_ref) = refs[:-2], refs[-2:]
+    features = mixed_ref.shape[1]
+    for ref, place in ((mixed_ref, pl.ds(0, features)), (grad_ref, pl.ds(features, features))):
+        ref[...] = sum(part[:, place].astype(jnp.float32) for part in parts).astype(jnp.bfloat16)
+
+
+def total(parts):
+    rows, features = parts[0].shape
+    shape = jax.ShapeDtypeStruct((rows, features // 2), jnp.bfloat16)
+    return pl.pallas_call(
+        total_kernel,
+        out_shape=(shape, shape),
+        compiler_params=pltpu.CompilerParams(vmem_limit_bytes=VMEM_BYTES),
+        cost_estimate=pl.CostEstimate(flops=1, bytes_accessed=1, transcendentals=0),
+    )(*parts)
+
+
 def dense_shards(tokens, grad_out, routes, route_weight, w_gate, w_up, w_down):
     n_node, n_local = lax.axis_size("node"), lax.axis_size("local")
     experts = n_node * n_local // 2
@@ -502,10 +520,10 @@
     )
     grad_wg = wait(grad_wg)
     arrived = (back0, wait(back2), wait(back1), wait(back3))
-    final = sum(part.astype(jnp.float32) for part in arrived).astype(jnp.bfloat16)
+    mixed, grad_tokens = total(arrived)
     return (
-        final[:, :features],
-        final[:, features:],
+        mixed,
+        grad_tokens,
         grad_wg[None],
         grad_wu[None],
         grad_wd[None],

time: 116 us -> 116 us (level)
  no operation moved by 1% of the time
where the time goes in v4:
time: 116 us
  waiting for transfers between devices  42.6 us (37%)
  Pallas kernels  33.3 us (29%)
  starting transfers between devices  32.7 us (28%)
  local copies, waits for them, and re-layouts  3.08 us (3%)
  other arithmetic  2.85 us (2%)
    ppermute x34, waiting for transfers between devices, exchange(): return lax.ppermute(value, axes, pairs)  42.6 us
    ppermute x34, starting transfers between devices, exchange(): return lax.ppermute(value, axes, pairs)  32.7 us
    pallas_call x4, Pallas kernels, forward(): pl.pallas_call(functools.partial(forward_kernel, experts, len(pieces)), o...  20.7 us
    pallas_call x1, Pallas kernels, weight_grads(): pl.pallas_call(functools.partial(grads_kernel, len(pieces), len(hids), ti...  9.29 us
    unnamed x24, local copies, waits for them, and re-layouts  2.86 us
  transfers between devices with their start and end apart: 34, of which 16 were waited for; matrix products, arithmetic and copies ran while one was open for 3% of the time, Pallas kernels for 26%

profile of v4, /device:TPU:0, one launch (start us, length us, event | category | flops | bytes accessed | tf_op | source)
XLA Modules:
  0.0 115.5 jit_solution(5095889538302553310)
XLA Ops:
  0.6 2.0 %shard_map.110 = bf16[32,4224]{1,0:T(8,128)(2,1)} custom-call(bf16[32,2048]{1,0:T(8,128)(2,1)} %tok_ref.1, bf16[32,2048]{1,0:T(8,128)(2,1)} %grad_ref.1, s32[8,32]{1,0:T(8,128)} %bitcast.12, f32[8,32]{1,0:T(8,128)} %bitcast.13), custom_call_target="tpu_custom_call" | custom-call | tf_op jit(solution)/shard_map/pallas_call | solution.py:131
  2.7 2.9 %collective-permute-start = (bf16[32,4224]{1,0:T(8,128)(2,1)}, bf16[32,4224]{1,0:T(8,128)(2,1)S(1)}, u32[]{:S(2)}, u32[]{:S(2)}) collective-permute-start(bf16[32,4224]{1,0:T(8,128)(2,1)} %shard_map.110), channel_id=1, source_target_pairs={{0,1},{1,0},{2,3},{3,2},{4,6},{5,7},{6,4},{7,5},{8,9},{9,8},{10,11... | collective-permute-start | bytes 811016 | tf_op jit(solution)/shard_map/ppermute | solution.py:415
  5.6 1.6 %collective-permute-start.2 = (bf16[32,4224]{1,0:T(8,128)(2,1)}, bf16[32,4224]{1,0:T(8,128)(2,1)S(1)}, u32[]{:S(2)}, u32[]{:S(2)}) collective-permute-start(bf16[32,4224]{1,0:T(8,128)(2,1)} %shard_map.110), channel_id=1, source_target_pairs={{0,8},{1,9},{2,10},{3,11},{4,12},{5,13},{6,14},{7,15},{8,0},{9,1},... | collective-permute-start | bytes 811016 | tf_op jit(solution)/shard_map/ppermute | solution.py:415
  7.2 2.6 %collective-permute-start.1 = (bf16[32,4224]{1,0:T(8,128)(2,1)}, bf16[32,4224]{1,0:T(8,128)(2,1)S(1)}, u32[]{:S(2)}, u32[]{:S(2)}) collective-permute-start(bf16[32,4224]{1,0:T(8,128)(2,1)} %shard_map.110), channel_id=1, source_target_pairs={{0,16},{1,17},{2,18},{3,19},{4,20},{5,21},{6,22},{7,23},{8,24},{9,... | collective-permute-start | bytes 811016 | tf_op jit(solution)/shard_map/ppermute | solution.py:415
  11.3 2.1 %collective-permute-start.4 = (bf16[64,4224]{1,0:T(8,128)(2,1)S(1)}, bf16[64,4224]{1,0:T(8,128)(2,1)S(1)}, u32[]{:S(2)}, u32[]{:S(2)}) collective-permute-start(bf16[64,4224]{1,0:T(8,128)(2,1)S(1)} %pad_maximum_fusion.refs_0_), channel_id=1, source_target_pairs={{0,2},{1,3},{2,0},{3,1},{4,5},{5,4},{6,7},{7,6},{8,10},{9,11},{10,... | collective-permute-start | bytes 1622024 | tf_op jit(solution)/shard_map/ppermute | solution.py:415
  13.4 1.4 %copy-done.3 = bf16[1,2048,384]{2,1,0:T(8,128)(2,1)S(1)} copy-done((bf16[1,2048,384]{2,1,0:T(8,128)(2,1)S(1)}, bf16[1,2048,384]{2,1,0:T(8,128)(2,1)}, u32[]{:S(2)}) %copy-start.3) | copy-done | bytes 1572888
  14.8 1.4 %copy-done.4 = bf16[1,384,2048]{2,1,0:T(8,128)(2,1)S(1)} copy-done((bf16[1,384,2048]{2,1,0:T(8,128)(2,1)S(1)}, bf16[1,384,2048]{2,1,0:T(8,128)(2,1)}, u32[]{:S(2)}) %copy-start.4) | copy-done | bytes 1572888
  16.7 2.8 %collective-permute-done.2 = bf16[32,4224]{1,0:T(8,128)(2,1)S(1)} collective-permute-done((bf16[32,4224]{1,0:T(8,128)(2,1)}, bf16[32,4224]{1,0:T(8,128)(2,1)S(1)}, u32[]{:S(2)}, u32[]{:S(2)}) %collective-permute-start.2) | collective-permute-done | bytes 270368 | tf_op jit(solution)/shard_map/ppermute | solution.py:415
  19.5 1.5 %collective-permute-start.3 = (bf16[32,4224]{1,0:T(8,128)(2,1)S(1)}, bf16[32,4224]{1,0:T(8,128)(2,1)S(1)}, u32[]{:S(2)}, u32[]{:S(2)}) collective-permute-start(bf16[32,4224]{1,0:T(8,128)(2,1)S(1)} %collective-permute-done.2), channel_id=1, source_target_pairs={{0,1},{1,0},{2,3},{3,2},{4,6},{5,7},{6,4},{7,5},{8,9},{9,8},{10,11... | collective-permute-start | bytes 811016 | tf_op jit(solution)/shard_map/ppermute | solution.py:415
  21.0 2.5 %collective-permute-start.10 = (bf16[32,4224]{1,0:T(8,128)(2,1)S(1)}, bf16[32,4224]{1,0:T(8,128)(2,1)S(1)}, u32[]{:S(2)}, u32[]{:S(2)}) collective-permute-start(bf16[32,4224]{1,0:T(8,128)(2,1)S(1)} %copy-done.11), channel_id=1, source_target_pairs={{0,24},{1,25},{2,26},{3,27},{4,28},{5,29},{6,30},{7,31},{8,16},{9,... | collective-permute-start | bytes 811016 | tf_op jit(solution)/shard_map/ppermute | solution.py:415
  23.5 2.5 %collective-permute-done.3 = bf16[32,4224]{1,0:T(8,128)(2,1)S(1)} collective-permute-done((bf16[32,4224]{1,0:T(8,128)(2,1)S(1)}, bf16[32,4224]{1,0:T(8,128)(2,1)S(1)}, u32[]{:S(2)}, u32[]{:S(2)}) %collective-permute-start.3) | collective-permute-done | bytes 270368 | tf_op jit(solution)/shard_map/ppermute | solution.py:415
  26.5 1.3 %collective-permute-start.13 = (bf16[64,4224]{1,0:T(8,128)(2,1)S(1)}, bf16[64,4224]{1,0:T(8,128)(2,1)S(1)}, u32[]{:S(2)}, u32[]{:S(2)}) collective-permute-start(bf16[64,4224]{1,0:T(8,128)(2,1)S(1)} %pad_maximum_fusion.1.refs_0_.refs_4_), channel_id=1, source_target_pairs={{0,4},{1,5},{2,6},{3,7},{4,0},{5,1},{6,2},{7,3},{8,12},{9,13},{10,... | collective-permute-start | bytes 1622024 | tf_op jit(solution)/shard_map/ppermute | solution.py:415
  28.3 5.1 %shard_map.112 = (bf16[128,4096]{1,0:T(8,128)(2,1)S(1)}, bf16[128,4096]{1,0:T(8,128)(2,1)S(1)}, bf16[256,384]{1,0:T(8,128)(2,1)S(1)}, bf16[256,768]{1,0:T(8,128)(2,1)S(1)}) custom-call(s32[1]{0:T(128)} %bitcast.expert_ref, bf16[64,4224]{1,0:T(8,128)(2,1)S(1)} %pad_maximum_fusion.refs_0_, bf16[64,4224]{1,0:T(8,128)(2,1)S(1)} %collective-permute-done.4.refs_1_, ...), custom_call_target="tpu_custom_call" | custom-call | flops 48318382080 | bytes 8912896 | tf_op jit(solution)/shard_map/pallas_call | solution.py:254
  33.5 3.7 %collective-permute-done.8 = bf16[32,4224]{1,0:T(8,128)(2,1)S(1)} collective-permute-done((bf16[32,4224]{1,0:T(8,128)(2,1)S(1)}, bf16[32,4224]{1,0:T(8,128)(2,1)S(1)}, u32[]{:S(2)}, u32[]{:S(2)}) %collective-permute-start.8) | collective-permute-done | bytes 270368 | tf_op jit(solution)/shard_map/ppermute | solution.py:415
  38.8 1.3 %collective-permute-start.15 = (bf16[64,4224]{1,0:T(8,128)(2,1)S(1)}, bf16[64,4224]{1,0:T(8,128)(2,1)S(1)}, u32[]{:S(2)}, u32[]{:S(2)}) collective-permute-start(bf16[64,4224]{1,0:T(8,128)(2,1)S(1)} %pad_maximum_fusion.2.refs_0_.refs_8_), channel_id=1, source_target_pairs={{0,4},{1,5},{2,6},{3,7},{4,0},{5,1},{6,2},{7,3},{8,12},{9,13},{10,... | collective-permute-start | bytes 1622024 | tf_op jit(solution)/shard_map/ppermute | solution.py:415
  40.7 5.1 %shard_map.113 = (bf16[128,4096]{1,0:T(8,128)(2,1)S(1)}, bf16[128,4096]{1,0:T(8,128)(2,1)S(1)}, bf16[256,384]{1,0:T(8,128)(2,1)S(1)}, bf16[256,768]{1,0:T(8,128)(2,1)S(1)}) custom-call(s32[1]{0:T(128)} %bitcast.expert_ref, bf16[64,4224]{1,0:T(8,128)(2,1)S(1)} %pad_maximum_fusion.1.refs_0_.refs_4_, ...), custom_call_target="tpu_custom_call" | custom-call | flops 48318382080 | bytes 8912896 | tf_op jit(solution)/shard_map/pallas_call | solution.py:254
  45.8 3.7 %collective-permute-done.11 = bf16[32,4224]{1,0:T(8,128)(2,1)S(1)} collective-permute-done((bf16[32,4224]{1,0:T(8,128)(2,1)S(1)}, bf16[32,4224]{1,0:T(8,128)(2,1)S(1)}, u32[]{:S(2)}, u32[]{:S(2)}) %collective-permute-start.11) | collective-permute-done | bytes 270368 | tf_op jit(solution)/shard_map/ppermute | solution.py:415
  51.0 1.3 %collective-permute-start.21 = (bf16[64,4224]{1,0:T(8,128)(2,1)S(1)}, bf16[64,4224]{1,0:T(8,128)(2,1)S(1)}, u32[]{:S(2)}, u32[]{:S(2)}) collective-permute-start(bf16[64,4224]{1,0:T(8,128)(2,1)S(1)} %pad_maximum_fusion.3.refs_0_.refs_12_), channel_id=1, source_target_pairs={{0,4},{1,5},{2,6},{3,7},{4,0},{5,1},{6,2},{7,3},{8,12},{9,13},{10,... | collective-permute-start | bytes 1622024 | tf_op jit(solution)/shard_map/ppermute | solution.py:415
  52.6 5.3 %shard_map.114 = (bf16[128,4096]{1,0:T(8,128)(2,1)S(1)}, bf16[128,4096]{1,0:T(8,128)(2,1)S(1)}, bf16[256,384]{1,0:T(8,128)(2,1)S(1)}, bf16[256,768]{1,0:T(8,128)(2,1)S(1)}) custom-call(s32[1]{0:T(128)} %bitcast.expert_ref, bf16[64,4224]{1,0:T(8,128)(2,1)S(1)} %pad_maximum_fusion.2.refs_0_.refs_8_, ...), custom_call_target="tpu_custom_call" | custom-call | flops 48318382080 | bytes 8912896 | tf_op jit(solution)/shard_map/pallas_call | solution.py:254
  58.5 1.5 %collective-permute-done.18.refs_1_.refs_13_ = bf16[64,4224]{1,0:T(8,128)(2,1)S(1)} collective-permute-done((bf16[64,4224]{1,0:T(8,128)(2,1)S(1)}, bf16[64,4224]{1,0:T(8,128)(2,1)S(1)}, u32[]{:S(2)}, u32[]{:S(2)}) %collective-permute-start.18) | collective-permute-done | bytes 540704 | tf_op jit(solution)/shard_map/ppermute | solution.py:415
  61.2 1.6 %collective-permute-start.20 = (bf16[64,4096]{1,0:T(8,128)(2,1)S(1)}, bf16[64,4096]{1,0:T(8,128)(2,1)S(1)}, u32[]{:S(2)}, u32[]{:S(2)}) collective-permute-start(bf16[64,4096]{1,0:T(8,128)(2,1)S(1)} %slice.49), channel_id=1, source_target_pairs={{0,2},{1,3},{2,0},{3,1},{4,5},{5,4},{6,7},{7,6},{8,10},{9,11},{10,... | collective-permute-start | bytes 1572872 | tf_op jit(solution)/shard_map/ppermute | solution.py:415
  62.8 5.1 %shard_map.115 = (bf16[128,4096]{1,0:T(8,128)(2,1)S(1)}, bf16[128,4096]{1,0:T(8,128)(2,1)S(1)}, bf16[256,384]{1,0:T(8,128)(2,1)S(1)}, bf16[256,768]{1,0:T(8,128)(2,1)S(1)}) custom-call(s32[1]{0:T(128)} %bitcast.expert_ref, bf16[64,4224]{1,0:T(8,128)(2,1)S(1)} %pad_maximum_fusion.3.refs_0_.refs_12_, ...), custom_call_target="tpu_custom_call" | custom-call | flops 48318382080 | bytes 8912896 | tf_op jit(solution)/shard_map/pallas_call | solution.py:254
  68.6 6.3 %collective-permute-done.20 = bf16[64,4096]{1,0:T(8,128)(2,1)S(1)} collective-permute-done((bf16[64,4096]{1,0:T(8,128)(2,1)S(1)}, bf16[64,4096]{1,0:T(8,128)(2,1)S(1)}, u32[]{:S(2)}, u32[]{:S(2)}) %collective-permute-start.20) | collective-permute-done | bytes 524320 | tf_op jit(solution)/shard_map/ppermute | solution.py:415
  75.1 1.6 %collective-permute-start.23 = (bf16[32,4096]{1,0:T(8,128)(2,1)S(1)}, bf16[32,4096]{1,0:T(8,128)(2,1)S(1)}, u32[]{:S(2)}, u32[]{:S(2)}) collective-permute-start(bf16[32,4096]{1,0:T(8,128)(2,1)S(1)} %slice.51), channel_id=1, source_target_pairs={{0,1},{1,0},{2,3},{3,2},{4,6},{5,7},{6,4},{7,5},{8,9},{9,8},{10,11... | collective-permute-start | bytes 786440 | tf_op jit(solution)/shard_map/ppermute | solution.py:415
  76.9 6.5 %collective-permute-done.25 = bf16[64,4096]{1,0:T(8,128)(2,1)S(1)} collective-permute-done((bf16[64,4096]{1,0:T(8,128)(2,1)S(1)}, bf16[64,4096]{1,0:T(8,128)(2,1)S(1)}, u32[]{:S(2)}, u32[]{:S(2)}) %collective-permute-start.25) | collective-permute-done | bytes 524320 | tf_op jit(solution)/shard_map/ppermute | solution.py:415
  83.5 1.6 %collective-permute-start.29 = (bf16[32,4096]{1,0:T(8,128)(2,1)S(1)}, bf16[32,4096]{1,0:T(8,128)(2,1)S(1)}, u32[]{:S(2)}, u32[]{:S(2)}) collective-permute-start(bf16[32,4096]{1,0:T(8,128)(2,1)S(1)} %slice.61), channel_id=1, source_target_pairs={{0,1},{1,0},{2,3},{3,2},{4,6},{5,7},{6,4},{7,5},{8,9},{9,8},{10,11... | collective-permute-start | bytes 786440 | tf_op jit(solution)/shard_map/ppermute | solution.py:415
  86.2 6.6 %collective-permute-done.29 = bf16[32,4096]{1,0:T(8,128)(2,1)S(1)} collective-permute-done((bf16[32,4096]{1,0:T(8,128)(2,1)S(1)}, bf16[32,4096]{1,0:T(8,128)(2,1)S(1)}, u32[]{:S(2)}, u32[]{:S(2)}) %collective-permute-start.29) | collective-permute-done | bytes 262176 | tf_op jit(solution)/shard_map/ppermute | solution.py:415
  93.6 1.9 %collective-permute-done.28 = bf16[64,4096]{1,0:T(8,128)(2,1)S(1)} collective-permute-done((bf16[64,4096]{1,0:T(8,128)(2,1)S(1)}, bf16[64,4096]{1,0:T(8,128)(2,1)S(1)}, u32[]{:S(2)}, u32[]{:S(2)}) %collective-permute-start.28) | collective-permute-done | bytes 524320 | tf_op jit(solution)/shard_map/ppermute | solution.py:415
  96.0 1.7 %collective-permute-start.32 = (bf16[32,4096]{1,0:T(8,128)(2,1)S(1)}, bf16[32,4096]{1,0:T(8,128)(2,1)S(1)}, u32[]{:S(2)}, u32[]{:S(2)}) collective-permute-start(bf16[32,4096]{1,0:T(8,128)(2,1)S(1)} %slice.63), channel_id=1, source_target_pairs={{0,1},{1,0},{2,3},{3,2},{4,6},{5,7},{6,4},{7,5},{8,9},{9,8},{10,11... | collective-permute-start | bytes 786440 | tf_op jit(solution)/shard_map/ppermute | solution.py:415
  98.5 3.9 %collective-permute-done.32 = bf16[32,4096]{1,0:T(8,128)(2,1)S(1)} collective-permute-done((bf16[32,4096]{1,0:T(8,128)(2,1)S(1)}, bf16[32,4096]{1,0:T(8,128)(2,1)S(1)}, u32[]{:S(2)}, u32[]{:S(2)}) %collective-permute-start.32) | collective-permute-done | bytes 262176 | tf_op jit(solution)/shard_map/ppermute | solution.py:415
  102.5 2.8 %collective-permute-start.33 = (bf16[32,4096]{1,0:T(8,128)(2,1)S(1)}, bf16[32,4096]{1,0:T(8,128)(2,1)S(1)}, u32[]{:S(2)}, u32[]{:S(2)}) collective-permute-start(bf16[32,4096]{1,0:T(8,128)(2,1)S(1)} %add_convert_fusion.8), channel_id=1, source_target_pairs={{0,24},{1,25},{2,26},{3,27},{4,28},{5,29},{6,30},{7,31},{8,16},{9,... | collective-permute-start | bytes 786440 | tf_op jit(solution)/shard_map/ppermute | solution.py:415
  105.4 9.3 %shard_map.117 = (bf16[2048,384]{1,0:T(8,128)(2,1)}, bf16[2048,384]{1,0:T(8,128)(2,1)}, bf16[384,2048]{1,0:T(8,128)(2,1)}) custom-call(bf16[64,4224]{1,0:T(8,128)(2,1)S(1)} %copy-done.1, bf16[64,4224]{1,0:T(8,128)(2,1)S(1)} %copy-done.6, bf16[64,4224]{1,0:T(8,128)(2,1)S(1)} %copy-done.8, bf16[64,4224]{1,0:T(8,128)(2,1)S(1)} %copy-done.10, ...), custom_call_target="tpu_custom_call" | custom-call | flops 1 | bytes 13107200 | tf_op jit(solution)/shard_map/pallas_call | solution.py:336
  (92 shorter events, 13.9 us)
Async XLA Ops:
  2.7 7.6 %collective-permute-start = (bf16[32,4224]{1,0:T(8,128)(2,1)}, bf16[32,4224]{1,0:T(8,128)(2,1)S(1)}, u32[]{:S(2)}, u32[]{:S(2)}) collective-permute-start(bf16[32,4224]{1,0:T(8,128)(2,1)} %shard_map.110), channel_id=1, source_target_pairs={{0,1},{1,0},{2,3},{3,2},{4,6},{5,7},{6,4},{7,5},{8,9},{9,8},{10,11... | collective-permute-start | bytes 811016 | tf_op jit(solution)/shard_map/ppermute | solution.py:415
  5.6 13.8 %collective-permute-start.2 = (bf16[32,4224]{1,0:T(8,128)(2,1)}, bf16[32,4224]{1,0:T(8,128)(2,1)S(1)}, u32[]{:S(2)}, u32[]{:S(2)}) collective-permute-start(bf16[32,4224]{1,0:T(8,128)(2,1)} %shard_map.110), channel_id=1, source_target_pairs={{0,8},{1,9},{2,10},{3,11},{4,12},{5,13},{6,14},{7,15},{8,0},{9,1},... | collective-permute-start | bytes 811016 | tf_op jit(solution)/shard_map/ppermute | solution.py:415
  7.2 18.9 %collective-permute-start.1 = (bf16[32,4224]{1,0:T(8,128)(2,1)}, bf16[32,4224]{1,0:T(8,128)(2,1)S(1)}, u32[]{:S(2)}, u32[]{:S(2)}) collective-permute-start(bf16[32,4224]{1,0:T(8,128)(2,1)} %shard_map.110), channel_id=1, source_target_pairs={{0,16},{1,17},{2,18},{3,19},{4,20},{5,21},{6,22},{7,23},{8,24},{9,... | collective-permute-start | bytes 811016 | tf_op jit(solution)/shard_map/ppermute | solution.py:415
  11.3 12.2 %collective-permute-start.4 = (bf16[64,4224]{1,0:T(8,128)(2,1)S(1)}, bf16[64,4224]{1,0:T(8,128)(2,1)S(1)}, u32[]{:S(2)}, u32[]{:S(2)}) collective-permute-start(bf16[64,4224]{1,0:T(8,128)(2,1)S(1)} %pad_maximum_fusion.refs_0_), channel_id=1, source_target_pairs={{0,2},{1,3},{2,0},{3,1},{4,5},{5,4},{6,7},{7,6},{8,10},{9,11},{10,... | collective-permute-start | bytes 1622024 | tf_op jit(solution)/shard_map/ppermute | solution.py:415
  13.4 14.4 %collective-permute-start.5 = (bf16[64,4224]{1,0:T(8,128)(2,1)S(1)}, bf16[64,4224]{1,0:T(8,128)(2,1)S(1)}, u32[]{:S(2)}, u32[]{:S(2)}) collective-permute-start(bf16[64,4224]{1,0:T(8,128)(2,1)S(1)} %pad_maximum_fusion.refs_0_), channel_id=1, source_target_pairs={{0,4},{1,5},{2,6},{3,7},{4,0},{5,1},{6,2},{7,3},{8,12},{9,13},{10,... | collective-permute-start | bytes 1622024 | tf_op jit(solution)/shard_map/ppermute | solution.py:415
  19.5 6.5 %collective-permute-start.3 = (bf16[32,4224]{1,0:T(8,128)(2,1)S(1)}, bf16[32,4224]{1,0:T(8,128)(2,1)S(1)}, u32[]{:S(2)}, u32[]{:S(2)}) collective-permute-start(bf16[32,4224]{1,0:T(8,128)(2,1)S(1)} %collective-permute-done.2), channel_id=1, source_target_pairs={{0,1},{1,0},{2,3},{3,2},{4,6},{5,7},{6,4},{7,5},{8,9},{9,8},{10,11... | collective-permute-start | bytes 811016 | tf_op jit(solution)/shard_map/ppermute | solution.py:415
  21.0 16.3 %collective-permute-start.10 = (bf16[32,4224]{1,0:T(8,128)(2,1)S(1)}, bf16[32,4224]{1,0:T(8,128)(2,1)S(1)}, u32[]{:S(2)}, u32[]{:S(2)}) collective-permute-start(bf16[32,4224]{1,0:T(8,128)(2,1)S(1)} %copy-done.11), channel_id=1, source_target_pairs={{0,24},{1,25},{2,26},{3,27},{4,28},{5,29},{6,30},{7,31},{8,16},{9,... | collective-permute-start | bytes 811016 | tf_op jit(solution)/shard_map/ppermute | solution.py:415
  26.0 2.3 %collective-permute-start.6 = (bf16[64,4224]{1,0:T(8,128)(2,1)S(1)}, bf16[64,4224]{1,0:T(8,128)(2,1)S(1)}, u32[]{:S(2)}, u32[]{:S(2)}) collective-permute-start(bf16[64,4224]{1,0:T(8,128)(2,1)S(1)} %collective-permute-done.4.refs_1_), channel_id=1, source_target_pairs={{0,4},{1,5},{2,6},{3,7},{4,0},{5,1},{6,2},{7,3},{8,12},{9,13},{10,... | collective-permute-start | bytes 1622024 | tf_op jit(solution)/shard_map/ppermute | solution.py:415
  26.1 12.3 %collective-permute-start.12 = (bf16[64,4224]{1,0:T(8,128)(2,1)S(1)}, bf16[64,4224]{1,0:T(8,128)(2,1)S(1)}, u32[]{:S(2)}, u32[]{:S(2)}) collective-permute-start(bf16[64,4224]{1,0:T(8,128)(2,1)S(1)} %pad_maximum_fusion.1.refs_0_.refs_4_), channel_id=1, source_target_pairs={{0,2},{1,3},{2,0},{3,1},{4,5},{5,4},{6,7},{7,6},{8,10},{9,11},{10,... | collective-permute-start | bytes 1622024 | tf_op jit(solution)/shard_map/ppermute | solution.py:415
  26.5 13.6 %collective-permute-start.13 = (bf16[64,4224]{1,0:T(8,128)(2,1)S(1)}, bf16[64,4224]{1,0:T(8,128)(2,1)S(1)}, u32[]{:S(2)}, u32[]{:S(2)}) collective-permute-start(bf16[64,4224]{1,0:T(8,128)(2,1)S(1)} %pad_maximum_fusion.1.refs_0_.refs_4_), channel_id=1, source_target_pairs={{0,4},{1,5},{2,6},{3,7},{4,0},{5,1},{6,2},{7,3},{8,12},{9,13},{10,... | collective-permute-start | bytes 1622024 | tf_op jit(solution)/shard_map/ppermute | solution.py:415
  27.8 9.4 %collective-permute-start.8 = (bf16[32,4224]{1,0:T(8,128)(2,1)S(1)}, bf16[32,4224]{1,0:T(8,128)(2,1)S(1)}, u32[]{:S(2)}, u32[]{:S(2)}) collective-permute-start(bf16[32,4224]{1,0:T(8,128)(2,1)S(1)} %collective-permute-done.1), channel_id=1, source_target_pairs={{0,1},{1,0},{2,3},{3,2},{4,6},{5,7},{6,4},{7,5},{8,9},{9,8},{10,11... | collective-permute-start | bytes 811016 | tf_op jit(solution)/shard_map/ppermute | solution.py:415
  38.4 12.3 %collective-permute-start.9 = (bf16[64,4224]{1,0:T(8,128)(2,1)S(1)}, bf16[64,4224]{1,0:T(8,128)(2,1)S(1)}, u32[]{:S(2)}, u32[]{:S(2)}) collective-permute-start(bf16[64,4224]{1,0:T(8,128)(2,1)S(1)} %pad_maximum_fusion.2.refs_0_.refs_8_), channel_id=1, source_target_pairs={{0,2},{1,3},{2,0},{3,1},{4,5},{5,4},{6,7},{7,6},{8,10},{9,11},{10,... | collective-permute-start | bytes 1622024 | tf_op jit(solution)/shard_map/ppermute | solution.py:415
  38.8 13.6 %collective-permute-start.15 = (bf16[64,4224]{1,0:T(8,128)(2,1)S(1)}, bf16[64,4224]{1,0:T(8,128)(2,1)S(1)}, u32[]{:S(2)}, u32[]{:S(2)}) collective-permute-start(bf16[64,4224]{1,0:T(8,128)(2,1)S(1)} %pad_maximum_fusion.2.refs_0_.refs_8_), channel_id=1, source_target_pairs={{0,4},{1,5},{2,6},{3,7},{4,0},{5,1},{6,2},{7,3},{8,12},{9,13},{10,... | collective-permute-start | bytes 1622024 | tf_op jit(solution)/shard_map/ppermute | solution.py:415
  40.1 9.4 %collective-permute-start.11 = (bf16[32,4224]{1,0:T(8,128)(2,1)S(1)}, bf16[32,4224]{1,0:T(8,128)(2,1)S(1)}, u32[]{:S(2)}, u32[]{:S(2)}) collective-permute-start(bf16[32,4224]{1,0:T(8,128)(2,1)S(1)} %collective-permute-done.10), channel_id=1, source_target_pairs={{0,1},{1,0},{2,3},{3,2},{4,6},{5,7},{6,4},{7,5},{8,9},{9,8},{10,11... | collective-permute-start | bytes 811016 | tf_op jit(solution)/shard_map/ppermute | solution.py:415
  40.6 20.2 %collective-permute-start.7 = (bf16[128,4096]{1,0:T(8,128)(2,1)S(1)}, bf16[128,4096]{1,0:T(8,128)(2,1)S(1)}, u32[]{:S(2)}, u32[]{:S(2)}) collective-permute-start(bf16[128,4096]{1,0:T(8,128)(2,1)S(1)} %get-tuple-element.238), channel_id=1, source_target_pairs={{0,4},{1,5},{2,6},{3,7},{4,0},{5,1},{6,2},{7,3},{8,12},{9,13},{10,... | collective-permute-start | bytes 3145736 | tf_op jit(solution)/shard_map/ppermute | solution.py:415
  50.6 9.4 %collective-permute-start.18 = (bf16[64,4224]{1,0:T(8,128)(2,1)S(1)}, bf16[64,4224]{1,0:T(8,128)(2,1)S(1)}, u32[]{:S(2)}, u32[]{:S(2)}) collective-permute-start(bf16[64,4224]{1,0:T(8,128)(2,1)S(1)} %pad_maximum_fusion.3.refs_0_.refs_12_), channel_id=1, source_target_pairs={{0,2},{1,3},{2,0},{3,1},{4,5},{5,4},{6,7},{7,6},{8,10},{9,11},{10,... | collective-permute-start | bytes 1622024 | tf_op jit(solution)/shard_map/ppermute | solution.py:415
  51.0 11.8 %collective-permute-start.21 = (bf16[64,4224]{1,0:T(8,128)(2,1)S(1)}, bf16[64,4224]{1,0:T(8,128)(2,1)S(1)}, u32[]{:S(2)}, u32[]{:S(2)}) collective-permute-start(bf16[64,4224]{1,0:T(8,128)(2,1)S(1)} %pad_maximum_fusion.3.refs_0_.refs_12_), channel_id=1, source_target_pairs={{0,4},{1,5},{2,6},{3,7},{4,0},{5,1},{6,2},{7,3},{8,12},{9,13},{10,... | collective-permute-start | bytes 1622024 | tf_op jit(solution)/shard_map/ppermute | solution.py:415
  52.4 5.9 %collective-permute-start.19 = (bf16[128,4096]{1,0:T(8,128)(2,1)S(1)}, bf16[128,4096]{1,0:T(8,128)(2,1)S(1)}, u32[]{:S(2)}, u32[]{:S(2)}) collective-permute-start(bf16[128,4096]{1,0:T(8,128)(2,1)S(1)} %get-tuple-element.285), channel_id=1, source_target_pairs={{0,4},{1,5},{2,6},{3,7},{4,0},{5,1},{6,2},{7,3},{8,12},{9,13},{10,... | collective-permute-start | bytes 3145736 | tf_op jit(solution)/shard_map/ppermute | solution.py:415
  57.9 2.7 %collective-permute-start.17 = (bf16[128,4096]{1,0:T(8,128)(2,1)S(1)}, bf16[128,4096]{1,0:T(8,128)(2,1)S(1)}, u32[]{:S(2)}, u32[]{:S(2)}) collective-permute-start(bf16[128,4096]{1,0:T(8,128)(2,1)S(1)} %get-tuple-element.281), channel_id=1, source_target_pairs={{0,4},{1,5},{2,6},{3,7},{4,0},{5,1},{6,2},{7,3},{8,12},{9,13},{10,... | collective-permute-start | bytes 3145736 | tf_op jit(solution)/shard_map/ppermute | solution.py:415
  60.0 2.8 %collective-permute-start.22 = (bf16[64,4224]{1,0:T(8,128)(2,1)S(1)}, bf16[64,4224]{1,0:T(8,128)(2,1)S(1)}, u32[]{:S(2)}, u32[]{:S(2)}) collective-permute-start(bf16[64,4224]{1,0:T(8,128)(2,1)S(1)} %collective-permute-done.18.refs_1_.refs_13_), channel_id=1, source_target_pairs={{0,4},{1,5},{2,6},{3,7},{4,0},{5,1},{6,2},{7,3},{8,12},{9,13},{10,... | collective-permute-start | bytes 1622024 | tf_op jit(solution)/shard_map/ppermute | solution.py:415
  60.0 25.0 %collective-permute-start.24 = (bf16[64,4096]{1,0:T(8,128)(2,1)S(1)}, bf16[64,4096]{1,0:T(8,128)(2,1)S(1)}, u32[]{:S(2)}, u32[]{:S(2)}) collective-permute-start(bf16[64,4096]{1,0:T(8,128)(2,1)S(1)} %slice.53), channel_id=1, source_target_pairs={{0,2},{1,3},{2,0},{3,1},{4,5},{5,4},{6,7},{7,6},{8,10},{9,11},{10,... | collective-permute-start | bytes 1572872 | tf_op jit(solution)/shard_map/ppermute | solution.py:415
  61.2 13.7 %collective-permute-start.20 = (bf16[64,4096]{1,0:T(8,128)(2,1)S(1)}, bf16[64,4096]{1,0:T(8,128)(2,1)S(1)}, u32[]{:S(2)}, u32[]{:S(2)}) collective-permute-start(bf16[64,4096]{1,0:T(8,128)(2,1)S(1)} %slice.49), channel_id=1, source_target_pairs={{0,2},{1,3},{2,0},{3,1},{4,5},{5,4},{6,7},{7,6},{8,10},{9,11},{10,... | collective-permute-start | bytes 1572872 | tf_op jit(solution)/shard_map/ppermute | solution.py:415
  68.0 8.7 %collective-permute-start.26 = (bf16[128,4096]{1,0:T(8,128)(2,1)S(1)}, bf16[128,4096]{1,0:T(8,128)(2,1)S(1)}, u32[]{:S(2)}, u32[]{:S(2)}) collective-permute-start(bf16[128,4096]{1,0:T(8,128)(2,1)S(1)} %get-tuple-element.322), channel_id=1, source_target_pairs={{0,4},{1,5},{2,6},{3,7},{4,0},{5,1},{6,2},{7,3},{8,12},{9,13},{10,... | collective-permute-start | bytes 3145736 | tf_op jit(solution)/shard_map/ppermute | solution.py:415
  68.0 15.3 %collective-permute-start.25 = (bf16[64,4096]{1,0:T(8,128)(2,1)S(1)}, bf16[64,4096]{1,0:T(8,128)(2,1)S(1)}, u32[]{:S(2)}, u32[]{:S(2)}) collective-permute-start(bf16[64,4096]{1,0:T(8,128)(2,1)S(1)} %slice.55), channel_id=1, source_target_pairs={{0,2},{1,3},{2,0},{3,1},{4,5},{5,4},{6,7},{7,6},{8,10},{9,11},{10,... | collective-permute-start | bytes 1572872 | tf_op jit(solution)/shard_map/ppermute | solution.py:415
  75.1 20.9 %collective-permute-start.23 = (bf16[32,4096]{1,0:T(8,128)(2,1)S(1)}, bf16[32,4096]{1,0:T(8,128)(2,1)S(1)}, u32[]{:S(2)}, u32[]{:S(2)}) collective-permute-start(bf16[32,4096]{1,0:T(8,128)(2,1)S(1)} %slice.51), channel_id=1, source_target_pairs={{0,1},{1,0},{2,3},{3,2},{4,6},{5,7},{6,4},{7,5},{8,9},{9,8},{10,11... | collective-permute-start | bytes 786440 | tf_op jit(solution)/shard_map/ppermute | solution.py:415
  83.5 9.3 %collective-permute-start.29 = (bf16[32,4096]{1,0:T(8,128)(2,1)S(1)}, bf16[32,4096]{1,0:T(8,128)(2,1)S(1)}, u32[]{:S(2)}, u32[]{:S(2)}) collective-permute-start(bf16[32,4096]{1,0:T(8,128)(2,1)S(1)} %slice.61), channel_id=1, source_target_pairs={{0,1},{1,0},{2,3},{3,2},{4,6},{5,7},{6,4},{7,5},{8,9},{9,8},{10,11... | collective-permute-start | bytes 786440 | tf_op jit(solution)/shard_map/ppermute | solution.py:415
  85.2 10.3 %collective-permute-start.28 = (bf16[64,4096]{1,0:T(8,128)(2,1)S(1)}, bf16[64,4096]{1,0:T(8,128)(2,1)S(1)}, u32[]{:S(2)}, u32[]{:S(2)}) collective-permute-start(bf16[64,4096]{1,0:T(8,128)(2,1)S(1)} %slice.59), channel_id=1, source_target_pairs={{0,2},{1,3},{2,0},{3,1},{4,5},{5,4},{6,7},{7,6},{8,10},{9,11},{10,... | collective-permute-start | bytes 1572872 | tf_op jit(solution)/shard_map/ppermute | solution.py:415
  85.8 10.1 %collective-permute-start.27 = (bf16[32,4096]{1,0:T(8,128)(2,1)S(1)}, bf16[32,4096]{1,0:T(8,128)(2,1)S(1)}, u32[]{:S(2)}, u32[]{:S(2)}) collective-permute-start(bf16[32,4096]{1,0:T(8,128)(2,1)S(1)} %slice.57), channel_id=1, source_target_pairs={{0,1},{1,0},{2,3},{3,2},{4,6},{5,7},{6,4},{7,5},{8,9},{9,8},{10,11... | collective-permute-start | bytes 786440 | tf_op jit(solution)/shard_map/ppermute | solution.py:415
  92.9 12.5 %collective-permute-start.30 = (bf16[32,4096]{1,0:T(8,128)(2,1)S(1)}, bf16[32,4096]{1,0:T(8,128)(2,1)S(1)}, u32[]{:S(2)}, u32[]{:S(2)}) collective-permute-start(bf16[32,4096]{1,0:T(8,128)(2,1)S(1)} %add_convert_fusion.11), channel_id=1, source_target_pairs={{0,16},{1,17},{2,18},{3,19},{4,20},{5,21},{6,22},{7,23},{8,24},{9,... | collective-permute-start | bytes 786440 | tf_op jit(solution)/shard_map/ppermute | solution.py:415
  96.0 6.4 %collective-permute-start.32 = (bf16[32,4096]{1,0:T(8,128)(2,1)S(1)}, bf16[32,4096]{1,0:T(8,128)(2,1)S(1)}, u32[]{:S(2)}, u32[]{:S(2)}) collective-permute-start(bf16[32,4096]{1,0:T(8,128)(2,1)S(1)} %slice.63), channel_id=1, source_target_pairs={{0,1},{1,0},{2,3},{3,2},{4,6},{5,7},{6,4},{7,5},{8,9},{9,8},{10,11... | collective-permute-start | bytes 786440 | tf_op jit(solution)/shard_map/ppermute | solution.py:415
  97.7 17.0 %collective-permute-start.31 = (bf16[32,4096]{1,0:T(8,128)(2,1)S(1)}, bf16[32,4096]{1,0:T(8,128)(2,1)S(1)}, u32[]{:S(2)}, u32[]{:S(2)}) collective-permute-start(bf16[32,4096]{1,0:T(8,128)(2,1)S(1)} %add_convert_fusion.10), channel_id=1, source_target_pairs={{0,8},{1,9},{2,10},{3,11},{4,12},{5,13},{6,14},{7,15},{8,0},{9,1},... | collective-permute-start | bytes 786440 | tf_op jit(solution)/shard_map/ppermute | solution.py:415
  102.5 12.2 %collective-permute-start.33 = (bf16[32,4096]{1,0:T(8,128)(2,1)S(1)}, bf16[32,4096]{1,0:T(8,128)(2,1)S(1)}, u32[]{:S(2)}, u32[]{:S(2)}) collective-permute-start(bf16[32,4096]{1,0:T(8,128)(2,1)S(1)} %add_convert_fusion.8), channel_id=1, source_target_pairs={{0,24},{1,25},{2,26},{3,27},{4,28},{5,29},{6,30},{7,31},{8,16},{9,... | collective-permute-start | bytes 786440 | tf_op jit(solution)/shard_map/ppermute | solution.py:415
  (14 other events, 101.4 us)
